TPU v7x, 32 devices: a whole 2x2x4 slice. The times are simulated.
32 devices in a mesh: dp: 8 (over z, x), rows: 4 (over y, core).
Axes of the slice: x: 2, y: 2, z: 4, core: 2. Of those that a mesh axis runs over, the one named last changes fastest.
Arguments:
- atoms_big: bfloat16 [4, 8, 256, 512], P(None, 'dp', 'rows'), may hold values from -6 to 6
- atoms_mid: bfloat16 [4, 8, 128, 512], P(None, 'dp', 'rows'), may hold values from -6 to 6
- atoms_small: bfloat16 [4, 16, 64, 512], P(None, 'dp', 'rows'), may hold values from -6 to 6
- pair_big: bfloat16 [4, 8, 64, 256, 256], P(None, 'dp', None, 'rows'), may hold values from -6 to 6
- pair_mid: bfloat16 [4, 8, 64, 128, 128], P(None, 'dp', None, 'rows'), may hold values from -6 to 6
- pair_small: bfloat16 [4, 16, 64, 64, 64], P(None, 'dp', None, 'rows'), may hold values from -6 to 6
- lengths_big: int32 [4, 8], P(None, 'dp'), may hold values from 129 to 256, as said below
- lengths_mid: int32 [4, 8], P(None, 'dp'), may hold values from 65 to 128, as said below
- lengths_small: int32 [4, 16], P(None, 'dp'), may hold values from 33 to 64, as said below
- query_weight: bfloat16 [512, 512], replicated, may hold values from -0.25 to 0.25
- key_weight: bfloat16 [512, 512], replicated, may hold values from -0.25 to 0.25
- value_weight: bfloat16 [512, 512], replicated, may hold values from -0.25 to 0.25
- out_weight: bfloat16 [512, 512], replicated, may hold values from -1.5 to 1.5
- up_weight: bfloat16 [512, 2048], replicated, may hold values from -0.25 to 0.25
- down_weight: bfloat16 [2048, 512], replicated, may hold values from -0.125 to 0.125
- gain_one: float32 [512], replicated, may hold values from 0.25 to 1.75
- shift_one: float32 [512], replicated, may hold values from -1.8 to 1.8
- gain_two: float32 [512], replicated, may hold values from 0.25 to 1.75
- shift_two: float32 [512], replicated, may hold values from -1.8 to 1.8
- cotangent_big: bfloat16 [4, 8, 256, 512], P(None, 'dp', 'rows'), may hold values from -6 to 6
- cotangent_mid: bfloat16 [4, 8, 128, 512], P(None, 'dp', 'rows'), may hold values from -6 to 6
- cotangent_small: bfloat16 [4, 16, 64, 512], P(None, 'dp', 'rows'), may hold values from -6 to 6
- cotangent_pair_big: bfloat16 [4, 8, 64, 256, 256], P(None, 'dp', None, 'rows'), may hold values from -0.29882812 to 0.29882812
- cotangent_pair_mid: bfloat16 [4, 8, 64, 128, 128], P(None, 'dp', None, 'rows'), may hold values from -0.29882812 to 0.29882812
- cotangent_pair_small: bfloat16 [4, 16, 64, 64, 64], P(None, 'dp', None, 'rows'), may hold values from -0.29882812 to 0.29882812
Outputs:
- atoms_out_big: bfloat16 [4, 8, 256, 512], P(None, 'dp', 'rows')
- atoms_out_mid: bfloat16 [4, 8, 128, 512], P(None, 'dp', 'rows')
- atoms_out_small: bfloat16 [4, 16, 64, 512], P(None, 'dp', 'rows')
- pair_out_big: bfloat16 [4, 8, 64, 256, 256], P(None, 'dp', None, 'rows')
- pair_out_mid: bfloat16 [4, 8, 64, 128, 128], P(None, 'dp', None, 'rows')
- pair_out_small: bfloat16 [4, 16, 64, 64, 64], P(None, 'dp', None, 'rows')
- grad_atoms_big: bfloat16 [4, 8, 256, 512], P(None, 'dp', 'rows')
- grad_atoms_mid: bfloat16 [4, 8, 128, 512], P(None, 'dp', 'rows')
- grad_atoms_small: bfloat16 [4, 16, 64, 512], P(None, 'dp', 'rows')
- grad_pair_big: bfloat16 [4, 8, 64, 256, 256], P(None, 'dp', None, 'rows')
- grad_pair_mid: bfloat16 [4, 8, 64, 128, 128], P(None, 'dp', None, 'rows')
- grad_pair_small: bfloat16 [4, 16, 64, 64, 64], P(None, 'dp', None, 'rows')
- grad_query_weight: float32 [512, 512], replicated
- grad_key_weight: float32 [512, 512], replicated
- grad_value_weight: float32 [512, 512], replicated
- grad_out_weight: float32 [512, 512], replicated
- grad_up_weight: float32 [512, 2048], replicated
- grad_down_weight: float32 [2048, 512], replicated
- grad_gain_one: float32 [512], replicated
- grad_shift_one: float32 [512], replicated
- grad_gain_two: float32 [512], replicated
- grad_shift_two: float32 [512], replicated
Inputs may be any that keep to these rules, and one draw needn't show every extreme that they name: `lengths_big`: atoms of each molecule; keys at or beyond the length are padding; some molecule fills the bucket. `lengths_mid`: atoms of each molecule; keys at or beyond the length are padding; some molecule fills the bucket. `lengths_small`: atoms of each molecule; keys at or beyond the length are padding; some molecule fills the bucket.
All inputs are finite; a program needn't handle non-finite values.
Results may differ from a plain program's by a relative error of at most 0.012.
The roundings to bfloat16 on the way count: a program that leaves them out, or rounds other values in their place, can miss the bound.
Values may be sent and summed in bfloat16 or wider, within the bound.
No kernel may reach another device: no remote copies, remote signals or barrier semaphores. Data moves between devices by JAX's collectives and lax.ppermute only.
A program may use at most 320 MiB of HBM per device.

v0:
```python
import jax
import jax.numpy as jnp
from jax import lax
from jax.sharding import PartitionSpec as P

EPSILON = 1e-05
MASKED_LOGIT = -1e30


def norm_rows(inputs, gain, shift):
    center = jnp.mean(inputs, axis=-1, keepdims=True)
    centred = inputs - center
    spread = jnp.mean(centred * centred, axis=-1, keepdims=True)
    return centred * lax.rsqrt(spread + EPSILON) * gain + shift


def gelu_tanh(inputs):
    return jax.nn.gelu(inputs, approximate=True)


def project(left, right):
    return jnp.dot(left, right, preferred_element_type=jnp.float32)


def back_project(grad, weight):
    return lax.dot_general(
        grad, weight, (((grad.ndim - 1,), (1,)), ((), ())), preferred_element_type=jnp.float32
    )


def outer_sum(left, right):
    flat_left = left.reshape(-1, left.shape[-1])
    flat_right = right.reshape(-1, right.shape[-1])
    return lax.dot_general(
        flat_left, flat_right, (((0,), (0,)), ((), ())), preferred_element_type=jnp.float32
    )


def split_heads(array, head_count):
    return array.reshape(array.shape[0], array.shape[1], head_count, array.shape[2] // head_count)


def logits_of(queries, key_rows, pair_block, lengths):
    head_count = pair_block.shape[1]
    head_width = queries.shape[-1] // head_count
    products = jnp.einsum(
        "srhc,sjhc->shrj",
        split_heads(queries, head_count),
        split_heads(key_rows, head_count),
        preferred_element_type=jnp.float32,
    )
    logits = products * head_width ** (-0.5) + pair_block.astype(jnp.float32)
    key_valid = (
        lax.broadcasted_iota(jnp.int32, (1, 1, 1, key_rows.shape[1]), 3)
        < lengths[:, None, None, None]
    )
    return (logits, key_valid)


def front_part(atom_block, params):
    atom_rows = atom_block.astype(jnp.float32)
    normed = norm_rows(atom_rows, params[6], params[7]).astype(jnp.bfloat16)
    queries = project(normed, params[0]).astype(jnp.bfloat16)
    key_rows = project(normed, params[1]).astype(jnp.bfloat16)
    values = project(normed, params[2]).astype(jnp.bfloat16)
    return (atom_rows, normed, queries, key_rows, values)


def forward_rest(atom_rows, queries, key_rows, values, pair_block, lengths, params):
    head_count = pair_block.shape[1]
    logits, key_valid = logits_of(queries, key_rows, pair_block, lengths)
    masked = jnp.where(key_valid, logits, MASKED_LOGIT)
    row_max = jnp.max(masked, axis=-1, keepdims=True)
    shifted = jnp.exp(masked - row_max)
    row_sum = jnp.sum(shifted, axis=-1, keepdims=True)
    softmax = (shifted / row_sum).astype(jnp.bfloat16)
    log_total = row_max + jnp.log(row_sum)
    mixed_heads = jnp.einsum(
        "shrj,sjhc->srhc",
        softmax,
        split_heads(values, head_count),
        preferred_element_type=jnp.float32,
    )
    mixed_heads = mixed_heads.reshape(queries.shape).astype(jnp.bfloat16)
    hidden = atom_rows + project(mixed_heads, params[3])
    normed_two = norm_rows(hidden, params[8], params[9]).astype(jnp.bfloat16)
    up_proj = project(normed_two, params[4])
    gelu_out = gelu_tanh(up_proj).astype(jnp.bfloat16)
    result = hidden + project(gelu_out, params[5])
    return (
        result.astype(jnp.bfloat16),
        logits.astype(jnp.bfloat16),
        (mixed_heads, hidden, normed_two, up_proj, gelu_out, log_total),
    )


def backward_rest(
    grad_out, grad_pair_out, queries, key_rows, values, pair_block, lengths, saved, params
):
    mixed_heads, hidden, normed_two, up_proj, gelu_out, log_total = saved
    head_count = pair_block.shape[1]
    head_width = queries.shape[-1] // head_count
    score_scale = head_width ** (-0.5)
    grad_result = grad_out.astype(jnp.float32)
    grad_down = outer_sum(gelu_out, grad_out)
    grad_gelu = back_project(grad_out, params[5])
    grad_up_proj = jax.vjp(gelu_tanh, up_proj)[1](grad_gelu)[0].astype(jnp.bfloat16)
    grad_up = outer_sum(normed_two, grad_up_proj)
    grad_normed_two = back_project(grad_up_proj, params[4])
    norm_back = jax.vjp(norm_rows, hidden, params[8], params[9])[1](grad_normed_two)
    grad_hidden = grad_result + norm_back[0]
    grad_branch = grad_hidden.astype(jnp.bfloat16)
    grad_out_proj = outer_sum(mixed_heads, grad_branch)
    grad_mixed = split_heads(back_project(grad_branch, params[3]).astype(jnp.bfloat16), head_count)
    logits, key_valid = logits_of(queries, key_rows, pair_block, lengths)
    softmax = jnp.where(key_valid, jnp.exp(logits - log_total), 0.0)
    grad_softmax = jnp.einsum(
        "srhc,sjhc->shrj",
        grad_mixed,
        split_heads(values, head_count),
        preferred_element_type=jnp.float32,
    )
    grad_values = jnp.einsum(
        "shrj,srhc->sjhc",
        softmax.astype(jnp.bfloat16),
        grad_mixed,
        preferred_element_type=jnp.float32,
    )
    row_inner = jnp.sum(softmax * grad_softmax, axis=-1, keepdims=True)
    grad_logits = (softmax * (grad_softmax - row_inner) + grad_pair_out.astype(jnp.float32)).astype(
        jnp.bfloat16
    )
    grad_queries = (
        jnp.einsum(
            "shrj,sjhc->srhc",
            grad_logits,
            split_heads(key_rows, head_count),
            preferred_element_type=jnp.float32,
        )
        * score_scale
    )
    grad_queries = grad_queries.reshape(queries.shape).astype(jnp.bfloat16)
    grad_keys = (
        jnp.einsum(
            "shrj,srhc->sjhc",
            grad_logits,
            split_heads(queries, head_count),
            preferred_element_type=jnp.float32,
        )
        * score_scale
    )
    partial_grads = (grad_out_proj, grad_up, grad_down, norm_back[1], norm_back[2])
    return (
        grad_logits,
        grad_queries,
        grad_hidden,
        grad_keys.reshape(key_rows.shape),
        grad_values.reshape(key_rows.shape),
        partial_grads,
    )


def finish_part(atom_rows, normed, grad_queries, grad_keys, grad_values, grad_hidden, params):
    grad_query = outer_sum(normed, grad_queries)
    grad_key = outer_sum(normed, grad_keys)
    grad_value = outer_sum(normed, grad_values)
    grad_normed = (
        back_project(grad_queries, params[0])
        + back_project(grad_keys, params[1])
        + back_project(grad_values, params[2])
    )
    norm_back = jax.vjp(norm_rows, atom_rows, params[6], params[7])[1](grad_normed)
    grad_atoms = (grad_hidden + norm_back[0]).astype(jnp.bfloat16)
    return (grad_atoms, (grad_query, grad_key, grad_value, norm_back[1], norm_back[2]))


def shards(
    atoms_big,
    atoms_mid,
    atoms_small,
    pair_big,
    pair_mid,
    pair_small,
    lengths_big,
    lengths_mid,
    lengths_small,
    query_weight,
    key_weight,
    value_weight,
    out_weight,
    up_weight,
    down_weight,
    gain_one,
    shift_one,
    gain_two,
    shift_two,
    cotangent_big,
    cotangent_mid,
    cotangent_small,
    cotangent_pair_big,
    cotangent_pair_mid,
    cotangent_pair_small,
):
    params = (
        query_weight,
        key_weight,
        value_weight,
        out_weight,
        up_weight,
        down_weight,
        gain_one,
        shift_one,
        gain_two,
        shift_two,
    )
    atom_sets = (atoms_big, atoms_mid, atoms_small)
    pair_sets = (pair_big, pair_mid, pair_small)
    length_sets = (lengths_big, lengths_mid, lengths_small)
    cotangent_sets = (cotangent_big, cotangent_mid, cotangent_small)
    pair_cot_sets = (cotangent_pair_big, cotangent_pair_mid, cotangent_pair_small)
    micro_count = atoms_big.shape[0]
    later_places = (3, 4, 5, 8, 9)
    front_places = (0, 1, 2, 6, 7)
    totals = tuple((jnp.zeros(weight.shape, jnp.float32) for weight in params))
    atoms_lists = ([], [], [])
    pair_lists = ([], [], [])
    grad_atom_lists = ([], [], [])
    grad_pair_lists = ([], [], [])
    for micro_step in range(micro_count):
        fronts = [front_part(atom_sets[bucket][micro_step], params) for bucket in range(3)]
        outgoing = (
            fronts[0][3],
            fronts[0][4],
            fronts[1][3],
            fronts[1][4],
            fronts[2][3],
            fronts[2][4],
        )
        gathered = (
            lax.all_gather(outgoing[0], "rows", axis=1, tiled=True),
            lax.all_gather(outgoing[1], "rows", axis=1, tiled=True),
            lax.all_gather(outgoing[2], "rows", axis=1, tiled=True),
            lax.all_gather(outgoing[3], "rows", axis=1, tiled=True),
            lax.all_gather(outgoing[4], "rows", axis=1, tiled=True),
            lax.all_gather(outgoing[5], "rows", axis=1, tiled=True),
        )
        saved_list = []
        for bucket in range(3):
            result, logits_low, saved = forward_rest(
                fronts[bucket][0],
                fronts[bucket][2],
                gathered[2 * bucket],
                gathered[2 * bucket + 1],
                pair_sets[bucket][micro_step],
                length_sets[bucket][micro_step],
                params,
            )
            atoms_lists[bucket].append(result)
            pair_lists[bucket].append(logits_low)
            saved_list.append(saved)
        local_grads = [jnp.zeros(weight.shape, jnp.float32) for weight in params]
        backs = []
        full_grads = []
        for bucket in range(3):
            grad_logits, grad_queries, grad_hidden, grad_keys, grad_values, partial_grads = (
                backward_rest(
                    cotangent_sets[bucket][micro_step],
                    pair_cot_sets[bucket][micro_step],
                    fronts[bucket][2],
                    gathered[2 * bucket],
                    gathered[2 * bucket + 1],
                    pair_sets[bucket][micro_step],
                    length_sets[bucket][micro_step],
                    saved_list[bucket],
                    params,
                )
            )
            grad_pair_lists[bucket].append(grad_logits)
            backs.append((grad_queries, grad_hidden))
            full_grads.append(grad_keys)
            full_grads.append(grad_values)
            for place, term in zip(later_places, partial_grads):
                local_grads[place] = local_grads[place] + term
        summed = (
            lax.psum_scatter(full_grads[0], "rows", scatter_dimension=1, tiled=True),
            lax.psum_scatter(full_grads[1], "rows", scatter_dimension=1, tiled=True),
            lax.psum_scatter(full_grads[2], "rows", scatter_dimension=1, tiled=True),
            lax.psum_scatter(full_grads[3], "rows", scatter_dimension=1, tiled=True),
            lax.psum_scatter(full_grads[4], "rows", scatter_dimension=1, tiled=True),
            lax.psum_scatter(full_grads[5], "rows", scatter_dimension=1, tiled=True),
        )
        for bucket in range(3):
            grad_atoms, front_grads = finish_part(
                fronts[bucket][0],
                fronts[bucket][1],
                backs[bucket][0],
                summed[2 * bucket].astype(jnp.bfloat16),
                summed[2 * bucket + 1].astype(jnp.bfloat16),
                backs[bucket][1],
                params,
            )
            grad_atom_lists[bucket].append(grad_atoms)
            for place, term in zip(front_places, front_grads):
                local_grads[place] = local_grads[place] + term
        totals = tuple((before + after for before, after in zip(totals, local_grads)))
    totals = lax.psum(totals, ("dp", "rows"))
    atoms_out = [jnp.stack(atoms_lists[bucket], axis=0) for bucket in range(3)]
    pair_out = [jnp.stack(pair_lists[bucket], axis=0) for bucket in range(3)]
    grad_atoms_out = [jnp.stack(grad_atom_lists[bucket], axis=0) for bucket in range(3)]
    grad_pair_out = [jnp.stack(grad_pair_lists[bucket], axis=0) for bucket in range(3)]
    return (
        atoms_out[0],
        atoms_out[1],
        atoms_out[2],
        pair_out[0],
        pair_out[1],
        pair_out[2],
        grad_atoms_out[0],
        grad_atoms_out[1],
        grad_atoms_out[2],
        grad_pair_out[0],
        grad_pair_out[1],
        grad_pair_out[2],
        totals[0],
        totals[1],
        totals[2],
        totals[3],
        totals[4],
        totals[5],
        totals[6],
        totals[7],
        totals[8],
        totals[9],
    )


def solution(mesh):
    in_specs = (
        P(None, "dp", "rows", None),
        P(None, "dp", "rows", None),
        P(None, "dp", "rows", None),
        P(None, "dp", None, "rows", None),
        P(None, "dp", None, "rows", None),
        P(None, "dp", None, "rows", None),
        P(None, "dp"),
        P(None, "dp"),
        P(None, "dp"),
        P(),
        P(),
        P(),
        P(),
        P(),
        P(),
        P(),
        P(),
        P(),
        P(),
        P(None, "dp", "rows", None),
        P(None, "dp", "rows", None),
        P(None, "dp", "rows", None),
        P(None, "dp", None, "rows", None),
        P(None, "dp", None, "rows", None),
        P(None, "dp", None, "rows", None),
    )
    out_specs = (
        P(None, "dp", "rows", None),
        P(None, "dp", "rows", None),
        P(None, "dp", "rows", None),
        P(None, "dp", None, "rows", None),
        P(None, "dp", None, "rows", None),
        P(None, "dp", None, "rows", None),
        P(None, "dp", "rows", None),
        P(None, "dp", "rows", None),
        P(None, "dp", "rows", None),
        P(None, "dp", None, "rows", None),
        P(None, "dp", None, "rows", None),
        P(None, "dp", None, "rows", None),
        P(),
        P(),
        P(),
        P(),
        P(),
        P(),
        P(),
        P(),
        P(),
        P(),
    )
    return jax.shard_map(shards, mesh=mesh, in_specs=in_specs, out_specs=out_specs, check_vma=False)
```

profile of v0, /device:TPU:0, one launch (start us, length us, event | category | flops | bytes accessed | tf_op | source)
XLA Modules:
  0.0 2068.5 jit_solution(6752950300695792741)
XLA Ops:
  12.7 6.5 all_gather.93
  26.8 5.6 all_gather.92
  46.1 13.2 fusion.168
  92.3 6.4 all-gather.7
  102.1 7.8 all-gather.6
  111.7 3.1 select_reduce_fusion
  114.9 3.4 convert_bitcast_fusion
  124.3 6.3 all-gather.5
  134.0 6.8 all-gather.4
  142.6 3.1 select_reduce_fusion.1
  145.7 3.5 convert_bitcast_fusion.1
  158.3 6.3 all-gather.1
  168.0 7.8 all-gather
  177.5 3.1 select_reduce_fusion.3
  180.7 3.5 convert_bitcast_fusion.3
  192.5 6.3 all-gather.3
  202.2 6.6 all-gather.2
  210.6 3.1 select_reduce_fusion.2
  213.8 3.8 convert_bitcast_fusion.2
  233.6 3.8 fusion.188
  237.4 8.3 fusion.12
  249.0 8.2 fusion.15
  257.2 3.8 fusion.179
  263.5 8.2 fusion.13
  271.7 3.1 fusion.236
  274.8 2.9 fusion.176
  282.6 8.1 fusion.14
  290.7 3.7 fusion.182
  296.2 5.9 all-gather.15
  305.2 7.0 all-gather.14
  323.4 5.9 all-gather.13
  332.4 6.1 all-gather.12
  352.2 5.9 all-gather.9
  361.2 6.8 all-gather.8
  380.9 5.9 all-gather.11
  390.0 6.5 all-gather.10
  428.6 13.1 fusion.172
  450.0 13.2 fusion.171
  471.4 13.1 fusion.174
  492.8 13.2 fusion.173
  533.1 2.9 fusion.1182
  544.6 2.9 fusion.1178
  610.2 847.4 %all-reduce.23 = (bf16[1,256,512]{2,0,1:T(2,128)(2,1)}, bf16[1,256,512]{2,0,1:T(2,128)(2,1)}, bf16[1,256,512]{2,0,1:T(2,128)(2,1)}, bf16[1,256,512]{2,0,1:T(2,12...) all-reduce(f32[1,256,512]{2,0,1:T(1,128)} %copy.383, ...), channel_id=24, replica_groups=mesh['dp'=8,'rows'=4] {'rows'}, use_global_device_ids=true, to_apply=%region_96.97.clone | all-reduce | flops 1572864 | bytes 9437184
  1502.2 2.9 fusion.1279
  1506.6 4.4 pad_maximum_fusion
  1514.4 3.9 pad_maximum_fusion.1
  1541.3 5.6 all_gather.95
  1549.4 5.6 all_gather.94
  1564.6 5.8 all_gather.91
  1573.9 5.9 all_gather.90
  1590.1 5.9 all_gather.89
  1599.3 6.3 all_gather.88
  1629.1 13.2 fusion.167
  1649.2 13.6 fusion.169
  1686.3 14.1 fusion.170
  1719.9 3.7 fusion.1136
  1726.3 3.7 fusion.1135
  1740.5 2.9 fusion.1278
  1749.8 17.8 fusion.16
  1767.7 17.6 add_add_fusion
  1802.2 3.7 fusion.156
  1807.1 3.7 fusion.159
  1827.7 41.7 %all-reduce.16 = (f32[512]{0:T(512)}, f32[512]{0:T(512)}, f32[512]{0:T(512)}, f32[512]{0:T(512)}) all-reduce(f32[512]{0:T(512)S(1)} %add_add_fusion.40, f32[512]{0:T(512)S(1)} %add_add_fusion.39, f32[512]{0:T(512)} %add_add_fusion.38, f32[512]{0:T(512)} %add_add_fusion.37), channel_id=1, replica_groups=mesh['dp'=8,'rows'=4] {'dp','rows'}, use_global_device_ids=true, to_apply=%region_174.175 | all-reduce | flops 2048 | bytes 16384 | tf_op jit(solution)/shard_map/psum | solution.py:306
  1872.0 177.3 %all-reduce.22.cloned.1.call-done = (f32[512,512]{1,0:T(8,128)}, f32[512,512]{1,0:T(8,128)}, f32[512,512]{1,0:T(8,128)}, f32[512,512]{1,0:T(8,128)}, f32[512,2048]{1,0:T(8,128)}, /*index=5*/f32[2048,512]{1,0:T(8,128)}) async-done(((f32[512,512]{1,0:T(8,128)}, f32[512,512]{1,0:T(8,128)}, f32[512,512]{1,0:T(8,128)}, f32[512,512]{1,0:T(8,128)}, f32[512,2048]{1,0:T(8,128)}, /*index=5*/f32[2048,512]{1,0:T(8,128)}), ...) | async-done | bytes 12582928 | tf_op jit(solution)/shard_map/psum | solution.py:306
  (1760 shorter events, 575.2 us)
Async XLA Ops:
  7.2 28.1 %copy-start = (bf16[512,2048]{1,0:T(8,128)(2,1)S(1)}, bf16[512,2048]{1,0:T(8,128)(2,1)}, u32[]{:S(2)}) copy-start(bf16[512,2048]{1,0:T(8,128)(2,1)} %param.38) | copy-start | bytes 6291460
  7.2 18.7 copy-start.39
  7.2 18.7 copy-start.41
  7.2 18.7 copy-start.38
  7.2 18.6 copy-start.19
  7.3 1514.6 %reduce-scatter.19.cloned.1.call-start = ((), (), s32[]{:S(2)}) async-start(), calls=%async_computation.13 | async-start | bytes 327680 | tf_op jit(solution)/shard_map/reduce_scatter | solution.py:290
  39.5 19.8 copy-start.302
  44.5 19.2 copy-start.29
  44.6 19.7 copy-start.13
  44.6 1478.6 %reduce-scatter.17.cloned.1.call-start = ((), (), s32[]{:S(2)}) async-start(), calls=%async_computation.12 | async-start | bytes 327680 | tf_op jit(solution)/shard_map/reduce_scatter | solution.py:289
  44.6 15.5 copy-start.139
  63.2 15.3 copy-start.37
  63.2 1722.1 %reduce-scatter.21.cloned.1.call-start = ((), (), s32[]{:S(2)}) async-start(), calls=%async_computation.14 | async-start | bytes 327680 | tf_op jit(solution)/shard_map/reduce_scatter | solution.py:289
  63.9 14.8 copy-start.403
  63.9 14.8 copy-start.406
  63.9 14.7 copy-start.400
  64.0 14.8 copy-start.409
  404.2 16.6 copy-start.124
  404.2 16.6 copy-start.467
  404.4 16.4 copy-start.506
  424.8 16.9 copy-start.264
  424.8 17.9 copy-start.277
  424.8 18.9 copy-start.295
  446.3 16.9 copy-start.263
  446.3 17.9 copy-start.276
  446.3 18.9 copy-start.291
  467.6 16.9 copy-start.265
  467.6 17.9 copy-start.278
  467.6 18.9 copy-start.293
  489.0 17.1 copy-start.266
  489.0 18.2 copy-start.279
  489.0 19.2 copy-start.15
  489.0 19.2 copy-start.204
  489.0 20.1 copy-start.410
  489.0 20.1 copy-start.448
  490.4 20.2 copy-start.202
  492.8 18.7 copy-start.401
  492.8 18.7 copy-start.434
  492.8 20.0 copy-start.205
  1523.2 15.0 copy-start.17
  1563.2 22.3 %copy-start.128 = (f32[2,16,512]{2,1,0:T(8,128)}, f32[2,16,512]{2,1,0:T(8,128)S(1)}, u32[]{:S(2)}) copy-start(f32[2,16,512]{2,1,0:T(8,128)S(1)} %get-tuple-element.329) | copy-start | bytes 196612
  1563.2 16.6 copy-start.412
  1563.3 16.4 copy-start.477
  1563.4 16.4 copy-start.436
  1625.1 17.3 copy-start.136
  1625.1 18.4 copy-start.142
  1626.5 18.0 copy-start.239
  1626.5 18.0 copy-start.325
  1626.5 18.7 copy-start.300
  1647.7 15.1 copy-start.137
  1647.7 16.2 copy-start.143
  1666.9 122.3 %reduce-scatter.13.cloned.1.call-start = ((), (), s32[]{:S(2)}) async-start(), calls=%async_computation.10 | async-start | bytes 327680 | tf_op jit(solution)/shard_map/reduce_scatter | solution.py:289
  1677.1 116.0 %reduce-scatter.23.cloned.1.call-start = ((), (), s32[]{:S(2)}) async-start(), calls=%async_computation.15 | async-start | bytes 327680 | tf_op jit(solution)/shard_map/reduce_scatter | solution.py:290
  1686.2 110.8 %reduce-scatter.15.cloned.1.call-start = ((), (), s32[]{:S(2)}) async-start(), calls=%async_computation.11 | async-start | bytes 327680 | tf_op jit(solution)/shard_map/reduce_scatter | solution.py:290
  1711.2 89.7 %reduce-scatter.9.cloned.1.call-start = ((), (), s32[]{:S(2)}) async-start(), calls=%async_computation.8 | async-start | bytes 327680 | tf_op jit(solution)/shard_map/reduce_scatter | solution.py:289
  1723.6 82.3 %reduce-scatter.11.cloned.1.call-start = ((), (), s32[]{:S(2)}) async-start(), calls=%async_computation.9 | async-start | bytes 327680 | tf_op jit(solution)/shard_map/reduce_scatter | solution.py:290
  1730.1 319.2 %all-reduce.22.cloned.1.call-start = ((), (), s32[]{:S(2)}) async-start(), calls=%async_computation.16 | async-start | bytes 25165824 | tf_op jit(solution)/shard_map/psum | solution.py:306
  1749.8 17.9 copy-start.169
  1749.8 17.9 copy-start.371
  1767.7 17.7 copy-start.374
  1820.9 48.5 %copy-start.160 = (bf16[4,2,16,512]{3,2,1,0:T(8,128)(2,1)S(1)}, bf16[4,2,16,512]{3,2,1,0:T(8,128)(2,1)}, u32[]{:S(2)}) copy-start(bf16[4,2,16,512]{3,2,1,0:T(8,128)(2,1)} %param.46) | copy-start | bytes 393220
  1821.0 49.5 %copy-start.229 = (f32[2,16,512]{2,1,0:T(8,128)S(1)}, f32[2,16,512]{2,1,0:T(8,128)}, u32[]{:S(2)}) copy-start(f32[2,16,512]{2,1,0:T(8,128)} %get-tuple-element.325) | copy-start | bytes 196612
  1821.0 49.5 %copy-start.242 = (f32[2,16,512]{2,1,0:T(8,128)S(1)}, f32[2,16,512]{2,1,0:T(8,128)}, u32[]{:S(2)}) copy-start(f32[2,16,512]{2,1,0:T(8,128)} %copy-done.241) | copy-start | bytes 196612
  1821.0 49.5 %copy-start.244 = (f32[2,16,512]{2,1,0:T(8,128)S(1)}, f32[2,16,512]{2,1,0:T(8,128)}, u32[]{:S(2)}) copy-start(f32[2,16,512]{2,1,0:T(8,128)} %copy-done.243) | copy-start | bytes 196612
  (543 other events, 2880.3 us)
Sparse Core Ops, SparseCore 0:
  44.7 21.5 reduce-scatter.18
  68.9 20.1 reduce-scatter.16
  1667.1 21.1 reduce-scatter.20
  1690.7 20.0 reduce-scatter.12
  1713.1 20.0 reduce-scatter.22
  1735.6 20.0 reduce-scatter.14
  1758.2 20.0 reduce-scatter.8
  1780.9 20.0 reduce-scatter.10
  1811.0 238.2 all-reduce.21
where the time goes:
time: 2080 us; the launch traced here: 2070 us
  blocking collectives  1040 us (50%)
  matrix products  469 us (23%)
  other arithmetic  196 us (9%)
  waiting for transfers between devices  177 us (9%)
  local copies, waits for them, and re-layouts  163 us (8%)
  between operations  21.9 us (1%)
    unnamed x1, blocking collectives  847 us
    dot_general x72, matrix products, outer_sum(): lax.dot_general(flat_left, flat_right, (((0,), (0,)), ((), ())), preferre...  179 us
    psum x1, waiting for transfers between devices, shards(): totals = lax.psum(totals, ('dp', 'rows'))  177 us
    sub x8, other arithmetic, backward_rest(): grad_softmax - row_inner  107 us
    dot_general x72, matrix products, project(): return jnp.dot(left, right, preferred_element_type=jnp.float32)  71.9 us
    dot_general x72, matrix products, back_project(): lax.dot_general(grad, weight, (((grad.ndim - 1,), (1,)), ((), ())), prefe...  60.3 us
    unnamed x1219, local copies, waits for them, and re-layouts  42.8 us
    psum x1, blocking collectives, shards(): totals = lax.psum(totals, ('dp', 'rows'))  41.7 us
  transfers between devices with their start and end apart: 9, of which 1 were waited for; matrix products, arithmetic and copies ran while one was open for 32% of the time, Pallas kernels for 0%

commit v1 on v0

v1 whole, which is shorter than its diff:
```python
import functools

import jax
import jax.numpy as jnp
from jax import lax
from jax.experimental import pallas as pl
from jax.experimental.pallas import tpu as pltpu
from jax.sharding import PartitionSpec as P

EPSILON = 1e-05
MASKED = -1e30
BF = jnp.bfloat16
F32 = jnp.float32
LANES = 128
GELU_C = 0.7978845608028654
GELU_A = 0.044715
MIB = 1 << 20


def dot_nn(a, b):
    return lax.dot_general(a, b, (((1,), (0,)), ((), ())), preferred_element_type=F32)


def dot_nt(a, b):
    return lax.dot_general(a, b, (((1,), (1,)), ((), ())), preferred_element_type=F32)


def dot_tn(a, b):
    return lax.dot_general(a, b, (((0,), (0,)), ((), ())), preferred_element_type=F32)


def normalize(x):
    centred = x - jnp.mean(x, axis=-1, keepdims=True)
    spread = jnp.mean(centred * centred, axis=-1, keepdims=True)
    inv = lax.rsqrt(spread + EPSILON)
    return centred * inv, inv


def norm_back(grad, gain, xhat, inv):
    g = grad * gain
    return inv * (
        g
        - jnp.mean(g, axis=-1, keepdims=True)
        - xhat * jnp.mean(g * xhat, axis=-1, keepdims=True)
    )


def front_kernel(
    layout, me_ref, x0, x1, x2, x3, wq, wk, wv, gain, shift, q_out, *outs
):
    me = me_ref[0]
    for piece, x_ref in enumerate((x0, x1, x2, x3)):
        xhat, _ = normalize(x_ref[...].astype(F32))
        a1 = (xhat * gain[...] + shift[...]).astype(BF)
        xhat = xhat.astype(BF)
        keys = dot_nn(a1, wk[...]).astype(BF)
        values = dot_nn(a1, wv[...]).astype(BF)
        if piece == 0:
            q_out[...] = dot_nn(a1, wq[...]).astype(BF)
        row = me ^ piece
        for bucket, (start, mols, rows, slots) in enumerate(layout):
            for mol in range(mols):
                src = slice(start + mol * rows, start + (mol + 1) * rows)
                at = pl.multiple_of(mol * slots + row * rows, rows)
                for kind, value in enumerate((keys, values, a1, xhat)):
                    outs[4 * bucket + kind][pl.ds(at, rows), :] = value[src]


def head_mask(heads, first):
    lane = lax.broadcasted_iota(jnp.int32, (1, LANES), 1) // (LANES // heads)
    return lane == first


def stacked(block, heads, first, count):
    zero = jnp.zeros_like(block)
    return jnp.concatenate(
        [jnp.where(head_mask(heads, first + t), block, zero) for t in range(count)], axis=0
    )


def unstacked(total, product, heads, first, count, rows):
    for t in range(count):
        part = product[t * rows : (t + 1) * rows]
        total = total + jnp.where(head_mask(heads, first + t), part, 0.0)
    return total


def attn_fwd_kernel(
    mols, groups, heads, rows, slots, scale,
    len_ref, q_ref, k_ref, v_ref, pair_ref, pout_ref, p_ref, o_ref,
):
    count = min(heads, max(1, 256 // rows))
    for mol in range(mols):
        length = len_ref[pl.program_id(0) * mols + mol]
        key_at = lax.broadcasted_iota(jnp.int32, (1, 1, slots), 2)
        mask = jnp.where(key_at < length, 0.0, MASKED)
        for group in range(groups):
            lanes = slice(group * LANES, (group + 1) * LANES)
            q = q_ref[mol * rows : (mol + 1) * rows, lanes]
            k = k_ref[mol * slots : (mol + 1) * slots, lanes]
            v = v_ref[mol * slots : (mol + 1) * slots, lanes]
            total = jnp.zeros((rows, LANES), F32)
            for first in range(0, heads, count):
                at = slice(group * heads + first, group * heads + first + count)
                s = dot_nt(stacked(q, heads, first, count), k)
                s = s.reshape(count, rows, slots) * scale + pair_ref[mol, at].astype(F32)
                pout_ref[mol, at] = s.astype(BF)
                s = s + mask
                e = jnp.exp(s - jnp.max(s, axis=-1, keepdims=True))
                p = (e * (1.0 / jnp.sum(e, axis=-1, keepdims=True))).astype(BF)
                p_ref[mol, at] = p
                pv = dot_nn(p.reshape(count * rows, slots), v)
                total = unstacked(total, pv, heads, first, count, rows)
            o_ref[mol * rows : (mol + 1) * rows, lanes] = total


def attn_bwd_kernel(
    mols, groups, heads, rows, slots, scale,
    q_ref, k_ref, v_ref, do_ref, dd_ref, p_ref, dpo_ref, dl_ref, dq_ref, dk_ref, dv_ref,
):
    count = min(heads, max(1, 256 // rows))
    for group in range(groups):
        lanes = slice(group * LANES, (group + 1) * LANES)
        dk_all = []
        dv_all = []
        for mol in range(mols):
            rs = slice(mol * rows, (mol + 1) * rows)
            ks = slice(mol * slots, (mol + 1) * slots)
            q = q_ref[rs, lanes]
            do = do_ref[rs, lanes]
            dd = dd_ref[rs, lanes]
            k = k_ref[ks, lanes]
            v = v_ref[ks, lanes]
            v_aug = jnp.concatenate([v, jnp.ones_like(v)], axis=1)
            total = jnp.zeros((rows, LANES), F32)
            dk = jnp.zeros((LANES, slots), F32)
            dv = jnp.zeros((LANES, slots), F32)
            for first in range(0, heads, count):
                at = slice(group * heads + first, group * heads + first + count)
                do_s = stacked(do, heads, first, count)
                t = dot_nt(
                    jnp.concatenate([do_s, stacked(dd, heads, first, count)], axis=1), v_aug
                )
                p = p_ref[mol, at]
                dl = p.astype(F32) * t.reshape(count, rows, slots) + dpo_ref[mol, at].astype(F32)
                dl = dl.astype(BF)
                dl_ref[mol, at] = dl
                dl = dl.reshape(count * rows, slots)
                total = unstacked(total, dot_nn(dl, k), heads, first, count, rows)
                dk = dk + dot_tn(stacked(q, heads, first, count), dl)
                dv = dv + dot_tn(do_s, p.reshape(count * rows, slots))
            dq_ref[rs, lanes] = (total * scale).astype(BF)
            dk_all.append((dk * scale).astype(BF))
            dv_all.append(dv.astype(BF))
        dk_ref[lanes, :] = jnp.concatenate(dk_all, axis=1)
        dv_ref[lanes, :] = jnp.concatenate(dv_all, axis=1)


def shard_rows(ref, lead, value, chunks, mine):
    size = value.shape[0] // chunks
    for chunk in range(chunks):
        at = pl.multiple_of((chunk ^ mine) * size, size)
        ref[lead, pl.ds(at, size), :] = value[chunk * size : (chunk + 1) * size].astype(ref.dtype)


def dense_kernel(
    tiles, chunks,
    ids, x_ref, ob, om, os, dyb, dym, dys, wo, wu, wd, gain, shift,
    yb, ym, ys, dh_ref, do_ref, dd_ref, go_ref, gs_ref, up_send, down_send, up_keep, down_keep,
    o_s, dy_s, h_s, a2_s, xhat_s, inv_s, y_s, da_s,
):
    step = pl.program_id(0)

    @pl.when(step == 0)
    def _():
        o_s[...] = jnp.concatenate([ob[...], om[...], os[...]], axis=0)
        dy_s[...] = jnp.concatenate([dyb[...], dym[...], dys[...]], axis=0)
        hidden = x_ref[...].astype(F32) + dot_nn(o_s[...].astype(BF), wo[...])
        xhat, inv = normalize(hidden)
        h_s[...] = hidden
        xhat_s[...] = xhat
        inv_s[...] = jnp.broadcast_to(inv, inv_s.shape)
        a2_s[...] = (xhat * gain[...] + shift[...]).astype(BF)
        y_s[...] = hidden
        da_s[...] = jnp.zeros_like(da_s)

    a2 = a2_s[...]
    dy = dy_s[...]
    u = dot_nn(a2, wu[...])
    u2 = u * u
    th = jnp.tanh(GELU_C * (u + GELU_A * u * u2))
    half = 0.5 * (1.0 + th)
    g = (u * half).astype(BF)
    slope = half + 0.5 * u * (1.0 - th * th) * (GELU_C * (1.0 + 3.0 * GELU_A * u2))
    y_s[...] += dot_nn(g, wd[...])
    grad_down = dot_tn(g, dy)
    du = (dot_nt(dy, wd[...]) * slope).astype(BF)
    grad_up = dot_tn(a2, du)
    da_s[...] += dot_nt(du, wu[...])

    @pl.when(step < tiles // 2)
    def _():
        shard_rows(up_send, 0, grad_up, chunks, ids[1])
        shard_rows(down_send, 0, grad_down, chunks, ids[2])

    @pl.when(step >= tiles // 2)
    def _():
        shard_rows(up_keep, 0, grad_up, chunks, ids[1])
        shard_rows(down_keep, 0, grad_down, chunks, ids[2])

    @pl.when(step == tiles - 1)
    def _():
        y = y_s[...].astype(BF)
        nb, nm = yb.shape[0], ym.shape[0]
        yb[...] = y[:nb]
        ym[...] = y[nb : nb + nm]
        ys[...] = y[nb + nm :]
        da = da_s[...]
        xhat = xhat_s[...]
        gs_ref[0:1, :] = jnp.sum(da * xhat, axis=0, keepdims=True)
        gs_ref[1:2, :] = jnp.sum(da, axis=0, keepdims=True)
        dh = dy.astype(F32) + norm_back(da, gain[...], xhat, inv_s[:, 0:1])
        dh_ref[...] = dh
        dh = dh.astype(BF)
        o = o_s[...]
        go_ref[...] = dot_tn(o.astype(BF), dh).astype(BF)
        do = dot_nt(dh, wo[...]).astype(BF)
        do_ref[...] = do
        dd_ref[...] = (-(do.astype(F32) * o)).astype(BF)


def back_kernel(
    layout, chunks,
    ids, dqb, dqm, dqs, dkb, dkm, dks, dvb, dvm, dvs,
    ab, am, as_, hb, hm, hs, wq, wk, wv, go_ref,
    own_ref, keep_ref, send_ref, gs_ref, w_send, w_keep, da_s,
):
    me = ids[3]
    core = ids[0]
    dq = jnp.concatenate([dqb[...], dqm[...], dqs[...]], axis=0)
    daq = dot_nt(dq, wq[...])
    grads = []
    gain_sum = jnp.zeros((1, daq.shape[1]), F32)
    shift_sum = jnp.sum(daq, axis=0, keepdims=True)
    gk = jnp.zeros((wk.shape[1], wk.shape[0]), F32)
    gv = jnp.zeros_like(gk)
    a_own = []
    h_own = []
    base = 0
    for (start, mols, rows, slots), dk, dv, a, h in zip(
        layout, (dkb, dkm, dks), (dvb, dvm, dvs), (ab, am, as_), (hb, hm, hs)
    ):
        size = mols * slots
        da = lax.dot_general(
            dk[...], wk[...], (((0,), (1,)), ((), ())), preferred_element_type=F32
        ) + lax.dot_general(
            dv[...], wv[...], (((0,), (1,)), ((), ())), preferred_element_type=F32
        )
        gk = gk + dot_nn(dk[...], a[...])
        gv = gv + dot_nn(dv[...], a[...])
        gain_sum = gain_sum + jnp.sum(da * h[...].astype(F32), axis=0, keepdims=True)
        shift_sum = shift_sum + jnp.sum(da, axis=0, keepdims=True)
        da_s[base : base + size, :] = da
        for mol in range(mols):
            at = pl.multiple_of(mol * slots + me * rows, rows)
            a_own.append(a[pl.ds(at, rows), :])
            h_own.append(h[pl.ds(at, rows), :])
        base += size
    a_own = jnp.concatenate(a_own, axis=0)
    h_own = jnp.concatenate(h_own, axis=0)
    gq = dot_tn(a_own, dq)
    gain_sum = gain_sum + jnp.sum(daq * h_own.astype(F32), axis=0, keepdims=True)
    gs_ref[0:1, :] = gain_sum
    gs_ref[1:2, :] = shift_sum
    for piece in range(4):
        base = 0
        for start, mols, rows, slots in layout:
            for mol in range(mols):
                at = pl.multiple_of(base + mol * slots + (me ^ piece) * rows, rows)
                value = da_s[pl.ds(at, rows), :]
                to = slice(start + mol * rows, start + (mol + 1) * rows)
                if piece == 0:
                    own_ref[to, :] = value + daq[to]
                elif piece == 2:
                    keep_ref[to, :] = value.astype(BF)
                else:
                    send_ref[piece // 2, to, :] = value.astype(BF)
            base += mols * slots

    @pl.when(core == 0)
    def _():
        shard_rows(w_keep, 0, go_ref[...], chunks, ids[1])
        shard_rows(w_keep, 1, gq, chunks, ids[2])
        shard_rows(w_send, 0, gk, chunks, ids[1])
        shard_rows(w_send, 1, gv, chunks, ids[2])

    @pl.when(core == 1)
    def _():
        shard_rows(w_send, 0, go_ref[...], chunks, ids[1])
        shard_rows(w_send, 1, gq, chunks, ids[2])
        shard_rows(w_keep, 0, gk, chunks, ids[1])
        shard_rows(w_keep, 1, gv, chunks, ids[2])


def last_kernel(x_ref, own, near, far, dh, gain, gb, gm, gs):
    xhat, inv = normalize(x_ref[...].astype(F32))
    da = own[...] + near[...].astype(F32) + far[...].astype(F32)
    grad = (dh[...] + norm_back(da, gain[...], xhat, inv)).astype(BF)
    nb, nm = gb.shape[0], gm.shape[0]
    gb[...] = grad[:nb]
    gm[...] = grad[nb : nb + nm]
    gs[...] = grad[nb + nm :]


def exchange(value, axis, distance, size):
    return lax.ppermute(value, axis, [(i, i ^ distance) for i in range(size)])


def add_low(first, *others):
    total = first.astype(F32)
    for other in others:
        total = total + other.astype(F32)
    return total.astype(BF)


def reduce_shards(tile, order, sizes):
    part = tile.reshape(tile.shape[0], 16, tile.shape[1] // 16, tile.shape[2])
    for axis, bit in order:
        half = part.shape[1] // 2
        part = add_low(part[:, :half], exchange(part[:, half:], axis, bit, sizes[axis]))
    quarter = part.shape[1] // 4
    piece = [part[:, k * quarter : (k + 1) * quarter] for k in range(4)]
    part = add_low(
        piece[0], *[exchange(piece[k], "dp", 2 * k, sizes["dp"]) for k in range(1, 4)]
    )
    distance = 8
    while distance < sizes["dp"]:
        part = add_low(part, exchange(part, "dp", distance, sizes["dp"]))
        distance *= 2
    return part


def gather_shards(part, order, sizes):
    part = jnp.concatenate(
        [part] + [exchange(part, "dp", 2 * k, sizes["dp"]) for k in range(1, 4)], axis=1
    )
    for axis, bit in reversed(order):
        part = jnp.concatenate([part, exchange(part, axis, bit, sizes[axis])], axis=1)
    return part.reshape(part.shape[0], part.shape[1] * part.shape[2], part.shape[3])


def all_sum(value, sizes):
    for axis in ("rows", "dp"):
        distance = 1
        while distance < sizes[axis]:
            value = value + exchange(value, axis, distance, sizes[axis])
            distance *= 2
    return value


ORDER_A = (("dp", 1), ("rows", 2))
ORDER_B = (("rows", 2), ("dp", 1))


def full(shape):
    return pl.BlockSpec(shape, lambda *_: (0,) * len(shape))


def params(limit_mib):
    return pltpu.CompilerParams(vmem_limit_bytes=limit_mib * MIB)


def shards(sizes, *args):
    atoms, pairs, lengths = args[0:3], args[3:6], args[6:9]
    wq, wk, wv, wo, wu, wd = args[9:15]
    gain_one, shift_one, gain_two, shift_two = (v.reshape(1, -1) for v in args[15:19])
    dys, dpos = args[19:22], args[22:25]
    width = atoms[0].shape[-1]
    hidden_units = wu.shape[1]
    head_count = pairs[0].shape[2]
    heads = head_count * LANES // width
    scale = float((width // head_count) ** -0.5)
    groups = width // LANES
    chunks = 16

    rows_at = lax.axis_index("rows")
    dp_at = lax.axis_index("dp")
    core, y = rows_at % 2, rows_at // 2
    xa, z = dp_at % 2, (dp_at // 2) % 4
    ids = jnp.stack(
        [core, xa * 8 + y * 4 + z, y * 8 + xa * 4 + z, rows_at, core ^ 1]
    ).astype(jnp.int32)

    layout = []
    start = 0
    for a in atoms:
        mols, rows = a.shape[0] * a.shape[1], a.shape[2]
        layout.append((start, mols, rows, rows * sizes["rows"]))
        start += mols * rows
    layout = tuple(layout)
    local = start

    x = jnp.concatenate([a.reshape(-1, width) for a in atoms], axis=0)
    dy = [d.reshape(-1, width) for d in dys]
    pair = [p.reshape((-1,) + p.shape[2:]) for p in pairs]
    dpo = [p.reshape((-1,) + p.shape[2:]) for p in dpos]
    lens = [n.reshape(-1) for n in lengths]

    x1 = exchange(x, "rows", 1, sizes["rows"])
    x2 = exchange(x, "rows", 2, sizes["rows"])
    x3 = exchange(x2, "rows", 1, sizes["rows"])

    smem = pl.BlockSpec(memory_space=pltpu.SMEM)
    vmem = pl.BlockSpec(memory_space=pltpu.VMEM)
    bucket_rows = [mols * slots for _, mols, _, slots in layout]
    front_shapes = [jax.ShapeDtypeStruct((local, width), BF)]
    for size in bucket_rows:
        front_shapes += [jax.ShapeDtypeStruct((size, width), BF)] * 4
    front = pl.pallas_call(
        functools.partial(front_kernel, layout),
        out_shape=front_shapes,
        in_specs=[smem] + [vmem] * 9,
        out_specs=[vmem] * len(front_shapes),
        compiler_params=params(40),
        name="front",
    )(ids[3:4], x, x1, x2, x3, wq, wk, wv, gain_one, shift_one)
    q = front[0]
    ks, vs, a1s, xhats = (front[1 + kind :: 4] for kind in range(4))

    def blocking(bucket):
        start, mols, rows, slots = layout[bucket]
        per = max(1, 128 // slots)
        per_groups = 1 if slots >= 256 else groups
        grid = (mols // per, groups // per_groups)
        lanes = per_groups * LANES
        offset = start // (per * rows)
        row_spec = pl.BlockSpec((per * rows, lanes), lambda m, g: (offset + m, g))
        out_spec = pl.BlockSpec((per * rows, lanes), lambda m, g: (m, g))
        key_spec = pl.BlockSpec((per * slots, lanes), lambda m, g: (m, g))
        key_t_spec = pl.BlockSpec((lanes, per * slots), lambda m, g: (g, m))
        pair_spec = pl.BlockSpec(
            (per, per_groups * heads, rows, slots), lambda m, g: (m, g, 0, 0)
        )
        args = (per, per_groups, heads, rows, slots, scale)
        return args, grid, row_spec, out_spec, key_spec, key_t_spec, pair_spec

    pair_out, probs, outs = [], [], []
    for bucket in range(3):
        start, mols, rows, slots = layout[bucket]
        static, grid, row_spec, out_spec, key_spec, _, pair_spec = blocking(bucket)
        shape = pair[bucket].shape
        res = pl.pallas_call(
            functools.partial(attn_fwd_kernel, *static),
            grid=grid,
            out_shape=[
                jax.ShapeDtypeStruct(shape, BF),
                jax.ShapeDtypeStruct(shape, BF),
                jax.ShapeDtypeStruct((mols * rows, width), F32),
            ],
            in_specs=[smem, row_spec, key_spec, key_spec, pair_spec],
            out_specs=[pair_spec, pair_spec, out_spec],
            compiler_params=params(32),
            name=f"attend{bucket}",
        )(lens[bucket], q, ks[bucket], vs[bucket], pair[bucket])
        pair_out.append(res[0])
        probs.append(res[1])
        outs.append(res[2])

    tiles = 4
    tile = hidden_units // tiles
    half = tiles // 2

    def tile_at(t, ids):
        return (t + half * ids[4]) % tiles

    def whole(shape):
        return pl.BlockSpec(shape, lambda t, ids: (0,) * len(shape))

    send_spec = pl.BlockSpec((1, tile, width), lambda t, ids: (jnp.minimum(t, half - 1), 0, 0))
    keep_spec = pl.BlockSpec((1, tile, width), lambda t, ids: (jnp.maximum(t - half, 0), 0, 0))
    half_shape = jax.ShapeDtypeStruct((half, tile, width), BF)
    local_shape = (local, width)
    dense = pl.pallas_call(
        functools.partial(dense_kernel, tiles, chunks),
        grid_spec=pltpu.PrefetchScalarGridSpec(
            num_scalar_prefetch=1,
            grid=(tiles,),
            in_specs=[whole(local_shape)]
            + [whole(o.shape) for o in outs]
            + [whole(d.shape) for d in dy]
            + [
                whole(wo.shape),
                pl.BlockSpec((width, tile), lambda t, ids: (0, tile_at(t, ids))),
                pl.BlockSpec((tile, width), lambda t, ids: (tile_at(t, ids), 0)),
                whole((1, width)),
                whole((1, width)),
            ],
            out_specs=[whole(d.shape) for d in dy]
            + [whole(local_shape)] * 3
            + [whole(wo.shape), whole((8, width)), send_spec, send_spec, keep_spec, keep_spec],
            scratch_shapes=[
                pltpu.VMEM(local_shape, F32),
                pltpu.VMEM(local_shape, BF),
                pltpu.VMEM(local_shape, F32),
                pltpu.VMEM(local_shape, BF),
                pltpu.VMEM(local_shape, F32),
                pltpu.VMEM((local, LANES), F32),
                pltpu.VMEM(local_shape, F32),
                pltpu.VMEM(local_shape, F32),
            ],
        ),
        out_shape=[jax.ShapeDtypeStruct(d.shape, BF) for d in dy]
        + [
            jax.ShapeDtypeStruct(local_shape, F32),
            jax.ShapeDtypeStruct(local_shape, BF),
            jax.ShapeDtypeStruct(local_shape, BF),
            jax.ShapeDtypeStruct(wo.shape, BF),
            jax.ShapeDtypeStruct((8, width), F32),
            half_shape,
            half_shape,
            half_shape,
            half_shape,
        ],
        compiler_params=params(56),
        name="dense",
    )(ids, x, *outs, *dy, wo, wu, wd, gain_two, shift_two)
    atoms_out = dense[0:3]
    dh, do, dd, go, gs_two, up_send, down_send, up_keep, down_keep = dense[3:]

    up = add_low(up_keep, exchange(up_send, "rows", 1, sizes["rows"]))
    down = add_low(down_keep, exchange(down_send, "rows", 1, sizes["rows"]))
    up = reduce_shards(up, ORDER_A, sizes)
    down = reduce_shards(down, ORDER_B, sizes)
    up = gather_shards(up, ORDER_A, sizes)
    down = gather_shards(down, ORDER_B, sizes)
    up_other = exchange(up, "rows", 1, sizes["rows"])
    down_other = exchange(down, "rows", 1, sizes["rows"])

    grad_pair, dqs, dks, dvs = [], [], [], []
    for bucket in range(3):
        start, mols, rows, slots = layout[bucket]
        static, grid, row_spec, out_spec, key_spec, key_t_spec, pair_spec = blocking(bucket)
        res = pl.pallas_call(
            functools.partial(attn_bwd_kernel, *static),
            grid=grid,
            out_shape=[
                jax.ShapeDtypeStruct(pair[bucket].shape, BF),
                jax.ShapeDtypeStruct((mols * rows, width), BF),
                jax.ShapeDtypeStruct((width, mols * slots), BF),
                jax.ShapeDtypeStruct((width, mols * slots), BF),
            ],
            in_specs=[row_spec, key_spec, key_spec, row_spec, row_spec, pair_spec, pair_spec],
            out_specs=[pair_spec, out_spec, key_t_spec, key_t_spec],
            compiler_params=params(32),
            name=f"attend_back{bucket}",
        )(q, ks[bucket], vs[bucket], do, dd, probs[bucket], dpo[bucket])
        grad_pair.append(res[0])
        dqs.append(res[1])
        dks.append(res[2])
        dvs.append(res[3])

    pair_tiles = jax.ShapeDtypeStruct((2, width, width), BF)
    own, keep, send, gs_one, w_send, w_keep = pl.pallas_call(
        functools.partial(back_kernel, layout, chunks),
        out_shape=[
            jax.ShapeDtypeStruct(local_shape, F32),
            jax.ShapeDtypeStruct(local_shape, BF),
            jax.ShapeDtypeStruct((2,) + local_shape, BF),
            jax.ShapeDtypeStruct((8, width), F32),
            pair_tiles,
            pair_tiles,
        ],
        in_specs=[smem] + [vmem] * 19,
        out_specs=[vmem] * 6,
        scratch_shapes=[pltpu.VMEM((sum(bucket_rows), width), F32)],
        compiler_params=params(56),
        name="back",
    )(ids, *dqs, *dks, *dvs, *a1s, *xhats, wq, wk, wv, go)

    near = exchange(send, "rows", 1, sizes["rows"])
    far = exchange(add_low(keep, near[1]), "rows", 2, sizes["rows"])
    grad_atoms = pl.pallas_call(
        last_kernel,
        out_shape=[jax.ShapeDtypeStruct(d.shape, BF) for d in dy],
        in_specs=[vmem] * 6,
        out_specs=[vmem] * 3,
        compiler_params=params(32),
        name="last",
    )(x, own, near[0], far, dh, gain_one)

    rest = add_low(w_keep, exchange(w_send, "rows", 1, sizes["rows"]))
    first = gather_shards(reduce_shards(rest[0:1], ORDER_A, sizes), ORDER_A, sizes)
    second = gather_shards(reduce_shards(rest[1:2], ORDER_B, sizes), ORDER_B, sizes)
    first_other = exchange(first, "rows", 1, sizes["rows"])
    second_other = exchange(second, "rows", 1, sizes["rows"])

    gs = jnp.concatenate([gs_one[0:2], gs_two[0:2], jnp.zeros((4, width), F32)], axis=0)
    gs = all_sum(gs, sizes)

    def ordered(ref, mine):
        size = ref.shape[1] // chunks
        return [
            ref[0, pl.ds(pl.multiple_of((c ^ mine) * size, size), size), :].astype(F32)
            for c in range(chunks)
        ]

    def finish_ff(ids, up_m, up_o, down_m, down_o, gu, gd):
        own_tile = (pl.program_id(0) // half) == ids[0]

        @pl.when(own_tile)
        def _():
            gu[...] = jnp.concatenate(ordered(up_m, ids[1]), axis=0)
            gd[...] = jnp.concatenate(ordered(down_m, ids[2]), axis=0)

        @pl.when(jnp.logical_not(own_tile))
        def _():
            gu[...] = jnp.concatenate(ordered(up_o, ids[1]), axis=0)
            gd[...] = jnp.concatenate(ordered(down_o, ids[2]), axis=0)

    half_spec = pl.BlockSpec((1, tile, width), lambda t, ids: (t % half, 0, 0))
    grad_up, grad_down = pl.pallas_call(
        finish_ff,
        grid_spec=pltpu.PrefetchScalarGridSpec(
            num_scalar_prefetch=1,
            grid=(tiles,),
            in_specs=[half_spec] * 4,
            out_specs=[
                pl.BlockSpec((width, tile), lambda t, ids: (0, t)),
                pl.BlockSpec((tile, width), lambda t, ids: (t, 0)),
            ],
        ),
        out_shape=[
            jax.ShapeDtypeStruct(wu.shape, F32),
            jax.ShapeDtypeStruct(wd.shape, F32),
        ],
        compiler_params=params(32),
        name="finish_ff",
    )(ids, up, up_other, down, down_other)

    def finish_rest(ids, first_m, first_o, second_m, second_o, go_out, gq_out, gk_out, gv_out):
        def put(zero_first, zero_second, one_first, one_second):
            go_out[...] = jnp.concatenate(ordered(zero_first, ids[1]), axis=0)
            gq_out[...] = jnp.concatenate(ordered(zero_second, ids[2]), axis=0)
            gk_out[...] = jnp.concatenate(ordered(one_first, ids[1]), axis=0).T
            gv_out[...] = jnp.concatenate(ordered(one_second, ids[2]), axis=0).T

        @pl.when(ids[0] == 0)
        def _():
            put(first_m, second_m, first_o, second_o)

        @pl.when(ids[0] == 1)
        def _():
            put(first_o, second_o, first_m, second_m)

    go, gq, gk, gv = pl.pallas_call(
        finish_rest,
        out_shape=[jax.ShapeDtypeStruct(wo.shape, F32)] * 4,
        in_specs=[smem] + [vmem] * 4,
        out_specs=[vmem] * 4,
        compiler_params=params(32),
        name="finish_rest",
    )(ids, first, first_other, second, second_other)

    return (
        *[v.reshape(a.shape) for v, a in zip(atoms_out, atoms)],
        *[v.reshape(a.shape) for v, a in zip(pair_out, pairs)],
        *[v.reshape(a.shape) for v, a in zip(grad_atoms, atoms)],
        *[v.reshape(a.shape) for v, a in zip(grad_pair, pairs)],
        gq,
        gk,
        gv,
        go,
        grad_up,
        grad_down,
        gs[0],
        gs[1],
        gs[2],
        gs[3],
    )


def solution(mesh):
    atom = P(None, "dp", "rows", None)
    pair = P(None, "dp", None, "rows", None)
    length = P(None, "dp")
    in_specs = (
        (atom,) * 3 + (pair,) * 3 + (length,) * 3 + (P(),) * 10 + (atom,) * 3 + (pair,) * 3
    )
    out_specs = (atom,) * 3 + (pair,) * 3 + (atom,) * 3 + (pair,) * 3 + (P(),) * 10
    body = functools.partial(shards, dict(mesh.shape))
    return jax.shard_map(
        body, mesh=mesh, in_specs=in_specs, out_specs=out_specs, check_vma=False
    )
```

time: 2080 us -> 305 us (0.15)
  blocking collectives: 1040 us -> 0 us
  matrix products: 469 us -> 0 us
  other arithmetic: 196 us -> 4.48 us
  local copies, waits for them, and re-layouts: 163 us -> 35.2 us
  Pallas kernels: 0 us -> 110 us
  waiting for transfers between devices: 177 us -> 90.7 us
  starting transfers between devices: 1.01 us -> 62.1 us
    unnamed x1 -> x0, blocking collectives: 847 us -> none
    dot_general x284 -> x0, matrix products: 437 us -> none  [the longest x72 179 us: outer_sum(): lax.dot_general(flat_left, flat_right, (((0,), (0,)), ((), ())), preferre...]
    psum x1 -> x0, waiting for transfers between devices: 177 us -> none  [shards(): totals = lax.psum(totals, ('dp', 'rows'))]
    all_gather x24 -> x0, blocking collectives: 151 us -> none  [the longest x4 29.1 us: shards(): lax.all_gather(outgoing[1], 'rows', axis=1, tiled=True)]
    pallas_call x0 -> x12, Pallas kernels: none -> 110 us  [the longest x3 37.8 us: shards(): pl.pallas_call(functools.partial(attn_bwd_kernel, *static), grid=grid, ou...]
    sub x8 -> x0, other arithmetic: 107 us -> none  [backward_rest(): grad_softmax - row_inner]
    ppermute x0 -> x57, waiting for transfers between devices: none -> 90.7 us  [exchange(): return lax.ppermute(value, axis, [(i, i ^ distance) for i in range(size)])]
    ppermute x0 -> x57, starting transfers between devices: none -> 62.1 us  [exchange(): return lax.ppermute(value, axis, [(i, i ^ distance) for i in range(size)])]
  transfers between devices with their start and end apart: 9 -> 57, of which waited for: 1 -> 31; matrix products, arithmetic and copies ran while one was open for 32% -> 3% of each run, Pallas kernels for 0% -> 2%
where the time goes in v1:
time: 305 us; the launch traced here: 304 us
  Pallas kernels  110 us (36%)
  waiting for transfers between devices  90.7 us (30%)
  starting transfers between devices  62.1 us (20%)
  local copies, waits for them, and re-layouts  35.2 us (12%)
  other arithmetic  4.48 us (1%)
    ppermute x57, waiting for transfers between devices, exchange(): return lax.ppermute(value, axis, [(i, i ^ distance) for i in range(size)])  90.7 us
    ppermute x57, starting transfers between devices, exchange(): return lax.ppermute(value, axis, [(i, i ^ distance) for i in range(size)])  62.1 us
    pallas_call x3, Pallas kernels, shards(): pl.pallas_call(functools.partial(attn_bwd_kernel, *static), grid=grid, ou...  37.8 us
    pallas_call x3, Pallas kernels, shards(): pl.pallas_call(functools.partial(attn_fwd_kernel, *static), grid=grid, ou...  32.1 us
    unnamed x121, local copies, waits for them, and re-layouts  31.8 us
    pallas_call x1, Pallas kernels, shards(): pl.pallas_call(functools.partial(dense_kernel, tiles, chunks), grid_spec=...  16.4 us
    pallas_call x1, Pallas kernels, shards(): pl.pallas_call(functools.partial(back_kernel, layout, chunks), out_shape=...  12 us
  transfers between devices with their start and end apart: 57, of which 31 were waited for; matrix products, arithmetic and copies ran while one was open for 3% of the time, Pallas kernels for 2%

profile of v1, /device:TPU:0, one launch (start us, length us, event | category | flops | bytes accessed | tf_op | source)
XLA Modules:
  0.0 304.2 jit_solution(11952711961485919526)
XLA Ops:
  1.8 3.0 collective-permute-start.1
  4.8 11.9 %collective-permute-done.1.x2 = bf16[512,512]{1,0:T(8,128)(2,1)S(1)} collective-permute-done((bf16[512,512]{1,0:T(8,128)(2,1)S(1)}, bf16[512,512]{1,0:T(8,128)(2,1)S(1)}, u32[]{:S(2)}, u32[]{:S(2)}) %collective-permute-start.1) | collective-permute-done | bytes 524320 | tf_op jit(solution)/shard_map/ppermute | solution.py:316
  25.0 3.2 %front.1 = (bf16[512,512]{1,0:T(8,128)(2,1)S(1)}, bf16[1024,512]{1,0:T(8,128)(2,1)S(1)}, bf16[1024,512]{1,0:T(8,128)(2,1)S(1)}, bf16[1024,512]{1,0:T(8,128)(2,1)...) custom-call(s32[1]{0:T(128)} %bitcast.3.me_ref, ...), custom_call_target="tpu_custom_call" | custom-call | tf_op jit(solution)/shard_map/front/pallas_call | solution.py:419
  31.8 4.1 %copy-done.2 = bf16[4,1,64,64,256]{4,3,2,1,0:T(8,128)(2,1)S(1)} copy-done((bf16[4,1,64,64,256]{4,3,2,1,0:T(8,128)(2,1)S(1)}, bf16[4,1,64,64,256]{4,3,2,1,0:T(8,128)(2,1)}, u32[]{:S(2)}) %copy-start.2) | copy-done | bytes 8388632
  36.0 20.1 %attend0.1 = (bf16[4,64,64,256]{3,2,1,0:T(8,128)(2,1)}, bf16[4,64,64,256]{3,2,1,0:T(8,128)(2,1)S(1)}, f32[256,512]{1,0:T(8,128)S(1)}) custom-call(s32[4]{0:T(128)S(1)} %bitcast.87, bf16[512,512]{1,0:T(8,128)(2,1)S(1)} %get-tuple-element.83.q_ref, bf16[1024,512]{1,0:T(8,128)(2,1)S(1)} %get-tuple-element.84.k_ref, ...), custom_call_target="tpu_custom_call" | custom-call | tf_op jit(solution)/shard_map/attend0/pallas_call | solution.py:452
  56.1 3.4 %copy-done.4 = bf16[4,64,64,256]{3,2,1,0:T(8,128)(2,1)} copy-done((bf16[4,64,64,256]{3,2,1,0:T(8,128)(2,1)}, bf16[4,64,64,256]{3,2,1,0:T(8,128)(2,1)S(1)}, u32[]{:S(2)}) %copy-start.4) | copy-done | bytes 8388632
  59.5 5.9 %attend1.1 = (bf16[4,64,32,128]{3,2,1,0:T(8,128)(2,1)}, bf16[4,64,32,128]{3,2,1,0:T(8,128)(2,1)S(1)}, f32[128,512]{1,0:T(8,128)S(1)}) custom-call(s32[4]{0:T(128)S(1)} %bitcast.88, bf16[512,512]{1,0:T(8,128)(2,1)S(1)} %get-tuple-element.83.q_ref, bf16[512,512]{1,0:T(8,128)(2,1)S(1)} %get-tuple-element.87.k_ref, ...), custom_call_target="tpu_custom_call" | custom-call | tf_op jit(solution)/shard_map/attend1/pallas_call | solution.py:452
  65.5 6.0 %attend2.1 = (bf16[8,64,16,64]{3,2,1,0:T(8,128)(2,1)}, bf16[8,64,16,64]{3,2,1,0:T(8,128)(2,1)S(1)}, f32[128,512]{1,0:T(8,128)S(1)}) custom-call(s32[8]{0:T(128)S(1)} %reshape.172.len_ref, bf16[512,512]{1,0:T(8,128)(2,1)S(1)} %get-tuple-element.83.q_ref, bf16[512,512]{1,0:T(8,128)(2,1)S(1)} %get-tuple-element.90.k_ref, ...), custom_call_target="tpu_custom_call" | custom-call | tf_op jit(solution)/shard_map/attend2/pallas_call | solution.py:452
  72.2 16.4 %dense.1 = (bf16[256,512]{1,0:T(8,128)(2,1)}, bf16[128,512]{1,0:T(8,128)(2,1)}, bf16[128,512]{1,0:T(8,128)(2,1)}, f32[512,512]{1,0:T(8,128)}, bf16[512,512]{1,0:...) custom-call(s32[5]{0:T(128)} %stack.23.ids, ...), custom_call_target="tpu_custom_call" | custom-call | tf_op jit(solution)/shard_map/dense/pallas_call | solution.py:483
  88.7 3.4 %copy-done.3 = bf16[4,1,64,64,256]{4,3,2,1,0:T(8,128)(2,1)S(1)} copy-done((bf16[4,1,64,64,256]{4,3,2,1,0:T(8,128)(2,1)S(1)}, bf16[4,1,64,64,256]{4,3,2,1,0:T(8,128)(2,1)}, u32[]{:S(2)}) %copy-start.3) | copy-done | bytes 8388632
  92.0 3.4 %copy-done.5 = bf16[4,64,64,256]{3,2,1,0:T(8,128)(2,1)S(1)} copy-done((bf16[4,64,64,256]{3,2,1,0:T(8,128)(2,1)S(1)}, bf16[4,64,64,256]{3,2,1,0:T(8,128)(2,1)}, u32[]{:S(2)}) %copy-start.5) | copy-done | bytes 8388632
  97.5 20.8 %attend_back0.1 = (bf16[4,64,64,256]{3,2,1,0:T(8,128)(2,1)}, bf16[256,512]{1,0:T(8,128)(2,1)S(1)}, bf16[512,1024]{1,0:T(8,128)(2,1)S(1)}, bf16[512,1024]{1,0:T(8,128)(2,1)S(1)}) custom-call(bf16[512,512]{1,0:T(8,128)(2,1)S(1)} %get-tuple-element.83.q_ref, bf16[1024,512]{1,0:T(8,128)(2,1)S(1)} %get-tuple-element.84.k_ref, ...), custom_call_target="tpu_custom_call" | custom-call | tf_op jit(solution)/shard_map/attend_back0/pallas_call | solution.py:543
  118.4 8.8 %attend_back1.1 = (bf16[4,64,32,128]{3,2,1,0:T(8,128)(2,1)}, bf16[128,512]{1,0:T(8,128)(2,1)S(1)}, bf16[512,512]{1,0:T(8,128)(2,1)S(1)}, bf16[512,512]{1,0:T(8,128)(2,1)S(1)}) custom-call(bf16[512,512]{1,0:T(8,128)(2,1)S(1)} %get-tuple-element.83.q_ref, bf16[512,512]{1,0:T(8,128)(2,1)S(1)} %copy-done.16, bf16[512,512]{1,0:T(8,128)(2,1)S(1)} %copy-done.18, ...), custom_call_target="tpu_custom_call" | custom-call | tf_op jit(solution)/shard_map/attend_back1/pallas_call | solution.py:543
  128.8 8.2 %attend_back2.1 = (bf16[8,64,16,64]{3,2,1,0:T(8,128)(2,1)}, bf16[128,512]{1,0:T(8,128)(2,1)S(1)}, bf16[512,512]{1,0:T(8,128)(2,1)S(1)}, bf16[512,512]{1,0:T(8,128)(2,1)S(1)}) custom-call(bf16[512,512]{1,0:T(8,128)(2,1)S(1)} %get-tuple-element.83.q_ref, bf16[512,512]{1,0:T(8,128)(2,1)S(1)} %get-tuple-element.90.k_ref, ...), custom_call_target="tpu_custom_call" | custom-call | tf_op jit(solution)/shard_map/attend_back2/pallas_call | solution.py:543
  139.3 12.0 %back.1 = (f32[512,512]{1,0:T(8,128)}, bf16[512,512]{1,0:T(8,128)(2,1)}, bf16[2,512,512]{2,1,0:T(8,128)(2,1)}, f32[8,512]{1,0:T(8,128)}, bf16[2,512,512]{2,1,0:T(8,128)(2,1)}, /*index=5*/bf16[2,512,512]{2,1,0:T(8,128)(2,1)}) custom-call(s32[5]{0:T(128)} %stack.23.ids, bf16[256,512]{1,0:T(8,128)(2,1)} %copy-done.36, bf16[128,512]{1,0:T(8,128)(2,1)} %copy-done.39, ...), custom_call_target="tpu_custom_call" | custom-call | tf_op jit(solution)/shard_map/back/pallas_call | solution.py:563
  153.9 1.6 collective-permute-done.52
  155.5 1.7 collective-permute-start.53
  157.3 2.0 collective-permute-done.53
  159.3 1.7 collective-permute-start.54
  161.0 2.0 collective-permute-done.54
  163.0 1.8 collective-permute-start.55
  164.8 1.9 collective-permute-done.55
  166.8 2.9 collective-permute-start.56
  169.7 1.5 add_convert_fusion.2
  171.3 1.6 collective-permute-start.6
  173.0 1.6 collective-permute-start.17
  175.3 2.5 collective-permute-done.6
  177.9 1.6 collective-permute-start.7
  181.1 1.8 collective-permute-done.7
  184.3 1.7 collective-permute-start.9
  190.9 2.2 collective-permute-start.19
  194.5 1.9 collective-permute-start.29
  198.4 3.2 %collective-permute-done.11 = bf16[1,1,32,512]{3,2,1,0:T(8,128)(2,1)S(1)} collective-permute-done((bf16[1,1,32,512]{3,2,1,0:T(8,128)(2,1)S(1)}, bf16[1,1,32,512]{3,2,1,0:T(8,128)(2,1)S(1)}, u32[]{:S(2)}, u32[]{:S(2)}) %collective-permute-start.11) | collective-permute-done | bytes 32800 | tf_op jit(solution)/shard_map/ppermute | solution.py:316
  202.1 4.5 %collective-permute-done.12 = bf16[1,1,32,512]{3,2,1,0:T(8,128)(2,1)S(1)} collective-permute-done((bf16[1,1,32,512]{3,2,1,0:T(8,128)(2,1)S(1)}, bf16[1,1,32,512]{3,2,1,0:T(8,128)(2,1)S(1)}, u32[]{:S(2)}, u32[]{:S(2)}) %collective-permute-start.12) | collective-permute-done | bytes 32800 | tf_op jit(solution)/shard_map/ppermute | solution.py:316
  206.6 1.9 collective-permute-start.13
  208.5 3.8 %collective-permute-done.13 = bf16[1,1,32,512]{3,2,1,0:T(8,128)(2,1)S(1)} collective-permute-done((bf16[1,1,32,512]{3,2,1,0:T(8,128)(2,1)S(1)}, bf16[1,1,32,512]{3,2,1,0:T(8,128)(2,1)S(1)}, u32[]{:S(2)}, u32[]{:S(2)}) %collective-permute-start.13) | collective-permute-done | bytes 32800 | tf_op jit(solution)/shard_map/ppermute | solution.py:316
  212.3 3.9 %collective-permute-done.22 = bf16[1,1,32,512]{3,2,1,0:T(8,128)(2,1)S(1)} collective-permute-done((bf16[1,1,32,512]{3,2,1,0:T(8,128)(2,1)S(1)}, bf16[1,1,32,512]{3,2,1,0:T(8,128)(2,1)S(1)}, u32[]{:S(2)}, u32[]{:S(2)}) %collective-permute-start.22) | collective-permute-done | bytes 32800 | tf_op jit(solution)/shard_map/ppermute | solution.py:316
  218.6 4.2 %collective-permute-done.30 = bf16[2,4,32,512]{3,2,1,0:T(8,128)(2,1)S(1)} collective-permute-done((bf16[2,4,32,512]{3,2,1,0:T(8,128)(2,1)S(1)}, bf16[2,4,32,512]{3,2,1,0:T(8,128)(2,1)S(1)}, u32[]{:S(2)}, u32[]{:S(2)}) %collective-permute-start.30) | collective-permute-done | bytes 262176 | tf_op jit(solution)/shard_map/ppermute | solution.py:316
  223.0 2.0 collective-permute-start.33
  224.9 2.5 collective-permute-start.31
  227.5 2.2 collective-permute-done.33
  229.7 1.8 collective-permute-start.45
  232.1 2.5 collective-permute-start.43
  234.6 1.5 collective-permute-done.45
  236.1 2.4 collective-permute-done.44
  238.6 1.9 collective-permute-start.36
  240.6 1.6 collective-permute-start.46
  242.2 1.6 collective-permute-done.35
  245.0 2.0 collective-permute-start.48
  248.9 2.0 collective-permute-start.37
  251.1 2.0 collective-permute-start.49
  253.2 4.3 %collective-permute-done.37 = bf16[2,4,32,512]{3,2,1,0:T(8,128)(2,1)S(1)} collective-permute-done((bf16[2,4,32,512]{3,2,1,0:T(8,128)(2,1)S(1)}, bf16[2,4,32,512]{3,2,1,0:T(8,128)(2,1)S(1)}, u32[]{:S(2)}, u32[]{:S(2)}) %collective-permute-start.37) | collective-permute-done | bytes 262176 | tf_op jit(solution)/shard_map/ppermute | solution.py:316
  257.5 1.7 collective-permute-start.24
  260.7 2.6 collective-permute-done.24
  263.2 1.7 collective-permute-start.14
  265.0 5.4 %collective-permute-done.14 = bf16[1,4,32,512]{3,2,1,0:T(8,128)(2,1)S(1)} collective-permute-done((bf16[1,4,32,512]{3,2,1,0:T(8,128)(2,1)S(1)}, bf16[1,4,32,512]{3,2,1,0:T(8,128)(2,1)S(1)}, u32[]{:S(2)}, u32[]{:S(2)}) %collective-permute-start.14) | collective-permute-done | bytes 131104 | tf_op jit(solution)/shard_map/ppermute | solution.py:316
  270.4 1.7 collective-permute-start.25
  272.7 2.6 collective-permute-done.25
  276.5 2.1 collective-permute-done.15
  279.1 5.5 %collective-permute-done.26 = bf16[1,8,32,512]{3,2,1,0:T(8,128)(2,1)S(1)} collective-permute-done((bf16[1,8,32,512]{3,2,1,0:T(8,128)(2,1)S(1)}, bf16[1,8,32,512]{3,2,1,0:T(8,128)(2,1)S(1)}, u32[]{:S(2)}, u32[]{:S(2)}) %collective-permute-start.26) | collective-permute-done | bytes 262176 | tf_op jit(solution)/shard_map/ppermute | solution.py:316
  285.8 9.6 %collective-permute-done.4.far = bf16[512,512]{1,0:T(8,128)(2,1)S(1)} collective-permute-done((bf16[512,512]{1,0:T(8,128)(2,1)S(1)}, bf16[512,512]{1,0:T(8,128)(2,1)S(1)}, u32[]{:S(2)}, u32[]{:S(2)}) %collective-permute-start.4) | collective-permute-done | bytes 524320 | tf_op jit(solution)/shard_map/ppermute | solution.py:316
  295.4 1.5 last.1
  297.0 3.1 %finish_rest.1 = (f32[512,512]{1,0:T(8,128)}, f32[512,512]{1,0:T(8,128)}, f32[512,512]{1,0:T(8,128)}, f32[512,512]{1,0:T(8,128)}) custom-call(s32[5]{0:T(128)S(1)} %copy-done.41, bf16[1,512,512]{2,1,0:T(8,128)(2,1)S(1)} %bitcast.83, bf16[1,512,512]{2,1,0:T(8,128)(2,1)S(1)} %collective-permute-done.16.first_o, bf16[1,512,512]{2,1,0:T(8,128)(2,1)S(1)} %bitcast.81, ...), custom_call_target="tpu_custom_call" | custom-call | tf_op jit(solution)/shard_map/finish_rest/pallas_call | solution.py:655
  300.0 4.2 %finish_ff.1 = (f32[512,2048]{1,0:T(8,128)}, f32[2048,512]{1,0:T(8,128)}) custom-call(s32[5]{0:T(128)S(1)} %copy-done.41, bf16[2,512,512]{2,1,0:T(8,128)(2,1)S(1)} %bitcast.77, bf16[2,512,512]{2,1,0:T(8,128)(2,1)S(1)} %collective-permute-done.39.up_o, bf16[2,512,512]{2,1,0:T(8,128)(2,1)S(1)} %bitcast.79, bf16[2,512,512]{2,1,0:T(8,128)(2,1)S(1)} %collective-permute-done.51.down_o), custom_call_target="tpu_custom_call" | custom-call | tf_op jit(solution)/shard_map/finish_ff/pallas_call | solution.py:621
  (239 shorter events, 46.6 us)
Async XLA Ops:
  1.8 54.3 %copy-start = (bf16[512,512]{1,0:T(8,128)(2,1)}, bf16[512,512]{1,0:T(8,128)(2,1)S(1)}, u32[]{:S(2)}) copy-start(bf16[512,512]{1,0:T(8,128)(2,1)S(1)} %pad_maximum_fusion.x0.x_ref) | copy-start | bytes 1572868
  1.8 30.0 %copy-start.45 = (s32[4,1]{0,1:T(1,128)S(1)}, s32[4,1]{0,1:T(1,128)}, u32[]{:S(2)}) copy-start(s32[4,1]{0,1:T(1,128)} %param.31) | copy-start | bytes 52
  1.8 15.0 %collective-permute-start.1 = (bf16[512,512]{1,0:T(8,128)(2,1)S(1)}, bf16[512,512]{1,0:T(8,128)(2,1)S(1)}, u32[]{:S(2)}, u32[]{:S(2)}) collective-permute-start(bf16[512,512]{1,0:T(8,128)(2,1)S(1)} %pad_maximum_fusion.x0.x_ref), channel_id=1, source_target_pairs={{0,2},{1,3},{2,0},{3,1},{4,6},{5,7},{6,4},{7,5},{8,10},{9,11},{10,... | collective-permute-start | bytes 1572872 | tf_op jit(solution)/shard_map/ppermute | solution.py:316
  4.8 13.4 %collective-permute-start = (bf16[512,512]{1,0:T(8,128)(2,1)S(1)}, bf16[512,512]{1,0:T(8,128)(2,1)S(1)}, u32[]{:S(2)}, u32[]{:S(2)}) collective-permute-start(bf16[512,512]{1,0:T(8,128)(2,1)S(1)} %pad_maximum_fusion.x0.x_ref), channel_id=1, source_target_pairs={{0,1},{1,0},{2,3},{3,2},{4,5},{5,4},{6,7},{7,6},{8,9},{9,8},{10,11... | collective-permute-start | bytes 1572872 | tf_op jit(solution)/shard_map/ppermute | solution.py:316
  16.8 1.9 collective-permute-start.2
  31.8 24.3 %copy-start.29 = (bf16[512,512]{1,0:T(8,128)(2,1)}, bf16[512,512]{1,0:T(8,128)(2,1)S(1)}, u32[]{:S(2)}) copy-start(bf16[512,512]{1,0:T(8,128)(2,1)S(1)} %get-tuple-element.115.as_) | copy-start | bytes 1572868
  31.8 24.3 %copy-start.30 = (bf16[512,512]{1,0:T(8,128)(2,1)}, bf16[512,512]{1,0:T(8,128)(2,1)S(1)}, u32[]{:S(2)}) copy-start(bf16[512,512]{1,0:T(8,128)(2,1)S(1)} %get-tuple-element.118.hs) | copy-start | bytes 1572868
  31.8 27.7 %copy-start.15 = (bf16[512,512]{1,0:T(8,128)(2,1)}, bf16[512,512]{1,0:T(8,128)(2,1)S(1)}, u32[]{:S(2)}) copy-start(bf16[512,512]{1,0:T(8,128)(2,1)S(1)} %get-tuple-element.87.k_ref) | copy-start | bytes 1572868
  31.8 27.7 %copy-start.17 = (bf16[512,512]{1,0:T(8,128)(2,1)}, bf16[512,512]{1,0:T(8,128)(2,1)S(1)}, u32[]{:S(2)}) copy-start(bf16[512,512]{1,0:T(8,128)(2,1)S(1)} %get-tuple-element.88.v_ref) | copy-start | bytes 1572868
  36.0 23.6 %copy-start.46 = (s32[4,1]{0,1:T(1,128)S(1)}, s32[4,1]{0,1:T(1,128)}, u32[]{:S(2)}) copy-start(s32[4,1]{0,1:T(1,128)} %param.32) | copy-start | bytes 52
  151.3 18.4 %collective-permute-start.5 = (bf16[2,512,512]{2,1,0:T(8,128)(2,1)}, bf16[2,512,512]{2,1,0:T(8,128)(2,1)S(1)}, u32[]{:S(2)}, u32[]{:S(2)}) collective-permute-start(bf16[2,512,512]{2,1,0:T(8,128)(2,1)} %get-tuple-element.131), channel_id=1, source_target_pairs={{0,1},{1,0},{2,3},{3,2},{4,5},{5,4},{6,7},{7,6},{8,9},{9,8},{10,11... | collective-permute-start | bytes 3145736 | tf_op jit(solution)/shard_map/ppermute | solution.py:316
  151.5 21.5 %collective-permute-start.28 = (bf16[2,512,512]{2,1,0:T(8,128)(2,1)S(1)}, bf16[2,512,512]{2,1,0:T(8,128)(2,1)S(1)}, u32[]{:S(2)}, u32[]{:S(2)}) collective-permute-start(bf16[2,512,512]{2,1,0:T(8,128)(2,1)S(1)} %copy-done.51), channel_id=1, source_target_pairs={{0,1},{1,0},{2,3},{3,2},{4,5},{5,4},{6,7},{7,6},{8,9},{9,8},{10,11... | collective-permute-start | bytes 3145736 | tf_op jit(solution)/shard_map/ppermute | solution.py:316
  153.4 2.1 collective-permute-start.52
  153.5 21.3 %collective-permute-start.40 = (bf16[2,512,512]{2,1,0:T(8,128)(2,1)S(1)}, bf16[2,512,512]{2,1,0:T(8,128)(2,1)S(1)}, u32[]{:S(2)}, u32[]{:S(2)}) collective-permute-start(bf16[2,512,512]{2,1,0:T(8,128)(2,1)S(1)} %copy-done.50), channel_id=1, source_target_pairs={{0,1},{1,0},{2,3},{3,2},{4,5},{5,4},{6,7},{7,6},{8,9},{9,8},{10,11... | collective-permute-start | bytes 3145736 | tf_op jit(solution)/shard_map/ppermute | solution.py:316
  155.5 3.7 %collective-permute-start.53 = (f32[8,512]{1,0:T(8,128)S(1)}, f32[8,512]{1,0:T(8,128)S(1)}, u32[]{:S(2)}, u32[]{:S(2)}) collective-permute-start(f32[8,512]{1,0:T(8,128)S(1)} %fusion.1), channel_id=1, source_target_pairs={{0,2},{1,3},{2,0},{3,1},{4,6},{5,7},{6,4},{7,5},{8,10},{9,11},{10,... | collective-permute-start | bytes 49160 | tf_op jit(solution)/shard_map/ppermute | solution.py:316
  159.3 3.7 %collective-permute-start.54 = (f32[8,512]{1,0:T(8,128)S(1)}, f32[8,512]{1,0:T(8,128)S(1)}, u32[]{:S(2)}, u32[]{:S(2)}) collective-permute-start(f32[8,512]{1,0:T(8,128)S(1)} %add.143), channel_id=1, source_target_pairs={{0,4},{4,0},{8,12},{12,8},{16,20},{20,16},{24,28},{28,24},{1,5},{5... | collective-permute-start | bytes 49160 | tf_op jit(solution)/shard_map/ppermute | solution.py:316
  163.0 3.7 %collective-permute-start.55 = (f32[8,512]{1,0:T(8,128)S(1)}, f32[8,512]{1,0:T(8,128)S(1)}, u32[]{:S(2)}, u32[]{:S(2)}) collective-permute-start(f32[8,512]{1,0:T(8,128)S(1)} %add.144), channel_id=1, source_target_pairs={{0,8},{4,12},{8,0},{12,4},{16,24},{20,28},{24,16},{28,20},{1,9},{5... | collective-permute-start | bytes 49160 | tf_op jit(solution)/shard_map/ppermute | solution.py:316
  164.8 110.5 %collective-permute-start.3 = (bf16[2,512,512]{2,1,0:T(8,128)(2,1)}, bf16[2,512,512]{2,1,0:T(8,128)(2,1)S(1)}, u32[]{:S(2)}, u32[]{:S(2)}) collective-permute-start(bf16[2,512,512]{2,1,0:T(8,128)(2,1)} %get-tuple-element.121), channel_id=1, source_target_pairs={{0,1},{1,0},{2,3},{3,2},{4,5},{5,4},{6,7},{7,6},{8,9},{9,8},{10,11... | collective-permute-start | bytes 3145736 | tf_op jit(solution)/shard_map/ppermute | solution.py:316
  166.8 117.8 %collective-permute-start.56 = (f32[8,512]{1,0:T(8,128)S(1)}, f32[8,512]{1,0:T(8,128)S(1)}, u32[]{:S(2)}, u32[]{:S(2)}) collective-permute-start(f32[8,512]{1,0:T(8,128)S(1)} %add.145), channel_id=1, source_target_pairs={{0,16},{4,20},{8,24},{12,28},{16,0},{20,4},{24,8},{28,12},{1,17},{... | collective-permute-start | bytes 49160 | tf_op jit(solution)/shard_map/ppermute | solution.py:316
  171.3 6.4 %collective-permute-start.6 = (bf16[1,8,32,512]{3,2,1,0:T(8,128)(2,1)S(1)}, bf16[1,8,32,512]{3,2,1,0:T(8,128)(2,1)S(1)}, u32[]{:S(2)}, u32[]{:S(2)}) collective-permute-start(bf16[1,8,32,512]{3,2,1,0:T(8,128)(2,1)S(1)} %slice.172), channel_id=1, source_target_pairs={{0,4},{4,0},{8,12},{12,8},{16,20},{20,16},{24,28},{28,24},{1,5},{5... | collective-permute-start | bytes 786440 | tf_op jit(solution)/shard_map/ppermute | solution.py:316
  173.0 7.8 %collective-permute-start.17 = (bf16[1,8,32,512]{3,2,1,0:T(8,128)(2,1)S(1)}, bf16[1,8,32,512]{3,2,1,0:T(8,128)(2,1)S(1)}, u32[]{:S(2)}, u32[]{:S(2)}) collective-permute-start(bf16[1,8,32,512]{3,2,1,0:T(8,128)(2,1)S(1)} %slice.181), channel_id=1, source_target_pairs={{0,2},{1,3},{2,0},{3,1},{4,6},{5,7},{6,4},{7,5},{8,10},{9,11},{10,... | collective-permute-start | bytes 786440 | tf_op jit(solution)/shard_map/ppermute | solution.py:316
  177.9 5.0 %collective-permute-start.7 = (bf16[1,4,32,512]{3,2,1,0:T(8,128)(2,1)S(1)}, bf16[1,4,32,512]{3,2,1,0:T(8,128)(2,1)S(1)}, u32[]{:S(2)}, u32[]{:S(2)}) collective-permute-start(bf16[1,4,32,512]{3,2,1,0:T(8,128)(2,1)S(1)} %slice.174), channel_id=1, source_target_pairs={{0,2},{1,3},{2,0},{3,1},{4,6},{5,7},{6,4},{7,5},{8,10},{9,11},{10,... | collective-permute-start | bytes 393224 | tf_op jit(solution)/shard_map/ppermute | solution.py:316
  180.9 5.1 %collective-permute-start.18 = (bf16[1,4,32,512]{3,2,1,0:T(8,128)(2,1)S(1)}, bf16[1,4,32,512]{3,2,1,0:T(8,128)(2,1)S(1)}, u32[]{:S(2)}, u32[]{:S(2)}) collective-permute-start(bf16[1,4,32,512]{3,2,1,0:T(8,128)(2,1)S(1)} %slice.183), channel_id=1, source_target_pairs={{0,4},{4,0},{8,12},{12,8},{16,20},{20,16},{24,28},{28,24},{1,5},{5... | collective-permute-start | bytes 393224 | tf_op jit(solution)/shard_map/ppermute | solution.py:316
  182.9 5.8 %collective-permute-start.10 = (bf16[1,1,32,512]{3,2,1,0:T(8,128)(2,1)S(1)}, bf16[1,1,32,512]{3,2,1,0:T(8,128)(2,1)S(1)}, u32[]{:S(2)}, u32[]{:S(2)}) collective-permute-start(bf16[1,1,32,512]{3,2,1,0:T(8,128)(2,1)S(1)} %get-tuple-element.216), channel_id=1, source_target_pairs={{0,24},{4,28},{8,16},{12,20},{16,8},{20,12},{24,0},{28,4},{1,25},{... | collective-permute-start | bytes 98312 | tf_op jit(solution)/shard_map/ppermute | solution.py:316
  184.3 6.2 %collective-permute-start.9 = (bf16[1,1,32,512]{3,2,1,0:T(8,128)(2,1)S(1)}, bf16[1,1,32,512]{3,2,1,0:T(8,128)(2,1)S(1)}, u32[]{:S(2)}, u32[]{:S(2)}) collective-permute-start(bf16[1,1,32,512]{3,2,1,0:T(8,128)(2,1)S(1)} %get-tuple-element.217), channel_id=1, source_target_pairs={{0,16},{4,20},{8,24},{12,28},{16,0},{20,4},{24,8},{28,12},{1,17},{... | collective-permute-start | bytes 98312 | tf_op jit(solution)/shard_map/ppermute | solution.py:316
  186.0 4.9 %collective-permute-start.8 = (bf16[1,1,32,512]{3,2,1,0:T(8,128)(2,1)S(1)}, bf16[1,1,32,512]{3,2,1,0:T(8,128)(2,1)S(1)}, u32[]{:S(2)}, u32[]{:S(2)}) collective-permute-start(bf16[1,1,32,512]{3,2,1,0:T(8,128)(2,1)S(1)} %get-tuple-element.215), channel_id=1, source_target_pairs={{0,8},{4,12},{8,0},{12,4},{16,24},{20,28},{24,16},{28,20},{1,9},{5... | collective-permute-start | bytes 98312 | tf_op jit(solution)/shard_map/ppermute | solution.py:316
  188.7 5.8 %collective-permute-start.21 = (bf16[1,1,32,512]{3,2,1,0:T(8,128)(2,1)S(1)}, bf16[1,1,32,512]{3,2,1,0:T(8,128)(2,1)S(1)}, u32[]{:S(2)}, u32[]{:S(2)}) collective-permute-start(bf16[1,1,32,512]{3,2,1,0:T(8,128)(2,1)S(1)} %get-tuple-element.211), channel_id=1, source_target_pairs={{0,24},{4,28},{8,16},{12,20},{16,8},{20,12},{24,0},{28,4},{1,25},{... | collective-permute-start | bytes 98312 | tf_op jit(solution)/shard_map/ppermute | solution.py:316
  190.5 5.8 %collective-permute-start.20 = (bf16[1,1,32,512]{3,2,1,0:T(8,128)(2,1)S(1)}, bf16[1,1,32,512]{3,2,1,0:T(8,128)(2,1)S(1)}, u32[]{:S(2)}, u32[]{:S(2)}) collective-permute-start(bf16[1,1,32,512]{3,2,1,0:T(8,128)(2,1)S(1)} %get-tuple-element.212), channel_id=1, source_target_pairs={{0,16},{4,20},{8,24},{12,28},{16,0},{20,4},{24,8},{28,12},{1,17},{... | collective-permute-start | bytes 98312 | tf_op jit(solution)/shard_map/ppermute | solution.py:316
  190.9 6.7 %collective-permute-start.19 = (bf16[1,1,32,512]{3,2,1,0:T(8,128)(2,1)S(1)}, bf16[1,1,32,512]{3,2,1,0:T(8,128)(2,1)S(1)}, u32[]{:S(2)}, u32[]{:S(2)}) collective-permute-start(bf16[1,1,32,512]{3,2,1,0:T(8,128)(2,1)S(1)} %get-tuple-element.210), channel_id=1, source_target_pairs={{0,8},{4,12},{8,0},{12,4},{16,24},{20,28},{24,16},{28,20},{1,9},{5... | collective-permute-start | bytes 98312 | tf_op jit(solution)/shard_map/ppermute | solution.py:316
  194.5 21.7 %collective-permute-start.29 = (bf16[2,8,32,512]{3,2,1,0:T(8,128)(2,1)S(1)}, bf16[2,8,32,512]{3,2,1,0:T(8,128)(2,1)S(1)}, u32[]{:S(2)}, u32[]{:S(2)}) collective-permute-start(bf16[2,8,32,512]{3,2,1,0:T(8,128)(2,1)S(1)} %slice.189), channel_id=1, source_target_pairs={{0,4},{4,0},{8,12},{12,8},{16,20},{20,16},{24,28},{28,24},{1,5},{5... | collective-permute-start | bytes 1572872 | tf_op jit(solution)/shard_map/ppermute | solution.py:316
  196.4 20.9 %collective-permute-start.41 = (bf16[2,8,32,512]{3,2,1,0:T(8,128)(2,1)S(1)}, bf16[2,8,32,512]{3,2,1,0:T(8,128)(2,1)S(1)}, u32[]{:S(2)}, u32[]{:S(2)}) collective-permute-start(bf16[2,8,32,512]{3,2,1,0:T(8,128)(2,1)S(1)} %slice.197), channel_id=1, source_target_pairs={{0,2},{1,3},{2,0},{3,1},{4,6},{5,7},{6,4},{7,5},{8,10},{9,11},{10,... | collective-permute-start | bytes 1572872 | tf_op jit(solution)/shard_map/ppermute | solution.py:316
  197.6 3.9 %collective-permute-start.11 = (bf16[1,1,32,512]{3,2,1,0:T(8,128)(2,1)S(1)}, bf16[1,1,32,512]{3,2,1,0:T(8,128)(2,1)S(1)}, u32[]{:S(2)}, u32[]{:S(2)}) collective-permute-start(bf16[1,1,32,512]{3,2,1,0:T(8,128)(2,1)S(1)} %get-tuple-element.195), channel_id=1, source_target_pairs={{0,8},{4,12},{8,0},{12,4},{16,24},{20,28},{24,16},{28,20},{1,9},{5... | collective-permute-start | bytes 98312 | tf_op jit(solution)/shard_map/ppermute | solution.py:316
  201.6 5.0 %collective-permute-start.12 = (bf16[1,1,32,512]{3,2,1,0:T(8,128)(2,1)S(1)}, bf16[1,1,32,512]{3,2,1,0:T(8,128)(2,1)S(1)}, u32[]{:S(2)}, u32[]{:S(2)}) collective-permute-start(bf16[1,1,32,512]{3,2,1,0:T(8,128)(2,1)S(1)} %get-tuple-element.195), channel_id=1, source_target_pairs={{0,16},{4,20},{8,24},{12,28},{16,0},{20,4},{24,8},{28,12},{1,17},{... | collective-permute-start | bytes 98312 | tf_op jit(solution)/shard_map/ppermute | solution.py:316
  206.6 5.7 %collective-permute-start.13 = (bf16[1,1,32,512]{3,2,1,0:T(8,128)(2,1)S(1)}, bf16[1,1,32,512]{3,2,1,0:T(8,128)(2,1)S(1)}, u32[]{:S(2)}, u32[]{:S(2)}) collective-permute-start(bf16[1,1,32,512]{3,2,1,0:T(8,128)(2,1)S(1)} %get-tuple-element.195), channel_id=1, source_target_pairs={{0,24},{4,28},{8,16},{12,20},{16,8},{20,12},{24,0},{28,4},{1,25},{... | collective-permute-start | bytes 98312 | tf_op jit(solution)/shard_map/ppermute | solution.py:316
  212.3 3.9 %collective-permute-start.22 = (bf16[1,1,32,512]{3,2,1,0:T(8,128)(2,1)S(1)}, bf16[1,1,32,512]{3,2,1,0:T(8,128)(2,1)S(1)}, u32[]{:S(2)}, u32[]{:S(2)}) collective-permute-start(bf16[1,1,32,512]{3,2,1,0:T(8,128)(2,1)S(1)} %get-tuple-element.193), channel_id=1, source_target_pairs={{0,8},{4,12},{8,0},{12,4},{16,24},{20,28},{24,16},{28,20},{1,9},{5... | collective-permute-start | bytes 98312 | tf_op jit(solution)/shard_map/ppermute | solution.py:316
  216.4 6.4 %collective-permute-start.30 = (bf16[2,4,32,512]{3,2,1,0:T(8,128)(2,1)S(1)}, bf16[2,4,32,512]{3,2,1,0:T(8,128)(2,1)S(1)}, u32[]{:S(2)}, u32[]{:S(2)}) collective-permute-start(bf16[2,4,32,512]{3,2,1,0:T(8,128)(2,1)S(1)} %slice.191), channel_id=1, source_target_pairs={{0,2},{1,3},{2,0},{3,1},{4,6},{5,7},{6,4},{7,5},{8,10},{9,11},{10,... | collective-permute-start | bytes 786440 | tf_op jit(solution)/shard_map/ppermute | solution.py:316
  217.5 7.4 %collective-permute-start.42 = (bf16[2,4,32,512]{3,2,1,0:T(8,128)(2,1)S(1)}, bf16[2,4,32,512]{3,2,1,0:T(8,128)(2,1)S(1)}, u32[]{:S(2)}, u32[]{:S(2)}) collective-permute-start(bf16[2,4,32,512]{3,2,1,0:T(8,128)(2,1)S(1)} %slice.199), channel_id=1, source_target_pairs={{0,4},{4,0},{8,12},{12,8},{16,20},{20,16},{24,28},{28,24},{1,5},{5... | collective-permute-start | bytes 786440 | tf_op jit(solution)/shard_map/ppermute | solution.py:316
  223.0 6.7 %collective-permute-start.33 = (bf16[2,1,32,512]{3,2,1,0:T(8,128)(2,1)S(1)}, bf16[2,1,32,512]{3,2,1,0:T(8,128)(2,1)S(1)}, u32[]{:S(2)}, u32[]{:S(2)}) collective-permute-start(bf16[2,1,32,512]{3,2,1,0:T(8,128)(2,1)S(1)} %get-tuple-element.206), channel_id=1, source_target_pairs={{0,24},{4,28},{8,16},{12,20},{16,8},{20,12},{24,0},{28,4},{1,25},{... | collective-permute-start | bytes 196616 | tf_op jit(solution)/shard_map/ppermute | solution.py:316
  224.9 7.1 %collective-permute-start.32 = (bf16[2,1,32,512]{3,2,1,0:T(8,128)(2,1)S(1)}, bf16[2,1,32,512]{3,2,1,0:T(8,128)(2,1)S(1)}, u32[]{:S(2)}, u32[]{:S(2)}) collective-permute-start(bf16[2,1,32,512]{3,2,1,0:T(8,128)(2,1)S(1)} %get-tuple-element.207), channel_id=1, source_target_pairs={{0,16},{4,20},{8,24},{12,28},{16,0},{20,4},{24,8},{28,12},{1,17},{... | collective-permute-start | bytes 196616 | tf_op jit(solution)/shard_map/ppermute | solution.py:316
  224.9 7.1 %collective-permute-start.31 = (bf16[2,1,32,512]{3,2,1,0:T(8,128)(2,1)S(1)}, bf16[2,1,32,512]{3,2,1,0:T(8,128)(2,1)S(1)}, u32[]{:S(2)}, u32[]{:S(2)}) collective-permute-start(bf16[2,1,32,512]{3,2,1,0:T(8,128)(2,1)S(1)} %get-tuple-element.205), channel_id=1, source_target_pairs={{0,8},{4,12},{8,0},{12,4},{16,24},{20,28},{24,16},{28,20},{1,9},{5... | collective-permute-start | bytes 196616 | tf_op jit(solution)/shard_map/ppermute | solution.py:316
  229.7 6.4 %collective-permute-start.45 = (bf16[2,1,32,512]{3,2,1,0:T(8,128)(2,1)S(1)}, bf16[2,1,32,512]{3,2,1,0:T(8,128)(2,1)S(1)}, u32[]{:S(2)}, u32[]{:S(2)}) collective-permute-start(bf16[2,1,32,512]{3,2,1,0:T(8,128)(2,1)S(1)} %get-tuple-element.201), channel_id=1, source_target_pairs={{0,24},{4,28},{8,16},{12,20},{16,8},{20,12},{24,0},{28,4},{1,25},{... | collective-permute-start | bytes 196616 | tf_op jit(solution)/shard_map/ppermute | solution.py:316
  232.1 6.5 %collective-permute-start.44 = (bf16[2,1,32,512]{3,2,1,0:T(8,128)(2,1)S(1)}, bf16[2,1,32,512]{3,2,1,0:T(8,128)(2,1)S(1)}, u32[]{:S(2)}, u32[]{:S(2)}) collective-permute-start(bf16[2,1,32,512]{3,2,1,0:T(8,128)(2,1)S(1)} %get-tuple-element.202), channel_id=1, source_target_pairs={{0,16},{4,20},{8,24},{12,28},{16,0},{20,4},{24,8},{28,12},{1,17},{... | collective-permute-start | bytes 196616 | tf_op jit(solution)/shard_map/ppermute | solution.py:316
  232.1 6.5 %collective-permute-start.43 = (bf16[2,1,32,512]{3,2,1,0:T(8,128)(2,1)S(1)}, bf16[2,1,32,512]{3,2,1,0:T(8,128)(2,1)S(1)}, u32[]{:S(2)}, u32[]{:S(2)}) collective-permute-start(bf16[2,1,32,512]{3,2,1,0:T(8,128)(2,1)S(1)} %get-tuple-element.200), channel_id=1, source_target_pairs={{0,8},{4,12},{8,0},{12,4},{16,24},{20,28},{24,16},{28,20},{1,9},{5... | collective-permute-start | bytes 196616 | tf_op jit(solution)/shard_map/ppermute | solution.py:316
  236.1 4.5 %collective-permute-start.34 = (bf16[2,1,32,512]{3,2,1,0:T(8,128)(2,1)S(1)}, bf16[2,1,32,512]{3,2,1,0:T(8,128)(2,1)S(1)}, u32[]{:S(2)}, u32[]{:S(2)}) collective-permute-start(bf16[2,1,32,512]{3,2,1,0:T(8,128)(2,1)S(1)} %get-tuple-element.191), channel_id=1, source_target_pairs={{0,8},{4,12},{8,0},{12,4},{16,24},{20,28},{24,16},{28,20},{1,9},{5... | collective-permute-start | bytes 196616 | tf_op jit(solution)/shard_map/ppermute | solution.py:316
  238.5 5.2 %collective-permute-start.35 = (bf16[2,1,32,512]{3,2,1,0:T(8,128)(2,1)S(1)}, bf16[2,1,32,512]{3,2,1,0:T(8,128)(2,1)S(1)}, u32[]{:S(2)}, u32[]{:S(2)}) collective-permute-start(bf16[2,1,32,512]{3,2,1,0:T(8,128)(2,1)S(1)} %get-tuple-element.191), channel_id=1, source_target_pairs={{0,16},{4,20},{8,24},{12,28},{16,0},{20,4},{24,8},{28,12},{1,17},{... | collective-permute-start | bytes 196616 | tf_op jit(solution)/shard_map/ppermute | solution.py:316
  238.6 6.4 %collective-permute-start.36 = (bf16[2,1,32,512]{3,2,1,0:T(8,128)(2,1)S(1)}, bf16[2,1,32,512]{3,2,1,0:T(8,128)(2,1)S(1)}, u32[]{:S(2)}, u32[]{:S(2)}) collective-permute-start(bf16[2,1,32,512]{3,2,1,0:T(8,128)(2,1)S(1)} %get-tuple-element.191), channel_id=1, source_target_pairs={{0,24},{4,28},{8,16},{12,20},{16,8},{20,12},{24,0},{28,4},{1,25},{... | collective-permute-start | bytes 196616 | tf_op jit(solution)/shard_map/ppermute | solution.py:316
  240.6 6.4 %collective-permute-start.46 = (bf16[2,1,32,512]{3,2,1,0:T(8,128)(2,1)S(1)}, bf16[2,1,32,512]{3,2,1,0:T(8,128)(2,1)S(1)}, u32[]{:S(2)}, u32[]{:S(2)}) collective-permute-start(bf16[2,1,32,512]{3,2,1,0:T(8,128)(2,1)S(1)} %get-tuple-element.189), channel_id=1, source_target_pairs={{0,8},{4,12},{8,0},{12,4},{16,24},{20,28},{24,16},{28,20},{1,9},{5... | collective-permute-start | bytes 196616 | tf_op jit(solution)/shard_map/ppermute | solution.py:316
  243.8 5.2 %collective-permute-start.47 = (bf16[2,1,32,512]{3,2,1,0:T(8,128)(2,1)S(1)}, bf16[2,1,32,512]{3,2,1,0:T(8,128)(2,1)S(1)}, u32[]{:S(2)}, u32[]{:S(2)}) collective-permute-start(bf16[2,1,32,512]{3,2,1,0:T(8,128)(2,1)S(1)} %get-tuple-element.189), channel_id=1, source_target_pairs={{0,16},{4,20},{8,24},{12,28},{16,0},{20,4},{24,8},{28,12},{1,17},{... | collective-permute-start | bytes 196616 | tf_op jit(solution)/shard_map/ppermute | solution.py:316
  245.0 6.1 %collective-permute-start.48 = (bf16[2,1,32,512]{3,2,1,0:T(8,128)(2,1)S(1)}, bf16[2,1,32,512]{3,2,1,0:T(8,128)(2,1)S(1)}, u32[]{:S(2)}, u32[]{:S(2)}) collective-permute-start(bf16[2,1,32,512]{3,2,1,0:T(8,128)(2,1)S(1)} %get-tuple-element.189), channel_id=1, source_target_pairs={{0,24},{4,28},{8,16},{12,20},{16,8},{20,12},{24,0},{28,4},{1,25},{... | collective-permute-start | bytes 196616 | tf_op jit(solution)/shard_map/ppermute | solution.py:316
  247.0 12.7 %collective-permute-start.23 = (bf16[1,1,32,512]{3,2,1,0:T(8,128)(2,1)S(1)}, bf16[1,1,32,512]{3,2,1,0:T(8,128)(2,1)S(1)}, u32[]{:S(2)}, u32[]{:S(2)}) collective-permute-start(bf16[1,1,32,512]{3,2,1,0:T(8,128)(2,1)S(1)} %get-tuple-element.193), channel_id=1, source_target_pairs={{0,16},{4,20},{8,24},{12,28},{16,0},{20,4},{24,8},{28,12},{1,17},{... | collective-permute-start | bytes 98312 | tf_op jit(solution)/shard_map/ppermute | solution.py:316
  248.9 8.6 %collective-permute-start.37 = (bf16[2,4,32,512]{3,2,1,0:T(8,128)(2,1)S(1)}, bf16[2,4,32,512]{3,2,1,0:T(8,128)(2,1)S(1)}, u32[]{:S(2)}, u32[]{:S(2)}) collective-permute-start(bf16[2,4,32,512]{3,2,1,0:T(8,128)(2,1)S(1)} %pad_maximum_fusion.1), channel_id=1, source_target_pairs={{0,2},{1,3},{2,0},{3,1},{4,6},{5,7},{6,4},{7,5},{8,10},{9,11},{10,... | collective-permute-start | bytes 786440 | tf_op jit(solution)/shard_map/ppermute | solution.py:316
  251.1 8.2 %collective-permute-start.49 = (bf16[2,4,32,512]{3,2,1,0:T(8,128)(2,1)S(1)}, bf16[2,4,32,512]{3,2,1,0:T(8,128)(2,1)S(1)}, u32[]{:S(2)}, u32[]{:S(2)}) collective-permute-start(bf16[2,4,32,512]{3,2,1,0:T(8,128)(2,1)S(1)} %pad_maximum_fusion.2), channel_id=1, source_target_pairs={{0,4},{4,0},{8,12},{12,8},{16,20},{20,16},{24,28},{28,24},{1,5},{5... | collective-permute-start | bytes 786440 | tf_op jit(solution)/shard_map/ppermute | solution.py:316
  257.5 5.7 %collective-permute-start.24 = (bf16[1,1,32,512]{3,2,1,0:T(8,128)(2,1)S(1)}, bf16[1,1,32,512]{3,2,1,0:T(8,128)(2,1)S(1)}, u32[]{:S(2)}, u32[]{:S(2)}) collective-permute-start(bf16[1,1,32,512]{3,2,1,0:T(8,128)(2,1)S(1)} %get-tuple-element.193), channel_id=1, source_target_pairs={{0,24},{4,28},{8,16},{12,20},{16,8},{20,12},{24,0},{28,4},{1,25},{... | collective-permute-start | bytes 98312 | tf_op jit(solution)/shard_map/ppermute | solution.py:316
  259.3 12.8 %collective-permute-start.38 = (bf16[2,8,32,512]{3,2,1,0:T(8,128)(2,1)S(1)}, bf16[2,8,32,512]{3,2,1,0:T(8,128)(2,1)S(1)}, u32[]{:S(2)}, u32[]{:S(2)}) collective-permute-start(bf16[2,8,32,512]{3,2,1,0:T(8,128)(2,1)S(1)} %get-tuple-element.203), channel_id=1, source_target_pairs={{0,4},{4,0},{8,12},{12,8},{16,20},{20,16},{24,28},{28,24},{1,5},{5... | collective-permute-start | bytes 1572872 | tf_op jit(solution)/shard_map/ppermute | solution.py:316
  259.7 12.8 %collective-permute-start.50 = (bf16[2,8,32,512]{3,2,1,0:T(8,128)(2,1)S(1)}, bf16[2,8,32,512]{3,2,1,0:T(8,128)(2,1)S(1)}, u32[]{:S(2)}, u32[]{:S(2)}) collective-permute-start(bf16[2,8,32,512]{3,2,1,0:T(8,128)(2,1)S(1)} %get-tuple-element.198), channel_id=1, source_target_pairs={{0,2},{1,3},{2,0},{3,1},{4,6},{5,7},{6,4},{7,5},{8,10},{9,11},{10,... | collective-permute-start | bytes 1572872 | tf_op jit(solution)/shard_map/ppermute | solution.py:316
  263.2 7.1 %collective-permute-start.14 = (bf16[1,4,32,512]{3,2,1,0:T(8,128)(2,1)S(1)}, bf16[1,4,32,512]{3,2,1,0:T(8,128)(2,1)S(1)}, u32[]{:S(2)}, u32[]{:S(2)}) collective-permute-start(bf16[1,4,32,512]{3,2,1,0:T(8,128)(2,1)S(1)} %pad_maximum_fusion.3), channel_id=1, source_target_pairs={{0,2},{1,3},{2,0},{3,1},{4,6},{5,7},{6,4},{7,5},{8,10},{9,11},{10,... | collective-permute-start | bytes 393224 | tf_op jit(solution)/shard_map/ppermute | solution.py:316
  270.4 5.0 %collective-permute-start.25 = (bf16[1,4,32,512]{3,2,1,0:T(8,128)(2,1)S(1)}, bf16[1,4,32,512]{3,2,1,0:T(8,128)(2,1)S(1)}, u32[]{:S(2)}, u32[]{:S(2)}) collective-permute-start(bf16[1,4,32,512]{3,2,1,0:T(8,128)(2,1)S(1)} %pad_maximum_fusion.4), channel_id=1, source_target_pairs={{0,4},{4,0},{8,12},{12,8},{16,20},{20,16},{24,28},{28,24},{1,5},{5... | collective-permute-start | bytes 393224 | tf_op jit(solution)/shard_map/ppermute | solution.py:316
  272.1 6.4 %collective-permute-start.15 = (bf16[1,8,32,512]{3,2,1,0:T(8,128)(2,1)S(1)}, bf16[1,8,32,512]{3,2,1,0:T(8,128)(2,1)S(1)}, u32[]{:S(2)}, u32[]{:S(2)}) collective-permute-start(bf16[1,8,32,512]{3,2,1,0:T(8,128)(2,1)S(1)} %get-tuple-element.213), channel_id=1, source_target_pairs={{0,4},{4,0},{8,12},{12,8},{16,20},{20,16},{24,28},{28,24},{1,5},{5... | collective-permute-start | bytes 786440 | tf_op jit(solution)/shard_map/ppermute | solution.py:316
  272.6 27.5 %collective-permute-start.39 = (bf16[2,512,512]{2,1,0:T(8,128)(2,1)S(1)}, bf16[2,512,512]{2,1,0:T(8,128)(2,1)S(1)}, u32[]{:S(2)}, u32[]{:S(2)}) collective-permute-start(bf16[2,512,512]{2,1,0:T(8,128)(2,1)S(1)} %bitcast.76), channel_id=1, source_target_pairs={{0,1},{1,0},{2,3},{3,2},{4,5},{5,4},{6,7},{7,6},{8,9},{9,8},{10,11... | collective-permute-start | bytes 3145736 | tf_op jit(solution)/shard_map/ppermute | solution.py:316
  275.3 24.7 %collective-permute-start.51 = (bf16[2,512,512]{2,1,0:T(8,128)(2,1)S(1)}, bf16[2,512,512]{2,1,0:T(8,128)(2,1)S(1)}, u32[]{:S(2)}, u32[]{:S(2)}) collective-permute-start(bf16[2,512,512]{2,1,0:T(8,128)(2,1)S(1)} %bitcast.78), channel_id=1, source_target_pairs={{0,1},{1,0},{2,3},{3,2},{4,5},{5,4},{6,7},{7,6},{8,9},{9,8},{10,11... | collective-permute-start | bytes 3145736 | tf_op jit(solution)/shard_map/ppermute | solution.py:316
  275.4 9.2 %collective-permute-start.26 = (bf16[1,8,32,512]{3,2,1,0:T(8,128)(2,1)S(1)}, bf16[1,8,32,512]{3,2,1,0:T(8,128)(2,1)S(1)}, u32[]{:S(2)}, u32[]{:S(2)}) collective-permute-start(bf16[1,8,32,512]{3,2,1,0:T(8,128)(2,1)S(1)} %get-tuple-element.208), channel_id=1, source_target_pairs={{0,2},{1,3},{2,0},{3,1},{4,6},{5,7},{6,4},{7,5},{8,10},{9,11},{10,... | collective-permute-start | bytes 786440 | tf_op jit(solution)/shard_map/ppermute | solution.py:316
  278.6 16.8 %collective-permute-start.4 = (bf16[512,512]{1,0:T(8,128)(2,1)S(1)}, bf16[512,512]{1,0:T(8,128)(2,1)S(1)}, u32[]{:S(2)}, u32[]{:S(2)}) collective-permute-start(bf16[512,512]{1,0:T(8,128)(2,1)S(1)} %fusion), channel_id=1, source_target_pairs={{0,2},{1,3},{2,0},{3,1},{4,6},{5,7},{6,4},{7,5},{8,10},{9,11},{10,... | collective-permute-start | bytes 1572872 | tf_op jit(solution)/shard_map/ppermute | solution.py:316
  284.5 12.4 %collective-permute-start.16 = (bf16[1,512,512]{2,1,0:T(8,128)(2,1)S(1)}, bf16[1,512,512]{2,1,0:T(8,128)(2,1)S(1)}, u32[]{:S(2)}, u32[]{:S(2)}) collective-permute-start(bf16[1,512,512]{2,1,0:T(8,128)(2,1)S(1)} %bitcast.82), channel_id=1, source_target_pairs={{0,1},{1,0},{2,3},{3,2},{4,5},{5,4},{6,7},{7,6},{8,9},{9,8},{10,11... | collective-permute-start | bytes 1572872 | tf_op jit(solution)/shard_map/ppermute | solution.py:316
  284.6 12.4 %collective-permute-start.27 = (bf16[1,512,512]{2,1,0:T(8,128)(2,1)S(1)}, bf16[1,512,512]{2,1,0:T(8,128)(2,1)S(1)}, u32[]{:S(2)}, u32[]{:S(2)}) collective-permute-start(bf16[1,512,512]{2,1,0:T(8,128)(2,1)S(1)} %bitcast.80), channel_id=1, source_target_pairs={{0,1},{1,0},{2,3},{3,2},{4,5},{5,4},{6,7},{7,6},{8,9},{9,8},{10,11... | collective-permute-start | bytes 1572872 | tf_op jit(solution)/shard_map/ppermute | solution.py:316
  (45 other events, 339.3 us)

commit v2 on v0

v2 whole, which is shorter than its diff:
```python
import functools

import jax
import jax.numpy as jnp
from jax import lax
from jax.experimental import pallas as pl
from jax.experimental.pallas import tpu as pltpu
from jax.sharding import PartitionSpec as P

EPSILON = 1e-05
MASKED = -1e30
BF = jnp.bfloat16
F32 = jnp.float32
LANES = 128
GELU_C = 0.7978845608028654
GELU_A = 0.044715
MIB = 1 << 20
CHUNKS = 4
LIMIT = 58


def dot_nn(a, b):
    return lax.dot_general(a, b, (((1,), (0,)), ((), ())), preferred_element_type=F32)


def dot_nt(a, b):
    return lax.dot_general(a, b, (((1,), (1,)), ((), ())), preferred_element_type=F32)


def dot_tn(a, b):
    return lax.dot_general(a, b, (((0,), (0,)), ((), ())), preferred_element_type=F32)


def normalize(x):
    centred = x - jnp.mean(x, axis=-1, keepdims=True)
    spread = jnp.mean(centred * centred, axis=-1, keepdims=True)
    inv = lax.rsqrt(spread + EPSILON)
    return centred * inv, inv


def norm_back(grad, gain, xhat, inv):
    g = grad * gain
    return inv * (
        g
        - jnp.mean(g, axis=-1, keepdims=True)
        - xhat * jnp.mean(g * xhat, axis=-1, keepdims=True)
    )


def front_kernel(pieces, copied, *refs):
    me_ref = refs[0]
    xs = refs[1 : 1 + pieces]
    wq, wk, wv, gain, shift = refs[1 + pieces : 6 + pieces]
    outs = refs[6 + pieces + copied :]
    step = pl.program_id(0)
    for piece in range(pieces):

        @pl.when(step == piece)
        def _(piece=piece):
            xhat, _ = normalize(xs[piece][...].astype(F32))
            a1 = (xhat * gain[...] + shift[...]).astype(BF)
            outs[0][0] = dot_nn(a1, wk[...]).astype(BF)
            outs[1][0] = dot_nn(a1, wv[...]).astype(BF)
            outs[2][0] = a1
            outs[3][0] = xhat.astype(BF)
            if not copied and piece == 0:
                outs[4][...] = dot_nn(a1, wq[...]).astype(BF)


def head_mask(heads, first):
    lane = lax.broadcasted_iota(jnp.int32, (1, LANES), 1) // (LANES // heads)
    return lane == first


def stacked(block, heads, first, count):
    zero = jnp.zeros_like(block)
    return jnp.concatenate(
        [jnp.where(head_mask(heads, first + t), block, zero) for t in range(count)], axis=0
    )


def unstacked(total, product, heads, first, count, rows):
    for t in range(count):
        part = product[t * rows : (t + 1) * rows]
        total = total + jnp.where(head_mask(heads, first + t), part, 0.0)
    return total


def key_rows(ref, start, rows, lanes):
    return jnp.concatenate(
        [ref[r, start : start + rows, lanes] for r in range(ref.shape[0])], axis=0
    )


def attn_fwd_kernel(layout, groups, heads, scale, *refs):
    lens, (q_ref, k_ref, v_ref), pairs = refs[0:3], refs[3:6], refs[6:9]
    pouts, ps, o_ref = refs[9:12], refs[12:15], refs[15]
    for (start, mols, rows, slots), len_ref, pair_ref, pout_ref, p_ref in zip(
        layout, lens, pairs, pouts, ps
    ):
        count = min(heads, max(1, 512 // rows))
        for mol in range(mols):
            length = len_ref[pl.program_id(0) * mols + mol]
            key_at = lax.broadcasted_iota(jnp.int32, (1, 1, slots), 2)
            mask = jnp.where(key_at < length, 0.0, MASKED)
            at_row = start + mol * rows
            for group in range(groups):
                lanes = slice(group * LANES, (group + 1) * LANES)
                q = q_ref[at_row : at_row + rows, lanes]
                k = key_rows(k_ref, at_row, rows, lanes)
                v = key_rows(v_ref, at_row, rows, lanes)
                total = jnp.zeros((rows, LANES), F32)
                for first in range(0, heads, count):
                    at = slice(group * heads + first, group * heads + first + count)
                    s = dot_nt(stacked(q, heads, first, count), k)
                    s = s.reshape(count, rows, slots) * scale + pair_ref[mol, at].astype(F32)
                    pout_ref[mol, at] = s.astype(BF)
                    s = s + mask
                    e = jnp.exp(s - jnp.max(s, axis=-1, keepdims=True))
                    p = (e * (1.0 / jnp.sum(e, axis=-1, keepdims=True))).astype(BF)
                    p_ref[mol, at] = p
                    pv = dot_nn(p.reshape(count * rows, slots), v)
                    total = unstacked(total, pv, heads, first, count, rows)
                o_ref[at_row : at_row + rows, lanes] = total


def attn_bwd_kernel(layout, groups, heads, scale, *refs):
    count_of = len(layout)
    q_ref, do_ref, dd_ref, k_ref, v_ref = refs[0:5]
    ps, dpos = refs[5 : 5 + count_of], refs[5 + count_of : 5 + 2 * count_of]
    dls = refs[5 + 2 * count_of : 5 + 3 * count_of]
    dq_ref, dk_ref, dv_ref = refs[5 + 3 * count_of :]
    ranks = k_ref.shape[0]
    origin = layout[0][0]
    for (start, mols, rows, slots), p_ref, dpo_ref, dl_ref in zip(layout, ps, dpos, dls):
        count = min(heads, max(1, 1024 // rows))
        base = (start - origin) * ranks
        for group in range(groups):
            lanes = slice(group * LANES, (group + 1) * LANES)
            dk_all = []
            dv_all = []
            for mol in range(mols):
                at_row = start + mol * rows
                rs = slice(at_row, at_row + rows)
                q = q_ref[rs, lanes]
                do = do_ref[rs, lanes]
                dd = dd_ref[rs, lanes]
                k = key_rows(k_ref, at_row, rows, lanes)
                v = key_rows(v_ref, at_row, rows, lanes)
                v_aug = jnp.concatenate([v, jnp.ones_like(v)], axis=1)
                total = jnp.zeros((rows, LANES), F32)
                dk = jnp.zeros((LANES, slots), F32)
                dv = jnp.zeros((LANES, slots), F32)
                for first in range(0, heads, count):
                    at = slice(group * heads + first, group * heads + first + count)
                    do_s = stacked(do, heads, first, count)
                    t = dot_nt(
                        jnp.concatenate([do_s, stacked(dd, heads, first, count)], axis=1), v_aug
                    )
                    p = p_ref[mol, at]
                    dl = p.astype(F32) * t.reshape(count, rows, slots)
                    dl = (dl + dpo_ref[mol, at].astype(F32)).astype(BF)
                    dl_ref[mol, at] = dl
                    dl = dl.reshape(count * rows, slots)
                    total = unstacked(total, dot_nn(dl, k), heads, first, count, rows)
                    dk = dk + dot_tn(stacked(q, heads, first, count), dl)
                    dv = dv + dot_tn(do_s, p.reshape(count * rows, slots))
                to = slice(at_row - origin, at_row - origin + rows)
                dq_ref[to, lanes] = (total * scale).astype(BF)
                dk_all.append((dk * scale).astype(BF))
                dv_all.append(dv.astype(BF))
            dk_ref[lanes, base : base + mols * slots] = jnp.concatenate(dk_all, axis=1)
            dv_ref[lanes, base : base + mols * slots] = jnp.concatenate(dv_all, axis=1)


def back_kernel(layout, share, parts, ids, *refs):
    dqs, dks, dvs = (refs[i * parts : (i + 1) * parts] for i in range(3))
    a_ref, h_ref, wq, wk, wv, gs_two = refs[3 * parts : 3 * parts + 6]
    own_ref, keep_ref, send_ref, w_send, w_keep = refs[3 * parts + 6 : 3 * parts + 11]
    gq_ref, gk_ref, gv_ref, gs_ref, da_s = refs[3 * parts + 11 :]
    step = pl.program_id(0)
    me = ids[3]
    ranks = a_ref.shape[0]

    @pl.when(step == 0)
    def _():
        for ref in (gq_ref, gk_ref, gv_ref, gs_ref):
            ref[...] = jnp.zeros_like(ref)

    def molecules(ref):
        return jnp.concatenate(
            [
                key_rows(ref, start + mol * rows, rows, slice(None))
                for start, mols, rows, slots in layout
                for mol in range(mols)
            ],
            axis=0,
        )

    dq = jnp.concatenate([ref[...] for ref in dqs], axis=0)
    dk = jnp.concatenate([ref[...] for ref in dks], axis=1)
    dv = jnp.concatenate([ref[...] for ref in dvs], axis=1)
    a1 = molecules(a_ref)
    gk_ref[...] += dot_nn(dk, a1)
    gv_ref[...] += dot_nn(dv, a1)
    gq_ref[...] += dot_tn(a_ref[me], dq)
    daq = dot_nt(dq, wq[...])
    across = (((0,), (1,)), ((), ()))
    da = lax.dot_general(dk, wk[...], across, preferred_element_type=F32) + lax.dot_general(
        dv, wv[...], across, preferred_element_type=F32
    )
    da_s[...] = da
    gs_ref[0:1, :] += jnp.sum(da * molecules(h_ref).astype(F32), axis=0, keepdims=True) + jnp.sum(
        daq * h_ref[me].astype(F32), axis=0, keepdims=True
    )
    gs_ref[1:2, :] += jnp.sum(da, axis=0, keepdims=True) + jnp.sum(daq, axis=0, keepdims=True)
    for piece in range(ranks):
        for start, mols, rows, slots in layout:
            for mol in range(mols):
                at = pl.multiple_of(start * ranks + mol * slots + (me ^ piece) * rows, rows)
                value = da_s[pl.ds(at, rows), :]
                to = slice(start + mol * rows, start + (mol + 1) * rows)
                if piece == 0:
                    own_ref[to, :] = value + daq[to]
                elif piece == 2:
                    keep_ref[to, :] = value.astype(BF)
                else:
                    send_ref[piece // 2, to, :] = value.astype(BF)

    @pl.when(step == pl.num_programs(0) - 1)
    def _():
        width = gq_ref.shape[1]
        size = width // CHUNKS
        half = width // 2
        gains = jnp.concatenate(
            [gs_ref[0:2, :], gs_two[0:2, :], jnp.zeros((12, width), F32)], axis=0
        ).astype(BF)
        for value in (0, 1):

            @pl.when(ids[0] == value)
            def _(value=value):
                for ref, owner, mine in ((w_keep, value, ids[1]), (w_send, 1 - value, ids[2])):
                    shard_rows(ref, (gk_ref if owner else gq_ref)[...], 0, share, mine)
                    gv = gv_ref[owner * half : (owner + 1) * half, :]
                    shard_rows(ref, gv, size, share, mine)

        w_keep[CHUNKS * share :, :] = gains
        w_send[CHUNKS * share :, :] = gains


def shard_rows(ref, value, at, rows, mine):
    size = value.shape[0] // CHUNKS
    for chunk in range(CHUNKS):
        to = pl.multiple_of((chunk ^ mine) * rows + at, 16)
        ref[pl.ds(to, size), :] = value[chunk * size : (chunk + 1) * size].astype(ref.dtype)


def store_by_bucket(refs, value):
    row = 0
    for micro in range(refs[0].shape[0]):
        for ref in refs:
            ref[micro] = value[row : row + ref.shape[1]]
            row += ref.shape[1]


def store_tile(send_ref, keep_ref, value, step, at, half_tiles, rows, ids):
    size = value.shape[0] // CHUNKS

    @pl.when(step < half_tiles)
    def _():
        shard_rows(send_ref, value, (2 * step + at) * size, rows, ids[2])

    @pl.when(step >= half_tiles)
    def _():
        shard_rows(keep_ref, value, (2 * (step - half_tiles) + at) * size, rows, ids[1])


def dense_kernel(
    tiles, rows, ids, x_ref, o_ref, dy_ref, wo, wu, wd, gain, shift,
    yb, ym, ys, dh_ref, do_ref, dd_ref, gs_ref, send_ref, keep_ref,
    a2_s, y_s, xhat_s, inv_s, da_s,
):
    step = pl.program_id(0)
    half_tiles = tiles // 2

    @pl.when(step == 0)
    def _():
        hidden = x_ref[...].astype(F32) + dot_nn(o_ref[...].astype(BF), wo[...])
        xhat, inv = normalize(hidden)
        y_s[...] = hidden
        xhat_s[...] = xhat
        inv_s[...] = jnp.broadcast_to(inv, inv_s.shape)
        a2_s[...] = (xhat * gain[...] + shift[...]).astype(BF)
        da_s[...] = jnp.zeros_like(da_s)

    dy = dy_ref[...]
    u = dot_nn(a2_s[...], wu[...])
    u2 = u * u
    th = jnp.tanh(GELU_C * (u + GELU_A * u * u2))
    half = 0.5 * (1.0 + th)
    g = (u * half).astype(BF)
    slope = half + 0.5 * u * (1.0 - th * th) * (GELU_C * (1.0 + 3.0 * GELU_A * u2))
    y_s[...] += dot_nn(g, wd[...])
    store_tile(send_ref, keep_ref, dot_tn(g, dy), step, 1, half_tiles, rows, ids)
    du = (dot_nt(dy, wd[...]) * slope).astype(BF)
    store_tile(send_ref, keep_ref, dot_tn(a2_s[...], du), step, 0, half_tiles, rows, ids)
    da_s[...] += dot_nt(du, wu[...])

    @pl.when(step == tiles - 1)
    def _():
        store_by_bucket((yb, ym, ys), y_s[...].astype(BF))
        da = da_s[...]
        xhat = xhat_s[...]
        gs_ref[0:1, :] = jnp.sum(da * xhat, axis=0, keepdims=True)
        gs_ref[1:2, :] = jnp.sum(da, axis=0, keepdims=True)
        dh = dy.astype(F32) + norm_back(da, gain[...], xhat, inv_s[:, 0:1])
        dh_ref[...] = dh
        dh = dh.astype(BF)
        o = o_ref[...]
        do = dot_nt(dh, wo[...]).astype(BF)
        do_ref[...] = do
        dd_ref[...] = (-(do.astype(F32) * o)).astype(BF)
        da_s[...] = dot_tn(o.astype(BF), dh)
        width = da.shape[1]
        part = width // 2
        for ref, core, mine in ((send_ref, ids[4], ids[2]), (keep_ref, ids[0], ids[1])):
            value = da_s[pl.ds(pl.multiple_of(core * part, part), part), :]
            shard_rows(ref, value, 2 * half_tiles * (width // CHUNKS), rows, mine)


def last_kernel(parts, x_ref, dh, gain, *refs):
    grads = []
    row = 0
    for part in range(parts):
        own, near, far = refs[3 * part : 3 * part + 3]
        at = slice(row, row + own.shape[0])
        row += own.shape[0]
        xhat, inv = normalize(x_ref[at, :].astype(F32))
        da = own[...] + near[0].astype(F32) + far[...].astype(F32)
        grads.append((dh[at, :] + norm_back(da, gain[...], xhat, inv)).astype(BF))
    store_by_bucket(refs[3 * parts :], jnp.concatenate(grads, axis=0))


def exchange(value, axis, distance, size):
    return lax.ppermute(value, axis, [(i, i ^ distance) for i in range(size)])


def add_low(first, *others):
    total = first.astype(F32)
    for other in others:
        total = total + other.astype(F32)
    return total.astype(BF)


def stage_permutes(sizes):
    rows = sizes["rows"]
    x, y, z_near, z_far = rows, 2, 2 * rows, 4 * rows
    pairs = [(x, y), (y, x), (z_near, z_far), (z_far, z_near)]
    extra = 8
    while extra < sizes["dp"]:
        pairs.append((extra * rows, extra * rows))
        extra *= 2
    total = rows * sizes["dp"]
    return [[(i, i ^ pair[i % 2]) for i in range(total)] for pair in pairs]


def send_all(value, perm):
    return lax.ppermute(value, ("dp", "rows"), perm)


def after(value, *others):
    return lax.optimization_barrier((value,) + others)[0]


class SumOverAll:
    def __init__(self, keep, send, tail, sizes):
        self.stages = stage_permutes(sizes)
        self.swap = functools.partial(exchange, axis="rows", distance=1, size=sizes["rows"])
        self.tail = tail
        self.block = (keep.shape[0] - tail) // CHUNKS
        self.size = CHUNKS * self.block
        self.keep = keep
        self.send = send

    def cut(self, value, start, stop):
        if not self.tail:
            return value[start:stop]
        return jnp.concatenate([value[start:stop], value[self.size :]], axis=0)

    def split(self, got):
        half = self.size // 2
        self.send = add_low(self.cut(self.keep, half, self.size), self.cut(got, half, self.size))
        self.keep = add_low(self.cut(self.keep, 0, half), self.cut(got, 0, half))
        self.size = half
        return self.send

    def reduce(self):
        got = yield self.send, self.swap
        for stage in self.stages[:2]:
            got = yield self.split(got), functools.partial(send_all, perm=stage)
        part = add_low(self.keep, got)
        for stage in self.stages[2:4]:
            got = yield part, functools.partial(send_all, perm=stage)
            part = add_low(part, got)
        for stage in self.stages[4:]:
            part = add_low(part, send_all(part, stage))
        block = part[: self.block]
        got = yield block, functools.partial(send_all, perm=self.stages[1])
        low = jnp.concatenate([block, got], axis=0)
        got = yield low, functools.partial(send_all, perm=self.stages[0])
        mine = jnp.concatenate([low, got, part[self.block :]], axis=0)
        other = yield mine, self.swap
        self.result = (mine, other)
        yield None, None

    def begin(self):
        self.run = self.reduce()
        return self.step(None)

    def step(self, got, *deps):
        self.operand, move = self.run.send(got)
        return None if move is None else move(after(self.operand, *deps))


def cost(micros):
    return pl.CostEstimate(flops=0, bytes_accessed=int(micros * 0.8e6), transcendentals=0)


def params():
    return pltpu.CompilerParams(vmem_limit_bytes=LIMIT * MIB)


def shards(sizes, *args):
    atoms, pairs, lengths = args[0:3], args[3:6], args[6:9]
    wq, wk, wv, wo, wu, wd = args[9:15]
    gain_one, shift_one, gain_two, shift_two = (v.reshape(1, -1) for v in args[15:19])
    dys, dpos = args[19:22], args[22:25]
    width = atoms[0].shape[-1]
    micros = atoms[0].shape[0]
    hidden_units = wu.shape[1]
    head_count = pairs[0].shape[2]
    heads = head_count * LANES // width
    scale = float((width // head_count) ** -0.5)
    groups = width // LANES
    ranks = sizes["rows"]

    rows_at = lax.axis_index("rows")
    core, y = rows_at % 2, rows_at // 2
    xa = lax.axis_index("dp") % 2
    order = (xa * 2 + y, y * 2 + xa)
    mine = jnp.where(core == 0, order[0], order[1])
    other = jnp.where(core == 0, order[1], order[0])
    ids = jnp.stack([core, mine, other, rows_at, core ^ 1]).astype(jnp.int32)

    layout = []
    start = 0
    for a in atoms:
        layout.append((start, a.shape[1], a.shape[2], a.shape[2] * ranks))
        start += a.shape[1] * a.shape[2]
    layout = tuple(layout)
    micro_rows = start
    local = micros * micro_rows

    def by_micro(arrays):
        return jnp.concatenate(
            [a.reshape(micros, -1, width) for a in arrays], axis=1
        ).reshape(local, width)

    x = by_micro(atoms)
    dy = by_micro(dys)
    pair = [p.reshape((-1,) + p.shape[2:]) for p in pairs]
    dpo = [p.reshape((-1,) + p.shape[2:]) for p in dpos]
    lens = [n.reshape(-1) for n in lengths]

    near_rows = functools.partial(exchange, axis="rows", distance=1, size=ranks)
    far_rows = functools.partial(exchange, axis="rows", distance=2, size=ranks)
    x1 = near_rows(x)
    x2 = far_rows(x)

    smem = pl.BlockSpec(memory_space=pltpu.SMEM)
    anywhere = pl.BlockSpec(memory_space=pl.ANY)

    def whole(shape):
        return pl.BlockSpec(tuple(shape), lambda *_: (0,) * len(shape))

    def call(kernel, name, micros, grid, operands, in_specs, outs, out_specs, scratch=(), **kw):
        return pl.pallas_call(
            kernel,
            grid_spec=pltpu.PrefetchScalarGridSpec(
                num_scalar_prefetch=1,
                grid=grid,
                in_specs=in_specs,
                out_specs=out_specs,
                scratch_shapes=list(scratch),
            ),
            out_shape=[jax.ShapeDtypeStruct(tuple(shape), kind) for shape, kind in outs],
            compiler_params=params(),
            cost_estimate=cost(micros),
            name=name,
            **kw,
        )(ids, *operands)

    gathered = (ranks, local, width)
    weights = [wq, wk, wv, gain_one, shift_one]

    def front(name, pieces, first, old):
        piece_spec = pl.BlockSpec((1, local, width), lambda t, ids: (ids[3] ^ (first + t), 0, 0))
        outs = [(gathered, BF)] * 4
        out_specs = [piece_spec] * 4
        if not old:
            outs = outs + [((local, width), BF)]
            out_specs = out_specs + [whole((local, width))]
        operands = list(pieces) + weights
        return call(
            functools.partial(front_kernel, len(pieces), len(old)),
            name,
            4,
            (len(pieces),),
            operands + list(old),
            [whole(v.shape) for v in operands] + [anywhere] * len(old),
            outs,
            out_specs,
            input_output_aliases={1 + len(operands) + i: i for i in range(len(old))},
        )

    *early, q = front("front_near", (x, x1), 0, [])
    x2 = after(x2, q)
    x3 = near_rows(x2)
    ks, vs, a1s, xhats = front("front_far", (x2, x3), 2, early)

    row_spec = pl.BlockSpec((micro_rows, width), lambda m, ids: (m, 0))
    rank_spec = pl.BlockSpec((ranks, micro_rows, width), lambda m, ids: (0, m, 0))
    pair_specs = [
        pl.BlockSpec((p.shape[0] // micros,) + p.shape[1:], lambda m, ids: (m, 0, 0, 0))
        for p in pair
    ]
    pair_outs = [(p.shape, BF) for p in pair]
    *res, o = call(
        lambda ids, *refs: attn_fwd_kernel(layout, groups, heads, scale, *refs),
        "attend",
        18,
        (micros,),
        [*lens, q, ks, vs, *pair],
        [smem] * 3 + [row_spec, rank_spec, rank_spec] + pair_specs,
        pair_outs * 2 + [((local, width), F32)],
        pair_specs * 2 + [row_spec],
    )
    pair_out, probs = res[0:3], res[3:6]

    tiles = 4
    tile = hidden_units // tiles
    half = tiles // 2

    def tile_at(t, ids):
        return (t + half * ids[4]) % tiles

    up_spec = pl.BlockSpec((width, tile), lambda t, ids: (0, tile_at(t, ids)))
    down_spec = pl.BlockSpec((tile, width), lambda t, ids: (tile_at(t, ids), 0))
    local_shape = (local, width)
    flat = whole(local_shape)
    ff_rows = (2 * half * tile + width // 2) // CHUNKS
    ff_shape = (CHUNKS * ff_rows, width)
    atom_outs = [((micros, a.shape[1] * a.shape[2], width), BF) for a in atoms]
    atom_specs = [whole(shape) for shape, _ in atom_outs]
    *atoms_out, dh, do, dd, gs_two, ff_send, ff_keep = call(
        functools.partial(dense_kernel, tiles, ff_rows),
        "dense",
        16,
        (tiles,),
        [x, o, dy, wo, wu, wd, gain_two, shift_two],
        [flat, flat, flat, whole(wo.shape), up_spec, down_spec] + [whole((1, width))] * 2,
        atom_outs
        + [(local_shape, F32), (local_shape, BF), (local_shape, BF), ((8, width), F32)]
        + [(ff_shape, BF)] * 2,
        atom_specs + [flat, flat, flat, whole((8, width)), whole(ff_shape), whole(ff_shape)],
        [
            pltpu.VMEM(local_shape, BF),
            pltpu.VMEM(local_shape, F32),
            pltpu.VMEM(local_shape, F32),
            pltpu.VMEM((local, LANES), F32),
            pltpu.VMEM(local_shape, F32),
        ],
    )
    ff = SumOverAll(ff_keep, ff_send, 0, sizes)
    moving = ff.step(ff.begin())
    do = after(do, ff.operand)

    dls = []
    dqs, dks, dvs = [], [], []
    for name, buckets in (("attend_back_big", (0,)), ("attend_back_rest", (1, 2))):
        here = tuple(layout[b] for b in buckets)
        rows_here = sum(mols * rows for _, mols, rows, _ in here)
        specs = [pair_specs[b] for b in buckets]
        key_spec = pl.BlockSpec((width, rows_here * ranks), lambda m, ids: (0, m))
        key_out = ((width, micros * rows_here * ranks), BF)
        res = call(
            lambda ids, *refs, here=here: attn_bwd_kernel(here, groups, heads, scale, *refs),
            name,
            15,
            (micros,),
            [q, do, dd, ks, vs] + [probs[b] for b in buckets] + [dpo[b] for b in buckets],
            [row_spec] * 3 + [rank_spec] * 2 + specs * 2,
            [pair_outs[b] for b in buckets]
            + [((micros * rows_here, width), BF), key_out, key_out],
            specs
            + [pl.BlockSpec((rows_here, width), lambda m, ids: (m, 0)), key_spec, key_spec],
        )
        dls += res[: len(buckets)]
        for values, value in zip((dqs, dks, dvs), res[len(buckets) :]):
            values.append(value)
        moving = ff.step(after(moving, dqs[-1]))
        if len(dqs) == 1:
            do = after(do, ff.operand)
        else:
            dqs[-1] = after(dqs[-1], ff.operand)

    share = (width + width // 2) // CHUNKS
    w_shape = (CHUNKS * share + 16, width)
    operands = [*dqs, *dks, *dvs, a1s, xhats, wq, wk, wv, gs_two]
    own, keep, send, w_send, w_keep = call(
        functools.partial(back_kernel, layout, share, len(dqs)),
        "back",
        9,
        (micros,),
        operands,
        [pl.BlockSpec((v.shape[0] // micros, width), lambda m, ids: (m, 0)) for v in dqs]
        + [pl.BlockSpec((width, v.shape[1] // micros), lambda m, ids: (0, m)) for v in dks + dvs]
        + [rank_spec] * 2
        + [whole(v.shape) for v in operands[-4:]],
        [
            (local_shape, F32),
            (local_shape, BF),
            ((2,) + local_shape, BF),
            (w_shape, BF),
            (w_shape, BF),
        ],
        [
            row_spec,
            row_spec,
            pl.BlockSpec((2, micro_rows, width), lambda m, ids: (0, m, 0)),
            whole(w_shape),
            whole(w_shape),
        ],
        [
            pltpu.VMEM((width, width), F32),
            pltpu.VMEM((width, width), F32),
            pltpu.VMEM((width, width), F32),
            pltpu.VMEM((8, width), F32),
            pltpu.VMEM((ranks * micro_rows, width), F32),
        ],
    )
    moving = ff.step(after(moving, w_send))
    w_send = after(w_send, ff.operand)
    w_sum = SumOverAll(w_keep, w_send, 16, sizes)
    w = w_sum.begin()
    near = near_rows(after(send, ff.operand))
    w = w_sum.step(w)
    near = after(near, w_sum.operand)
    far = far_rows(add_low(keep, near[1]))
    w = w_sum.step(w)
    moving = ff.step(after(moving, w_sum.operand))
    w = w_sum.step(w)
    w = w_sum.step(w)
    moving = ff.step(after(moving, w_sum.operand))
    w = w_sum.step(w)
    w = w_sum.step(w)
    fars = [(own, near, after(far, w_sum.operand))]
    last_args = [x, dh, gain_one] + [v for triple in fars for v in triple]
    grad_atoms = call(
        lambda ids, *refs: last_kernel(len(fars), *refs),
        "last",
        2,
        (1,),
        last_args,
        [whole(v.shape) for v in last_args],
        atom_outs,
        atom_specs,
    )
    moving = ff.step(after(moving, grad_atoms[0]))
    ff.step(moving)

    def ordered(ref, at, size, rows, mine):
        return jnp.concatenate(
            [
                ref[pl.ds(pl.multiple_of((c ^ mine) * rows + at, 16), size), :].astype(F32)
                for c in range(CHUNKS)
            ],
            axis=0,
        )

    def finish_ff(ids, mine_ref, other_ref, gu, gd, go):
        step = pl.program_id(0)
        own_tile = (step // half) == ids[0]
        size = width // CHUNKS
        at = (step % half) * 2 * size

        def put(ref, mine):
            gu[...] = ordered(ref, at, size, ff_rows, mine)
            gd[...] = ordered(ref, at + size, size, ff_rows, mine)

            @pl.when(step % half == 0)
            def _():
                go[...] = ordered(ref, 2 * half * size, size // 2, ff_rows, mine)

        pl.when(own_tile)(lambda: put(mine_ref, ids[1]))
        pl.when(jnp.logical_not(own_tile))(lambda: put(other_ref, ids[2]))

    grad_up, grad_down, go = call(
        finish_ff,
        "finish_ff",
        6,
        (tiles,),
        list(ff.result),
        [whole(ff_shape)] * 2,
        [(wu.shape, F32), (wd.shape, F32), (wo.shape, F32)],
        [
            pl.BlockSpec((width, tile), lambda t, ids: (0, t)),
            pl.BlockSpec((tile, width), lambda t, ids: (t, 0)),
            pl.BlockSpec((width // 2, width), lambda t, ids: (t // half, 0)),
        ],
    )
    w = w_sum.step(after(w, grad_down))
    w_sum.step(w)

    def finish_rest(ids, mine_ref, other_ref, gq_out, gk_out, gv_out, gs_out):
        size = width // CHUNKS

        def put(zero, zero_at, one, one_at):
            gq_out[...] = ordered(zero, 0, size, share, zero_at)
            gk_out[...] = ordered(one, 0, size, share, one_at).T
            gv_out[:, : width // 2] = ordered(zero, size, size // 2, share, zero_at).T
            gv_out[:, width // 2 :] = ordered(one, size, size // 2, share, one_at).T
            gs_out[...] = zero[CHUNKS * share :, :].astype(F32)

        pl.when(ids[0] == 0)(lambda: put(mine_ref, ids[1], other_ref, ids[2]))
        pl.when(ids[0] == 1)(lambda: put(other_ref, ids[2], mine_ref, ids[1]))

    gq, gk, gv, gs = call(
        finish_rest,
        "finish_rest",
        3,
        (1,),
        list(w_sum.result),
        [whole(w_shape)] * 2,
        [(wq.shape, F32)] * 3 + [((16, width), F32)],
        [whole(wq.shape)] * 3 + [whole((16, width))],
    )

    return (
        *[v.reshape(a.shape) for v, a in zip(atoms_out, atoms)],
        *[v.reshape(a.shape) for v, a in zip(pair_out, pairs)],
        *[v.reshape(a.shape) for v, a in zip(grad_atoms, atoms)],
        *[v.reshape(a.shape) for v, a in zip(dls, pairs)],
        gq,
        gk,
        gv,
        go,
        grad_up,
        grad_down,
        gs[0],
        gs[1],
        gs[2],
        gs[3],
    )


def solution(mesh):
    atom = P(None, "dp", "rows", None)
    pair = P(None, "dp", None, "rows", None)
    length = P(None, "dp")
    in_specs = (
        (atom,) * 3 + (pair,) * 3 + (length,) * 3 + (P(),) * 10 + (atom,) * 3 + (pair,) * 3
    )
    out_specs = (atom,) * 3 + (pair,) * 3 + (atom,) * 3 + (pair,) * 3 + (P(),) * 10
    body = functools.partial(shards, dict(mesh.shape))
    return jax.shard_map(
        body, mesh=mesh, in_specs=in_specs, out_specs=out_specs, check_vma=False
    )
```

time: 2080 us -> 213 us (0.10)
  blocking collectives: 1040 us -> 0 us
  matrix products: 469 us -> 0 us
  other arithmetic: 196 us -> 7.67 us
  local copies, waits for them, and re-layouts: 163 us -> 7.65 us
  waiting for transfers between devices: 177 us -> 59.3 us
  Pallas kernels: 0 us -> 110 us
  starting transfers between devices: 1.01 us -> 26.2 us
  between operations: 21.9 us -> 0.95 us
    unnamed x1 -> x0, blocking collectives: 847 us -> none
    dot_general x284 -> x0, matrix products: 437 us -> none  [the longest x72 179 us: outer_sum(): lax.dot_general(flat_left, flat_right, (((0,), (0,)), ((), ())), preferre...]
    psum x1 -> x0, waiting for transfers between devices: 177 us -> none  [shards(): totals = lax.psum(totals, ('dp', 'rows'))]
    all_gather x24 -> x0, blocking collectives: 151 us -> none  [the longest x4 29.1 us: shards(): lax.all_gather(outgoing[1], 'rows', axis=1, tiled=True)]
    pallas_call x0 -> x10, Pallas kernels: none -> 110 us  [call(): pl.pallas_call(kernel, grid_spec=pltpu.PrefetchScalarGridSpec(num_scalar_...]
    sub x8 -> x0, other arithmetic: 107 us -> none  [backward_rest(): grad_softmax - row_inner]
    ppermute x0 -> x21, waiting for transfers between devices: none -> 59.3 us  [the longest x12 41.4 us: send_all(): return lax.ppermute(value, ('dp', 'rows'), perm)]
    another operation x30 -> x0, other arithmetic: 53 us -> none  [the longest x15 39 us: shards(): pair_out = [jnp.stack(pair_lists[bucket], axis=0) for bucket in range(3)]]
  transfers between devices with their start and end apart: 9 -> 21, of which waited for: 1 -> 13; matrix products, arithmetic and copies ran while one was open for 32% -> 2% of each run, Pallas kernels for 0% -> 29%
where the time goes in v2:
time: 213 us; the launch traced here: 212 us
  Pallas kernels  110 us (52%)
  waiting for transfers between devices  59.3 us (28%)
  starting transfers between devices  26.2 us (12%)
  other arithmetic  7.67 us (4%)
  local copies, waits for them, and re-layouts  7.65 us (4%)
    pallas_call x10, Pallas kernels, call(): pl.pallas_call(kernel, grid_spec=pltpu.PrefetchScalarGridSpec(num_scalar_...  110 us
    ppermute x12, waiting for transfers between devices, send_all(): return lax.ppermute(value, ('dp', 'rows'), perm)  41.4 us
    ppermute x9, waiting for transfers between devices, exchange(): return lax.ppermute(value, axis, [(i, i ^ distance) for i in range(size)])  17.9 us
    ppermute x12, starting transfers between devices, send_all(): return lax.ppermute(value, ('dp', 'rows'), perm)  17.6 us
    ppermute x9, starting transfers between devices, exchange(): return lax.ppermute(value, axis, [(i, i ^ distance) for i in range(size)])  8.56 us
    unnamed x41, local copies, waits for them, and re-layouts  4.86 us
    convert_element_type x12, other arithmetic, add_low(): return total.astype(BF)  4.57 us
  transfers between devices with their start and end apart: 21, of which 13 were waited for; matrix products, arithmetic and copies ran while one was open for 2% of the time, Pallas kernels for 29%

profile of v2, /device:TPU:0, one launch (start us, length us, event | category | flops | bytes accessed | tf_op | source)
XLA Modules:
  0.0 212.2 jit_solution(8604148620662630772)
XLA Ops:
  0.7 1.2 pad_maximum_fusion.3
  1.9 0.5 collective-permute-start
  2.4 2.6 %collective-permute-start.1 = (bf16[512,512]{1,0:T(8,128)(2,1)S(1)}, bf16[512,512]{1,0:T(8,128)(2,1)S(1)}, u32[]{:S(2)}, u32[]{:S(2)}) collective-permute-start(bf16[512,512]{1,0:T(8,128)(2,1)S(1)} %bitcast.63), channel_id=1, source_target_pairs={{0,2},{1,3},{2,0},{3,1},{4,6},{5,7},{6,4},{7,5},{8,10},{9,11},{10,... | collective-permute-start | bytes 1572872 | tf_op jit(solution)/shard_map/ppermute | solution.py:345
  5.0 0.6 stack.23.refs_0_.ids
  5.6 0.8 copy-done.13
  6.4 6.3 %front_near.1 = (bf16[4,512,512]{2,1,0:T(8,128)(2,1)}, bf16[4,512,512]{2,1,0:T(8,128)(2,1)}, bf16[4,512,512]{2,1,0:T(8,128)(2,1)}, bf16[4,512,512]{2,1,0:T(8,128)(2,1)}, bf16[512,512]{1,0:T(8,128)(2,1)}) custom-call(s32[5]{0:T(128)} %stack.23.refs_0_.ids, bf16[512,512]{1,0:T(8,128)(2,1)} %bitcast.64, bf16[512,512]{1,0:T(8,128)(2,1)} %copy-done.13, ...), custom_call_target="tpu_custom_call" | custom-call | bytes 3200000 | tf_op jit(solution)/shard_map/front_near/pallas_call | solution.py:487
  12.7 4.8 %collective-permute-done.1.refs_1_ = bf16[512,512]{1,0:T(8,128)(2,1)S(1)} collective-permute-done((bf16[512,512]{1,0:T(8,128)(2,1)S(1)}, bf16[512,512]{1,0:T(8,128)(2,1)S(1)}, u32[]{:S(2)}, u32[]{:S(2)}) %collective-permute-start.1) | collective-permute-done | bytes 524320 | tf_op jit(solution)/shard_map/ppermute | solution.py:345
  17.5 0.1 copy.60
  17.6 0.6 reshape.151.refs_2_
  18.2 0.8 pad_maximum_fusion.4
  19.1 0.4 collective-permute-done.2.refs_2_
  19.4 0.8 copy-done.12
  20.2 5.9 %front_far.1 = (bf16[4,512,512]{2,1,0:T(8,128)(2,1)}, bf16[4,512,512]{2,1,0:T(8,128)(2,1)}, bf16[4,512,512]{2,1,0:T(8,128)(2,1)}, bf16[4,512,512]{2,1,0:T(8,128)(2,1)}) custom-call(s32[5]{0:T(128)} %stack.23.refs_0_.ids, bf16[512,512]{1,0:T(8,128)(2,1)} %copy-done.10, ...), custom_call_target="tpu_custom_call", output_to_operand_aliasing={{0}: (8, {}), {1}: (9, {}), {2}: (10, {}), {3}: (11, {})} | custom-call | bytes 3200000 | tf_op jit(solution)/shard_map/front_far/pallas_call | solution.py:487
  26.1 20.4 %attend.1 = (bf16[4,64,64,256]{3,2,1,0:T(8,128)(2,1)}, bf16[4,64,32,128]{3,2,1,0:T(8,128)(2,1)}, bf16[8,64,16,64]{3,2,1,0:T(8,128)(2,1)}, bf16[4,64,64,256]{3,2,...) custom-call(s32[5]{0:T(128)} %stack.23.refs_0_.ids, ...), custom_call_target="tpu_custom_call" | custom-call | bytes 14400000 | tf_op jit(solution)/shard_map/attend/pallas_call | solution.py:487
  46.4 19.3 %dense.1 = (bf16[4,64,512]{2,1,0:T(8,128)(2,1)}, bf16[4,32,512]{2,1,0:T(8,128)(2,1)}, bf16[4,32,512]{2,1,0:T(8,128)(2,1)}, f32[512,512]{1,0:T(8,128)}, bf16[512,...) custom-call(s32[5]{0:T(128)} %stack.23.refs_0_.ids, ...), custom_call_target="tpu_custom_call" | custom-call | bytes 12800000 | tf_op jit(solution)/shard_map/dense/pallas_call | solution.py:487
  65.8 0.1 collective-permute-start.3
  65.8 4.7 %collective-permute-done.3 = bf16[2304,512]{1,0:T(8,128)(2,1)S(1)} collective-permute-done((bf16[2304,512]{1,0:T(8,128)(2,1)}, bf16[2304,512]{1,0:T(8,128)(2,1)S(1)}, u32[]{:S(2)}, u32[]{:S(2)}) %collective-permute-start.3) | collective-permute-done | bytes 2359328 | tf_op jit(solution)/shard_map/ppermute | solution.py:345
  70.5 2.3 %add_convert_fusion = (bf16[1152,512]{1,0:T(8,128)(2,1)S(1)}, bf16[1152,512]{1,0:T(8,128)(2,1)S(1)}) fusion(bf16[2304,512]{1,0:T(8,128)(2,1)S(1)} %collective-permute-done.3, bf16[2304,512]{1,0:T(8,128)(2,1)} %get-tuple-element.103), kind=kLoop, calls=%fused_computation.1 | loop fusion | flops 4718592 | bytes 7077888 | tf_op jit(solution)/shard_map/convert_element_type | solution.py:352
  72.8 1.8 collective-permute-start.4
  74.6 16.5 %attend_back_big.1 = (bf16[4,64,64,256]{3,2,1,0:T(8,128)(2,1)}, bf16[256,512]{1,0:T(8,128)(2,1)}, bf16[512,1024]{1,0:T(8,128)(2,1)}, bf16[512,1024]{1,0:T(8,128)(2,1)}) custom-call(s32[5]{0:T(128)} %stack.23.refs_0_.ids, bf16[512,512]{1,0:T(8,128)(2,1)} %get-tuple-element.86.refs_3_.refs_0_, bf16[512,512]{1,0:T(8,128)(2,1)} %get-tuple-element.110.refs_1_, ...), custom_call_target="tpu_custom_call" | custom-call | bytes 12000000 | tf_op jit(solution)/shard_map/attend_back_big/pallas_call | solution.py:487
  91.1 0.2 add_convert_fusion.6
  91.2 1.6 collective-permute-start.5
  92.8 15.4 %attend_back_rest.1 = (bf16[4,64,32,128]{3,2,1,0:T(8,128)(2,1)}, bf16[8,64,16,64]{3,2,1,0:T(8,128)(2,1)}, bf16[256,512]{1,0:T(8,128)(2,1)}, bf16[512,1024]{1,0:T(8,128)(2,1)}, bf16[512,1024]{1,0:T(8,128)(2,1)}) custom-call(s32[5]{0:T(128)} %stack.23.refs_0_.ids, bf16[512,512]{1,0:T(8,128)(2,1)} %get-tuple-element.86.refs_3_.refs_0_, ...), custom_call_target="tpu_custom_call" | custom-call | bytes 12000000 | tf_op jit(solution)/shard_map/attend_back_rest/pallas_call | solution.py:487
  108.2 0.2 add_convert_fusion.4
  108.4 1.6 collective-permute-start.6
  110.0 11.4 %back.1 = (f32[512,512]{1,0:T(8,128)}, bf16[512,512]{1,0:T(8,128)(2,1)}, bf16[2,512,512]{2,1,0:T(8,128)(2,1)}, bf16[784,512]{1,0:T(8,128)(2,1)}, bf16[784,512]{1,0:T(8,128)(2,1)}) custom-call(s32[5]{0:T(128)} %stack.23.refs_0_.ids, bf16[256,512]{1,0:T(8,128)(2,1)} %get-tuple-element.108.refs_0_, bf16[256,512]{1,0:T(8,128)(2,1)} %get-tuple-element.115.refs_1_, ...), custom_call_target="tpu_custom_call" | custom-call | bytes 7200000 | tf_op jit(solution)/shard_map/back/pallas_call | solution.py:487
  121.4 2.3 %collective-permute-done.6 = bf16[576,512]{1,0:T(8,128)(2,1)S(1)} collective-permute-done((bf16[576,512]{1,0:T(8,128)(2,1)S(1)}, bf16[576,512]{1,0:T(8,128)(2,1)S(1)}, u32[]{:S(2)}, u32[]{:S(2)}) %collective-permute-start.6) | collective-permute-done | bytes 589856 | tf_op jit(solution)/shard_map/ppermute | solution.py:368
  123.8 0.2 add_convert_fusion.3
  123.9 0.3 collective-permute-start.8
  124.2 2.3 %collective-permute-done.8 = bf16[784,512]{1,0:T(8,128)(2,1)S(1)} collective-permute-done((bf16[784,512]{1,0:T(8,128)(2,1)}, bf16[784,512]{1,0:T(8,128)(2,1)S(1)}, u32[]{:S(2)}, u32[]{:S(2)}) %collective-permute-start.8) | collective-permute-done | bytes 802848 | tf_op jit(solution)/shard_map/ppermute | solution.py:345
  126.5 1.1 add_convert_fusion.8
  127.6 0.6 collective-permute-start.10
  128.2 2.5 %collective-permute-start.16 = (bf16[576,512]{1,0:T(8,128)(2,1)S(1)}, bf16[576,512]{1,0:T(8,128)(2,1)S(1)}, u32[]{:S(2)}, u32[]{:S(2)}) collective-permute-start(bf16[576,512]{1,0:T(8,128)(2,1)S(1)} %add_convert_fusion.3), channel_id=1, source_target_pairs={{0,16},{1,9},{2,18},{3,11},{4,20},{5,13},{6,22},{7,15},{8,24},{9,1... | collective-permute-start | bytes 1769480 | tf_op jit(solution)/shard_map/ppermute | solution.py:368
  130.8 0.1 add_convert_fusion.7
  130.9 4.7 %collective-permute-done.10 = bf16[400,512]{1,0:T(8,128)(2,1)S(1)} collective-permute-done((bf16[400,512]{1,0:T(8,128)(2,1)S(1)}, bf16[400,512]{1,0:T(8,128)(2,1)S(1)}, u32[]{:S(2)}, u32[]{:S(2)}) %collective-permute-start.10) | collective-permute-done | bytes 409632 | tf_op jit(solution)/shard_map/ppermute | solution.py:368
  135.7 8.2 %collective-permute-done.16 = bf16[576,512]{1,0:T(8,128)(2,1)S(1)} collective-permute-done((bf16[576,512]{1,0:T(8,128)(2,1)S(1)}, bf16[576,512]{1,0:T(8,128)(2,1)S(1)}, u32[]{:S(2)}, u32[]{:S(2)}) %collective-permute-start.16) | collective-permute-done | bytes 589856 | tf_op jit(solution)/shard_map/ppermute | solution.py:368
  143.9 0.6 collective-permute-start.11
  144.4 0.2 add_convert_fusion.2
  144.6 1.5 collective-permute-start.17
  146.1 3.6 %collective-permute-done.11 = bf16[208,512]{1,0:T(8,128)(2,1)S(1)} collective-permute-done((bf16[208,512]{1,0:T(8,128)(2,1)S(1)}, bf16[208,512]{1,0:T(8,128)(2,1)S(1)}, u32[]{:S(2)}, u32[]{:S(2)}) %collective-permute-start.11) | collective-permute-done | bytes 213024 | tf_op jit(solution)/shard_map/ppermute | solution.py:368
  149.7 0.1 add_convert_fusion.11
  149.8 2.7 %collective-permute-start.12 = (bf16[208,512]{1,0:T(8,128)(2,1)S(1)}, bf16[208,512]{1,0:T(8,128)(2,1)S(1)}, u32[]{:S(2)}, u32[]{:S(2)}) collective-permute-start(bf16[208,512]{1,0:T(8,128)(2,1)S(1)} %add_convert_fusion.11), channel_id=1, source_target_pairs={{0,8},{1,17},{2,10},{3,19},{4,12},{5,21},{6,14},{7,23},{8,0},{9,25... | collective-permute-start | bytes 638984 | tf_op jit(solution)/shard_map/ppermute | solution.py:368
  152.5 6.0 %collective-permute-done.12 = bf16[208,512]{1,0:T(8,128)(2,1)S(1)} collective-permute-done((bf16[208,512]{1,0:T(8,128)(2,1)S(1)}, bf16[208,512]{1,0:T(8,128)(2,1)S(1)}, u32[]{:S(2)}, u32[]{:S(2)}) %collective-permute-start.12) | collective-permute-done | bytes 213024 | tf_op jit(solution)/shard_map/ppermute | solution.py:368
  158.6 0.6 collective-permute-start.18
  159.2 2.1 %collective-permute-start.13 = (bf16[208,512]{1,0:T(8,128)(2,1)S(1)}, bf16[208,512]{1,0:T(8,128)(2,1)S(1)}, u32[]{:S(2)}, u32[]{:S(2)}) collective-permute-start(bf16[208,512]{1,0:T(8,128)(2,1)S(1)} %add_convert_fusion.10), channel_id=1, source_target_pairs={{0,16},{1,9},{2,18},{3,11},{4,20},{5,13},{6,22},{7,15},{8,24},{9,1... | collective-permute-start | bytes 638984 | tf_op jit(solution)/shard_map/ppermute | solution.py:368
  161.3 0.1 fusion
  161.5 0.7 collective-permute-start.9
  162.2 6.1 %collective-permute-done.13 = bf16[208,512]{1,0:T(8,128)(2,1)S(1)} collective-permute-done((bf16[208,512]{1,0:T(8,128)(2,1)S(1)}, bf16[208,512]{1,0:T(8,128)(2,1)S(1)}, u32[]{:S(2)}, u32[]{:S(2)}) %collective-permute-start.13) | collective-permute-done | bytes 213024 | tf_op jit(solution)/shard_map/ppermute | solution.py:368
  168.3 1.7 collective-permute-start.14
  170.0 10.6 %collective-permute-done.14 = bf16[192,512]{1,0:T(8,128)(2,1)S(1)} collective-permute-done((bf16[192,512]{1,0:T(8,128)(2,1)S(1)}, bf16[192,512]{1,0:T(8,128)(2,1)S(1)}, u32[]{:S(2)}, u32[]{:S(2)}) %collective-permute-start.14) | collective-permute-done | bytes 196640 | tf_op jit(solution)/shard_map/ppermute | solution.py:368
  180.6 0.8 pad_maximum_fusion.5
  181.4 0.8 copy-done.14
  182.2 4.3 %last.1 = (bf16[4,64,512]{2,1,0:T(8,128)(2,1)}, bf16[4,32,512]{2,1,0:T(8,128)(2,1)}, bf16[4,32,512]{2,1,0:T(8,128)(2,1)}) custom-call(s32[5]{0:T(128)} %stack.23.refs_0_.ids, bf16[512,512]{1,0:T(8,128)(2,1)} %bitcast.66, f32[512,512]{1,0:T(8,128)} %get-tuple-element.101.refs_1_, f32[1,512]{1,0:T(1,128)} %bitcast.80, f32[512,512]{1,0:T(8,128)} %get-tuple-element.123.refs_3_, ...), custom_call_target="tpu_custom_call" | custom-call | bytes 1600000 | tf_op jit(solution)/shard_map/last/pallas_call | solution.py:487
  186.5 0.2 pad_maximum_fusion.mine_ref
  186.7 3.9 %collective-permute-start.19 = (bf16[2304,512]{1,0:T(8,128)(2,1)S(1)}, bf16[2304,512]{1,0:T(8,128)(2,1)S(1)}, u32[]{:S(2)}, u32[]{:S(2)}) collective-permute-start(bf16[2304,512]{1,0:T(8,128)(2,1)S(1)} %pad_maximum_fusion.mine_ref), channel_id=1, source_target_pairs={{0,1},{1,0},{2,3},{3,2},{4,5},{5,4},{6,7},{7,6},{8,9},{9,8},{10,11... | collective-permute-start | bytes 7077896 | tf_op jit(solution)/shard_map/ppermute | solution.py:345
  190.7 0.4 collective-permute-start.15
  191.1 3.8 %collective-permute-done.19.other_ref = bf16[2304,512]{1,0:T(8,128)(2,1)S(1)} collective-permute-done((bf16[2304,512]{1,0:T(8,128)(2,1)S(1)}, bf16[2304,512]{1,0:T(8,128)(2,1)S(1)}, u32[]{:S(2)}, u32[]{:S(2)}) %collective-permute-start.19) | collective-permute-done | bytes 2359328 | tf_op jit(solution)/shard_map/ppermute | solution.py:345
  194.8 1.4 copy-done.3
  196.3 7.0 %finish_ff.1 = (f32[512,2048]{1,0:T(8,128)}, f32[2048,512]{1,0:T(8,128)}, f32[512,512]{1,0:T(8,128)}) custom-call(s32[5]{0:T(128)} %stack.23.refs_0_.ids, bf16[2304,512]{1,0:T(8,128)(2,1)} %copy-done, bf16[2304,512]{1,0:T(8,128)(2,1)} %copy-done.3), custom_call_target="tpu_custom_call" | custom-call | bytes 4800000 | tf_op jit(solution)/shard_map/finish_ff/pallas_call | solution.py:487
  203.4 0.4 collective-permute-start.20
  203.8 1.9 collective-permute-done.20.other_ref
  205.7 0.9 copy-done.7
  206.6 4.1 %finish_rest.1 = (f32[512,512]{1,0:T(8,128)}, f32[512,512]{1,0:T(8,128)}, f32[512,512]{1,0:T(8,128)}, f32[16,512]{1,0:T(8,128)}) custom-call(s32[5]{0:T(128)} %stack.23.refs_0_.ids, bf16[784,512]{1,0:T(8,128)(2,1)} %copy-done.2, bf16[784,512]{1,0:T(8,128)(2,1)} %copy-done.7), custom_call_target="tpu_custom_call" | custom-call | bytes 2400000 | tf_op jit(solution)/shard_map/finish_rest/pallas_call | solution.py:487
  210.8 1.5 fusion.1
  (61 shorter events, 0.5 us)
Async XLA Ops:
  0.7 16.9 %copy-start.18 = (s32[4,2]{0,1:T(2,128)S(1)}, s32[4,2]{0,1:T(2,128)}, u32[]{:S(2)}) copy-start(s32[4,2]{0,1:T(2,128)} %param.33) | copy-start | bytes 100
  0.7 17.5 %copy-start.16 = (bf16[4,2,16,512]{3,2,1,0:T(8,128)(2,1)S(1)}, bf16[4,2,16,512]{3,2,1,0:T(8,128)(2,1)}, u32[]{:S(2)}) copy-start(bf16[4,2,16,512]{3,2,1,0:T(8,128)(2,1)} %param.46) | copy-start | bytes 393220
  0.7 17.5 %copy-start.17 = (bf16[4,1,32,512]{3,2,1,0:T(8,128)(2,1)S(1)}, bf16[4,1,32,512]{3,2,1,0:T(8,128)(2,1)}, u32[]{:S(2)}) copy-start(bf16[4,1,32,512]{3,2,1,0:T(8,128)(2,1)} %param.45) | copy-start | bytes 393220
  0.7 17.5 %copy-start.15 = (bf16[4,1,64,512]{3,2,1,0:T(8,128)(2,1)S(1)}, bf16[4,1,64,512]{3,2,1,0:T(8,128)(2,1)}, u32[]{:S(2)}) copy-start(bf16[4,1,64,512]{3,2,1,0:T(8,128)(2,1)} %param.44) | copy-start | bytes 786436
  1.9 3.8 %copy-start.1 = (bf16[4,128,512]{2,1,0:T(8,128)(2,1)}, bf16[4,128,512]{2,1,0:T(8,128)(2,1)S(1)}, u32[]{:S(2)}) copy-start(bf16[4,128,512]{2,1,0:T(8,128)(2,1)S(1)} %pad_maximum_fusion.3) | copy-start | bytes 1572868
  1.9 3.7 %collective-permute-start = (bf16[512,512]{1,0:T(8,128)(2,1)S(1)}, bf16[512,512]{1,0:T(8,128)(2,1)S(1)}, u32[]{:S(2)}, u32[]{:S(2)}) collective-permute-start(bf16[512,512]{1,0:T(8,128)(2,1)S(1)} %bitcast.62), channel_id=1, source_target_pairs={{0,1},{1,0},{2,3},{3,2},{4,5},{5,4},{6,7},{7,6},{8,9},{9,8},{10,11... | collective-permute-start | bytes 1572872 | tf_op jit(solution)/shard_map/ppermute | solution.py:345
  2.4 15.1 %collective-permute-start.1 = (bf16[512,512]{1,0:T(8,128)(2,1)S(1)}, bf16[512,512]{1,0:T(8,128)(2,1)S(1)}, u32[]{:S(2)}, u32[]{:S(2)}) collective-permute-start(bf16[512,512]{1,0:T(8,128)(2,1)S(1)} %bitcast.63), channel_id=1, source_target_pairs={{0,2},{1,3},{2,0},{3,1},{4,6},{5,7},{6,4},{7,5},{8,10},{9,11},{10,... | collective-permute-start | bytes 1572872 | tf_op jit(solution)/shard_map/ppermute | solution.py:345
  5.6 0.8 copy-start.13
  17.5 1.9 copy-start.10
  17.5 1.9 collective-permute-start.2
  19.4 0.8 copy-start.12
  65.8 4.7 %collective-permute-start.3 = (bf16[2304,512]{1,0:T(8,128)(2,1)}, bf16[2304,512]{1,0:T(8,128)(2,1)S(1)}, u32[]{:S(2)}, u32[]{:S(2)}) collective-permute-start(bf16[2304,512]{1,0:T(8,128)(2,1)} %get-tuple-element.104), channel_id=1, source_target_pairs={{0,1},{1,0},{2,3},{3,2},{4,5},{5,4},{6,7},{7,6},{8,9},{9,8},{10,11... | collective-permute-start | bytes 7077896 | tf_op jit(solution)/shard_map/ppermute | solution.py:345
  72.8 18.3 %collective-permute-start.4 = (bf16[1152,512]{1,0:T(8,128)(2,1)S(1)}, bf16[1152,512]{1,0:T(8,128)(2,1)S(1)}, u32[]{:S(2)}, u32[]{:S(2)}) collective-permute-start(bf16[1152,512]{1,0:T(8,128)(2,1)S(1)} %get-tuple-element.195), channel_id=1, source_target_pairs={{0,4},{1,3},{2,6},{3,1},{4,0},{5,7},{6,2},{7,5},{8,12},{9,11},{10,... | collective-permute-start | bytes 3538952 | tf_op jit(solution)/shard_map/ppermute | solution.py:368
  91.2 16.9 %collective-permute-start.5 = (bf16[576,512]{1,0:T(8,128)(2,1)S(1)}, bf16[576,512]{1,0:T(8,128)(2,1)S(1)}, u32[]{:S(2)}, u32[]{:S(2)}) collective-permute-start(bf16[576,512]{1,0:T(8,128)(2,1)S(1)} %add_convert_fusion.6), channel_id=1, source_target_pairs={{0,2},{1,5},{2,0},{3,7},{4,6},{5,1},{6,4},{7,3},{8,10},{9,13},{10,... | collective-permute-start | bytes 1769480 | tf_op jit(solution)/shard_map/ppermute | solution.py:368
  108.4 15.4 %collective-permute-start.6 = (bf16[576,512]{1,0:T(8,128)(2,1)S(1)}, bf16[576,512]{1,0:T(8,128)(2,1)S(1)}, u32[]{:S(2)}, u32[]{:S(2)}) collective-permute-start(bf16[576,512]{1,0:T(8,128)(2,1)S(1)} %add_convert_fusion.4), channel_id=1, source_target_pairs={{0,8},{1,17},{2,10},{3,19},{4,12},{5,21},{6,14},{7,23},{8,0},{9,25... | collective-permute-start | bytes 1769480 | tf_op jit(solution)/shard_map/ppermute | solution.py:368
  121.4 9.3 %copy-start.6 = (bf16[784,512]{1,0:T(8,128)(2,1)S(1)}, bf16[784,512]{1,0:T(8,128)(2,1)}, u32[]{:S(2)}) copy-start(bf16[784,512]{1,0:T(8,128)(2,1)} %get-tuple-element.128) | copy-start | bytes 2408452
  123.9 2.6 %collective-permute-start.8 = (bf16[784,512]{1,0:T(8,128)(2,1)}, bf16[784,512]{1,0:T(8,128)(2,1)S(1)}, u32[]{:S(2)}, u32[]{:S(2)}) collective-permute-start(bf16[784,512]{1,0:T(8,128)(2,1)} %get-tuple-element.129), channel_id=1, source_target_pairs={{0,1},{1,0},{2,3},{3,2},{4,5},{5,4},{6,7},{7,6},{8,9},{9,8},{10,11... | collective-permute-start | bytes 2408456 | tf_op jit(solution)/shard_map/ppermute | solution.py:345
  127.6 8.0 %collective-permute-start.10 = (bf16[400,512]{1,0:T(8,128)(2,1)S(1)}, bf16[400,512]{1,0:T(8,128)(2,1)S(1)}, u32[]{:S(2)}, u32[]{:S(2)}) collective-permute-start(bf16[400,512]{1,0:T(8,128)(2,1)S(1)} %add_convert_fusion.8), channel_id=1, source_target_pairs={{0,4},{1,3},{2,6},{3,1},{4,0},{5,7},{6,2},{7,5},{8,12},{9,11},{10,... | collective-permute-start | bytes 1228808 | tf_op jit(solution)/shard_map/ppermute | solution.py:368
  128.2 15.7 %collective-permute-start.16 = (bf16[576,512]{1,0:T(8,128)(2,1)S(1)}, bf16[576,512]{1,0:T(8,128)(2,1)S(1)}, u32[]{:S(2)}, u32[]{:S(2)}) collective-permute-start(bf16[576,512]{1,0:T(8,128)(2,1)S(1)} %add_convert_fusion.3), channel_id=1, source_target_pairs={{0,16},{1,9},{2,18},{3,11},{4,20},{5,13},{6,22},{7,15},{8,24},{9,1... | collective-permute-start | bytes 1769480 | tf_op jit(solution)/shard_map/ppermute | solution.py:368
  130.9 21.6 %copy-start.19 = (bf16[2,512,512]{2,1,0:T(8,128)(2,1)S(1)}, bf16[2,512,512]{2,1,0:T(8,128)(2,1)}, u32[]{:S(2)}) copy-start(bf16[2,512,512]{2,1,0:T(8,128)(2,1)} %get-tuple-element.127) | copy-start | bytes 3145732
  143.9 5.8 %collective-permute-start.11 = (bf16[208,512]{1,0:T(8,128)(2,1)S(1)}, bf16[208,512]{1,0:T(8,128)(2,1)S(1)}, u32[]{:S(2)}, u32[]{:S(2)}) collective-permute-start(bf16[208,512]{1,0:T(8,128)(2,1)S(1)} %add_convert_fusion.12), channel_id=1, source_target_pairs={{0,2},{1,5},{2,0},{3,7},{4,6},{5,1},{6,4},{7,3},{8,10},{9,13},{10,... | collective-permute-start | bytes 638984 | tf_op jit(solution)/shard_map/ppermute | solution.py:368
  144.6 14.0 %collective-permute-start.17 = (bf16[576,512]{1,0:T(8,128)(2,1)S(1)}, bf16[576,512]{1,0:T(8,128)(2,1)S(1)}, u32[]{:S(2)}, u32[]{:S(2)}) collective-permute-start(bf16[576,512]{1,0:T(8,128)(2,1)S(1)} %add_convert_fusion.2), channel_id=1, source_target_pairs={{0,2},{1,5},{2,0},{3,7},{4,6},{5,1},{6,4},{7,3},{8,10},{9,13},{10,... | collective-permute-start | bytes 1769480 | tf_op jit(solution)/shard_map/ppermute | solution.py:368
  146.1 15.2 %copy-start.11 = (bf16[512,512]{1,0:T(8,128)(2,1)S(1)}, bf16[512,512]{1,0:T(8,128)(2,1)}, u32[]{:S(2)}) copy-start(bf16[512,512]{1,0:T(8,128)(2,1)} %get-tuple-element.131) | copy-start | bytes 1572868
  149.8 8.7 %collective-permute-start.12 = (bf16[208,512]{1,0:T(8,128)(2,1)S(1)}, bf16[208,512]{1,0:T(8,128)(2,1)S(1)}, u32[]{:S(2)}, u32[]{:S(2)}) collective-permute-start(bf16[208,512]{1,0:T(8,128)(2,1)S(1)} %add_convert_fusion.11), channel_id=1, source_target_pairs={{0,8},{1,17},{2,10},{3,19},{4,12},{5,21},{6,14},{7,23},{8,0},{9,25... | collective-permute-start | bytes 638984 | tf_op jit(solution)/shard_map/ppermute | solution.py:368
  152.5 6.7 %collective-permute-start.7 = (bf16[2,512,512]{2,1,0:T(8,128)(2,1)S(1)}, bf16[2,512,512]{2,1,0:T(8,128)(2,1)S(1)}, u32[]{:S(2)}, u32[]{:S(2)}) collective-permute-start(bf16[2,512,512]{2,1,0:T(8,128)(2,1)S(1)} %copy-done.19), channel_id=1, source_target_pairs={{0,1},{1,0},{2,3},{3,2},{4,5},{5,4},{6,7},{7,6},{8,9},{9,8},{10,11... | collective-permute-start | bytes 3145736 | tf_op jit(solution)/shard_map/ppermute | solution.py:345
  158.6 27.9 %collective-permute-start.18 = (bf16[1152,512]{1,0:T(8,128)(2,1)S(1)}, bf16[1152,512]{1,0:T(8,128)(2,1)S(1)}, u32[]{:S(2)}, u32[]{:S(2)}) collective-permute-start(bf16[1152,512]{1,0:T(8,128)(2,1)S(1)} %pad_maximum_fusion.1), channel_id=1, source_target_pairs={{0,4},{1,3},{2,6},{3,1},{4,0},{5,7},{6,2},{7,5},{8,12},{9,11},{10,... | collective-permute-start | bytes 3538952 | tf_op jit(solution)/shard_map/ppermute | solution.py:368
  159.2 23.0 %copy-start.4 = (bf16[2,512,512]{2,1,0:T(8,128)(2,1)}, bf16[2,512,512]{2,1,0:T(8,128)(2,1)S(1)}, u32[]{:S(2)}) copy-start(bf16[2,512,512]{2,1,0:T(8,128)(2,1)S(1)} %collective-permute-done.7.refs_4_) | copy-start | bytes 3145732
  159.2 9.0 %collective-permute-start.13 = (bf16[208,512]{1,0:T(8,128)(2,1)S(1)}, bf16[208,512]{1,0:T(8,128)(2,1)S(1)}, u32[]{:S(2)}, u32[]{:S(2)}) collective-permute-start(bf16[208,512]{1,0:T(8,128)(2,1)S(1)} %add_convert_fusion.10), channel_id=1, source_target_pairs={{0,16},{1,9},{2,18},{3,11},{4,20},{5,13},{6,22},{7,15},{8,24},{9,1... | collective-permute-start | bytes 638984 | tf_op jit(solution)/shard_map/ppermute | solution.py:368
  161.5 20.0 %collective-permute-start.9 = (bf16[512,512]{1,0:T(8,128)(2,1)S(1)}, bf16[512,512]{1,0:T(8,128)(2,1)S(1)}, u32[]{:S(2)}, u32[]{:S(2)}) collective-permute-start(bf16[512,512]{1,0:T(8,128)(2,1)S(1)} %fusion), channel_id=1, source_target_pairs={{0,2},{1,3},{2,0},{3,1},{4,6},{5,7},{6,4},{7,5},{8,10},{9,11},{10,... | collective-permute-start | bytes 1572872 | tf_op jit(solution)/shard_map/ppermute | solution.py:345
  168.3 22.8 %copy-start.5 = (bf16[208,512]{1,0:T(8,128)(2,1)}, bf16[208,512]{1,0:T(8,128)(2,1)S(1)}, u32[]{:S(2)}) copy-start(bf16[208,512]{1,0:T(8,128)(2,1)S(1)} %add_convert_fusion.9) | copy-start | bytes 638980
  168.3 12.3 %collective-permute-start.14 = (bf16[192,512]{1,0:T(8,128)(2,1)S(1)}, bf16[192,512]{1,0:T(8,128)(2,1)S(1)}, u32[]{:S(2)}, u32[]{:S(2)}) collective-permute-start(bf16[192,512]{1,0:T(8,128)(2,1)S(1)} %slice.113), channel_id=1, source_target_pairs={{0,2},{1,5},{2,0},{3,7},{4,6},{5,1},{6,4},{7,3},{8,10},{9,13},{10,... | collective-permute-start | bytes 589832 | tf_op jit(solution)/shard_map/ppermute | solution.py:368
  180.6 5.9 %copy-start.8 = (bf16[192,512]{1,0:T(8,128)(2,1)}, bf16[192,512]{1,0:T(8,128)(2,1)S(1)}, u32[]{:S(2)}) copy-start(bf16[192,512]{1,0:T(8,128)(2,1)S(1)} %collective-permute-done.14) | copy-start | bytes 589828
  181.4 0.8 copy-start.14
  186.7 8.1 %copy-start = (bf16[2304,512]{1,0:T(8,128)(2,1)}, bf16[2304,512]{1,0:T(8,128)(2,1)S(1)}, u32[]{:S(2)}) copy-start(bf16[2304,512]{1,0:T(8,128)(2,1)S(1)} %pad_maximum_fusion.mine_ref) | copy-start | bytes 7077892
  186.7 8.1 %collective-permute-start.19 = (bf16[2304,512]{1,0:T(8,128)(2,1)S(1)}, bf16[2304,512]{1,0:T(8,128)(2,1)S(1)}, u32[]{:S(2)}, u32[]{:S(2)}) collective-permute-start(bf16[2304,512]{1,0:T(8,128)(2,1)S(1)} %pad_maximum_fusion.mine_ref), channel_id=1, source_target_pairs={{0,1},{1,0},{2,3},{3,2},{4,5},{5,4},{6,7},{7,6},{8,9},{9,8},{10,11... | collective-permute-start | bytes 7077896 | tf_op jit(solution)/shard_map/ppermute | solution.py:345
  190.7 12.6 %collective-permute-start.15 = (bf16[384,512]{1,0:T(8,128)(2,1)}, bf16[384,512]{1,0:T(8,128)(2,1)S(1)}, u32[]{:S(2)}, u32[]{:S(2)}) collective-permute-start(bf16[384,512]{1,0:T(8,128)(2,1)} %pad_maximum_fusion.5), channel_id=1, source_target_pairs={{0,4},{1,3},{2,6},{3,1},{4,0},{5,7},{6,2},{7,5},{8,12},{9,11},{10,... | collective-permute-start | bytes 1179656 | tf_op jit(solution)/shard_map/ppermute | solution.py:368
  191.0 12.2 %slice-start = ((bf16[208,512]{1,0:T(8,128)(2,1)}), bf16[16,512]{1,0:T(8,128)(2,1)S(1)}, s32[]{:S(2)}) async-start(bf16[208,512]{1,0:T(8,128)(2,1)} %copy-done.5), calls=%async_computation | async-start | bytes 32768 | tf_op jit(solution)/shard_map/slice | solution.py:411
  191.1 12.2 %copy-start.9 = (bf16[192,512]{1,0:T(8,128)(2,1)S(1)}, bf16[192,512]{1,0:T(8,128)(2,1)}, u32[]{:S(2)}) copy-start(bf16[192,512]{1,0:T(8,128)(2,1)} %copy-done.8) | copy-start | bytes 589828
  194.8 1.4 copy-start.3
  203.4 2.4 %copy-start.2 = (bf16[784,512]{1,0:T(8,128)(2,1)}, bf16[784,512]{1,0:T(8,128)(2,1)S(1)}, u32[]{:S(2)}) copy-start(bf16[784,512]{1,0:T(8,128)(2,1)S(1)} %pad_maximum_fusion.2.mine_ref) | copy-start | bytes 2408452
  203.4 2.4 %collective-permute-start.20 = (bf16[784,512]{1,0:T(8,128)(2,1)S(1)}, bf16[784,512]{1,0:T(8,128)(2,1)S(1)}, u32[]{:S(2)}, u32[]{:S(2)}) collective-permute-start(bf16[784,512]{1,0:T(8,128)(2,1)S(1)} %pad_maximum_fusion.2.mine_ref), channel_id=1, source_target_pairs={{0,1},{1,0},{2,3},{3,2},{4,5},{5,4},{6,7},{7,6},{8,9},{9,8},{10,11... | collective-permute-start | bytes 2408456 | tf_op jit(solution)/shard_map/ppermute | solution.py:345
  205.7 0.9 copy-start.7

commit v3 on v2

--- a/solution.py
+++ b/solution.py
@@ -16,7 +16,7 @@
 GELU_A = 0.044715
 MIB = 1 << 20
 CHUNKS = 4
-LIMIT = 58
+LIMIT = 60
 
 
 def dot_nn(a, b):
@@ -47,24 +47,24 @@
     )
 
 
-def front_kernel(pieces, copied, *refs):
-    me_ref = refs[0]
-    xs = refs[1 : 1 + pieces]
-    wq, wk, wv, gain, shift = refs[1 + pieces : 6 + pieces]
-    outs = refs[6 + pieces + copied :]
-    step = pl.program_id(0)
-    for piece in range(pieces):
-
-        @pl.when(step == piece)
-        def _(piece=piece):
-            xhat, _ = normalize(xs[piece][...].astype(F32))
-            a1 = (xhat * gain[...] + shift[...]).astype(BF)
-            outs[0][0] = dot_nn(a1, wk[...]).astype(BF)
-            outs[1][0] = dot_nn(a1, wv[...]).astype(BF)
-            outs[2][0] = a1
-            outs[3][0] = xhat.astype(BF)
-            if not copied and piece == 0:
-                outs[4][...] = dot_nn(a1, wq[...]).astype(BF)
+def front_kernel(ids, x0, x1, wq, wk, wv, gain, shift, q_out, *outs):
+    for piece, x_ref in enumerate((x0, x1)):
+
+        @pl.when(pl.program_id(0) == piece)
+        def _(piece=piece, x_ref=x_ref):
+            a1 = front_rows(x_ref[...], gain, shift, wk, wv, [out.at[0] for out in outs])
+            if piece == 0:
+                q_out[...] = dot_nn(a1, wq[...]).astype(BF)
+
+
+def front_rows(x, gain, shift, wk, wv, outs):
+    xhat, _ = normalize(x.astype(F32))
+    a1 = (xhat * gain[...] + shift[...]).astype(BF)
+    outs[0][...] = dot_nn(a1, wk[...]).astype(BF)
+    outs[1][...] = dot_nn(a1, wv[...]).astype(BF)
+    outs[2][...] = a1
+    outs[3][...] = xhat.astype(BF)
+    return a1
 
 
 def head_mask(heads, first):
@@ -86,15 +86,28 @@
     return total
 
 
-def key_rows(ref, start, rows, lanes):
+def key_rows(ref, me, start, rows, lanes):
     return jnp.concatenate(
-        [ref[r, start : start + rows, lanes] for r in range(ref.shape[0])], axis=0
-    )
-
-
-def attn_fwd_kernel(layout, groups, heads, scale, *refs):
-    lens, (q_ref, k_ref, v_ref), pairs = refs[0:3], refs[3:6], refs[6:9]
-    pouts, ps, o_ref = refs[9:12], refs[12:15], refs[15]
+        [ref[me ^ r, start : start + rows, lanes] for r in range(ref.shape[0])], axis=0
+    )
+
+
+def attn_fwd_kernel(layout, groups, heads, scale, ids, *refs):
+    lens, q_ref, far_xs, weights, pairs = refs[0:3], refs[3], refs[4:6], refs[6:10], refs[10:13]
+    k_near, v_near = refs[13:15]
+    pouts, ps, o_ref, fronts, (k_ref, v_ref) = (
+        refs[17:20], refs[20:23], refs[23], refs[24:28], refs[28:30]
+    )
+    wk, wv, gain, shift = weights
+    me = ids[3]
+    near = k_near.shape[0]
+    for i in range(near):
+        k_ref[i] = k_near[i]
+        v_ref[i] = v_near[i]
+    for i, x_ref in enumerate(far_xs):
+        front_rows(x_ref[...], gain, shift, wk, wv, [out.at[i] for out in fronts])
+        k_ref[near + i] = fronts[0][i]
+        v_ref[near + i] = fronts[1][i]
     for (start, mols, rows, slots), len_ref, pair_ref, pout_ref, p_ref in zip(
         layout, lens, pairs, pouts, ps
     ):
@@ -107,8 +120,8 @@
             for group in range(groups):
                 lanes = slice(group * LANES, (group + 1) * LANES)
                 q = q_ref[at_row : at_row + rows, lanes]
-                k = key_rows(k_ref, at_row, rows, lanes)
-                v = key_rows(v_ref, at_row, rows, lanes)
+                k = key_rows(k_ref, me, at_row, rows, lanes)
+                v = key_rows(v_ref, me, at_row, rows, lanes)
                 total = jnp.zeros((rows, LANES), F32)
                 for first in range(0, heads, count):
                     at = slice(group * heads + first, group * heads + first + count)
@@ -124,7 +137,8 @@
                 o_ref[at_row : at_row + rows, lanes] = total
 
 
-def attn_bwd_kernel(layout, groups, heads, scale, *refs):
+def attn_bwd_kernel(layout, groups, heads, scale, ids, *refs):
+    me = ids[3]
     count_of = len(layout)
     q_ref, do_ref, dd_ref, k_ref, v_ref = refs[0:5]
     ps, dpos = refs[5 : 5 + count_of], refs[5 + count_of : 5 + 2 * count_of]
@@ -140,13 +154,13 @@
             dk_all = []
             dv_all = []
             for mol in range(mols):
-                at_row = start + mol * rows
+                at_row = start - origin + mol * rows
                 rs = slice(at_row, at_row + rows)
                 q = q_ref[rs, lanes]
                 do = do_ref[rs, lanes]
                 dd = dd_ref[rs, lanes]
-                k = key_rows(k_ref, at_row, rows, lanes)
-                v = key_rows(v_ref, at_row, rows, lanes)
+                k = key_rows(k_ref, me, at_row, rows, lanes)
+                v = key_rows(v_ref, me, at_row, rows, lanes)
                 v_aug = jnp.concatenate([v, jnp.ones_like(v)], axis=1)
                 total = jnp.zeros((rows, LANES), F32)
                 dk = jnp.zeros((LANES, slots), F32)
@@ -165,8 +179,7 @@
                     total = unstacked(total, dot_nn(dl, k), heads, first, count, rows)
                     dk = dk + dot_tn(stacked(q, heads, first, count), dl)
                     dv = dv + dot_tn(do_s, p.reshape(count * rows, slots))
-                to = slice(at_row - origin, at_row - origin + rows)
-                dq_ref[to, lanes] = (total * scale).astype(BF)
+                dq_ref[rs, lanes] = (total * scale).astype(BF)
                 dk_all.append((dk * scale).astype(BF))
                 dv_all.append(dv.astype(BF))
             dk_ref[lanes, base : base + mols * slots] = jnp.concatenate(dk_all, axis=1)
@@ -190,7 +203,7 @@
     def molecules(ref):
         return jnp.concatenate(
             [
-                key_rows(ref, start + mol * rows, rows, slice(None))
+                key_rows(ref, me, start + mol * rows, rows, slice(None))
                 for start, mols, rows, slots in layout
                 for mol in range(mols)
             ],
@@ -203,7 +216,7 @@
     a1 = molecules(a_ref)
     gk_ref[...] += dot_nn(dk, a1)
     gv_ref[...] += dot_nn(dv, a1)
-    gq_ref[...] += dot_tn(a_ref[me], dq)
+    gq_ref[...] += dot_tn(a_ref[0], dq)
     daq = dot_nt(dq, wq[...])
     across = (((0,), (1,)), ((), ()))
     da = lax.dot_general(dk, wk[...], across, preferred_element_type=F32) + lax.dot_general(
@@ -211,7 +224,7 @@
     )
     da_s[...] = da
     gs_ref[0:1, :] += jnp.sum(da * molecules(h_ref).astype(F32), axis=0, keepdims=True) + jnp.sum(
-        daq * h_ref[me].astype(F32), axis=0, keepdims=True
+        daq * h_ref[0].astype(F32), axis=0, keepdims=True
     )
     gs_ref[1:2, :] += jnp.sum(da, axis=0, keepdims=True) + jnp.sum(daq, axis=0, keepdims=True)
     for piece in range(ranks):
@@ -372,6 +385,10 @@
     return lax.optimization_barrier((value,) + others)[0]
 
 
+def after_all(values, *others):
+    return list(lax.optimization_barrier((*values, *others)))[: len(values)]
+
+
 class SumOverAll:
     def __init__(self, keep, send, tail, sizes):
         self.stages = stage_permutes(sizes)
@@ -379,38 +396,42 @@
         self.tail = tail
         self.block = (keep.shape[0] - tail) // CHUNKS
         self.size = CHUNKS * self.block
-        self.keep = keep
+        self.terms = [keep]
         self.send = send
 
     def cut(self, value, start, stop):
         if not self.tail:
             return value[start:stop]
-        return jnp.concatenate([value[start:stop], value[self.size :]], axis=0)
+        return jnp.concatenate([value[start:stop], value[value.shape[0] - self.tail :]], axis=0)
 
     def split(self, got):
+        self.terms.append(got)
         half = self.size // 2
-        self.send = add_low(self.cut(self.keep, half, self.size), self.cut(got, half, self.size))
-        self.keep = add_low(self.cut(self.keep, 0, half), self.cut(got, 0, half))
+        send = add_low(*[self.cut(v, half, self.size) for v in self.terms])
         self.size = half
-        return self.send
+        return send
 
     def reduce(self):
         got = yield self.send, self.swap
         for stage in self.stages[:2]:
             got = yield self.split(got), functools.partial(send_all, perm=stage)
-        part = add_low(self.keep, got)
+        part = add_low(*[self.cut(v, 0, self.size) for v in self.terms + [got]])
         for stage in self.stages[2:4]:
             got = yield part, functools.partial(send_all, perm=stage)
             part = add_low(part, got)
         for stage in self.stages[4:]:
             part = add_low(part, send_all(part, stage))
         block = part[: self.block]
-        got = yield block, functools.partial(send_all, perm=self.stages[1])
-        low = jnp.concatenate([block, got], axis=0)
-        got = yield low, functools.partial(send_all, perm=self.stages[0])
-        mine = jnp.concatenate([low, got, part[self.block :]], axis=0)
-        other = yield mine, self.swap
-        self.result = (mine, other)
+        self.own = [part]
+        self.other = [self.swap(part)]
+        second = yield block, functools.partial(send_all, perm=self.stages[1])
+        self.own.append(second)
+        self.other.append(self.swap(second))
+        low = jnp.concatenate([block, second], axis=0)
+        high = yield low, functools.partial(send_all, perm=self.stages[0])
+        self.own.append(high)
+        got = yield high, self.swap
+        self.other.append(got)
         yield None, None
 
     def begin(self):
@@ -474,8 +495,8 @@
 
     near_rows = functools.partial(exchange, axis="rows", distance=1, size=ranks)
     far_rows = functools.partial(exchange, axis="rows", distance=2, size=ranks)
+    x2 = far_rows(x)
     x1 = near_rows(x)
-    x2 = far_rows(x)
 
     smem = pl.BlockSpec(memory_space=pltpu.SMEM)
     anywhere = pl.BlockSpec(memory_space=pl.ANY)
@@ -500,33 +521,21 @@
             **kw,
         )(ids, *operands)
 
-    gathered = (ranks, local, width)
-    weights = [wq, wk, wv, gain_one, shift_one]
-
-    def front(name, pieces, first, old):
-        piece_spec = pl.BlockSpec((1, local, width), lambda t, ids: (ids[3] ^ (first + t), 0, 0))
-        outs = [(gathered, BF)] * 4
-        out_specs = [piece_spec] * 4
-        if not old:
-            outs = outs + [((local, width), BF)]
-            out_specs = out_specs + [whole((local, width))]
-        operands = list(pieces) + weights
-        return call(
-            functools.partial(front_kernel, len(pieces), len(old)),
-            name,
-            4,
-            (len(pieces),),
-            operands + list(old),
-            [whole(v.shape) for v in operands] + [anywhere] * len(old),
-            outs,
-            out_specs,
-            input_output_aliases={1 + len(operands) + i: i for i in range(len(old))},
-        )
-
-    *early, q = front("front_near", (x, x1), 0, [])
-    x2 = after(x2, q)
+    near = 2
+    gathered = ((ranks, local, width), BF)
+    operands = [x, x1, wq, wk, wv, gain_one, shift_one]
+    q, *fronts = call(
+        front_kernel,
+        "front",
+        4,
+        (near,),
+        operands,
+        [whole(v.shape) for v in operands],
+        [((local, width), BF)] + [gathered] * 4,
+        [whole((local, width))] + [pl.BlockSpec((1, local, width), lambda t, ids: (t, 0, 0))] * 4,
+    )
+    x2 = after(x2, q, dy, *lens)
     x3 = near_rows(x2)
-    ks, vs, a1s, xhats = front("front_far", (x2, x3), 2, early)
 
     row_spec = pl.BlockSpec((micro_rows, width), lambda m, ids: (m, 0))
     rank_spec = pl.BlockSpec((ranks, micro_rows, width), lambda m, ids: (0, m, 0))
@@ -535,16 +544,28 @@
         for p in pair
     ]
     pair_outs = [(p.shape, BF) for p in pair]
-    *res, o = call(
-        lambda ids, *refs: attn_fwd_kernel(layout, groups, heads, scale, *refs),
+    near_spec = pl.BlockSpec((near, micro_rows, width), lambda m, ids: (0, m, 0))
+    far_spec = pl.BlockSpec((ranks - near, micro_rows, width), lambda m, ids: (1, m, 0))
+    operands = [*lens, q, x2, x3, wk, wv, gain_one, shift_one, *pair, *fronts]
+    res = call(
+        functools.partial(attn_fwd_kernel, layout, groups, heads, scale),
         "attend",
         18,
         (micros,),
-        [*lens, q, ks, vs, *pair],
-        [smem] * 3 + [row_spec, rank_spec, rank_spec] + pair_specs,
-        pair_outs * 2 + [((local, width), F32)],
-        pair_specs * 2 + [row_spec],
-    )
+        operands,
+        [smem] * 3
+        + [row_spec] * 3
+        + [whole(v.shape) for v in operands[6:10]]
+        + pair_specs
+        + [near_spec] * 2
+        + [anywhere] * 2,
+        pair_outs * 2 + [((local, width), F32)] + [gathered] * 4,
+        pair_specs * 2 + [row_spec] + [far_spec] * 4,
+        [pltpu.VMEM((ranks, micro_rows, width), BF)] * 2,
+        input_output_aliases={14 + i: 7 + i for i in range(4)},
+    )
+    o = res[6]
+    ks, vs, a1s, xhats = res[7:11]
     pair_out, probs = res[0:3], res[3:6]
 
     tiles = 4
@@ -591,15 +612,22 @@
         here = tuple(layout[b] for b in buckets)
         rows_here = sum(mols * rows for _, mols, rows, _ in here)
         specs = [pair_specs[b] for b in buckets]
+        per, at = micro_rows // rows_here, here[0][0] // rows_here
+        rows_spec = pl.BlockSpec(
+            (rows_here, width), lambda m, ids, per=per, at=at: (m * per + at, 0)
+        )
+        ranks_spec = pl.BlockSpec(
+            (ranks, rows_here, width), lambda m, ids, per=per, at=at: (0, m * per + at, 0)
+        )
         key_spec = pl.BlockSpec((width, rows_here * ranks), lambda m, ids: (0, m))
         key_out = ((width, micros * rows_here * ranks), BF)
         res = call(
-            lambda ids, *refs, here=here: attn_bwd_kernel(here, groups, heads, scale, *refs),
+            functools.partial(attn_bwd_kernel, here, groups, heads, scale),
             name,
             15,
             (micros,),
             [q, do, dd, ks, vs] + [probs[b] for b in buckets] + [dpo[b] for b in buckets],
-            [row_spec] * 3 + [rank_spec] * 2 + specs * 2,
+            [rows_spec] * 3 + [ranks_spec] * 2 + specs * 2,
             [pair_outs[b] for b in buckets]
             + [((micros * rows_here, width), BF), key_out, key_out],
             specs
@@ -650,24 +678,76 @@
         ],
     )
     moving = ff.step(after(moving, w_send))
-    w_send = after(w_send, ff.operand)
-    w_sum = SumOverAll(w_keep, w_send, 16, sizes)
+    ff_outs = [
+        ((CHUNKS, width // CHUNKS, hidden_units), F32),
+        ((2, half, CHUNKS, tile // CHUNKS, width), F32),
+        ((2, CHUNKS, width // 2 // CHUNKS, width), F32),
+    ]
+
+    def finish_ff(name, own, other, first, offsets, old):
+        def place(h, j, ids):
+            core = jnp.where(h == 0, ids[0], ids[4])
+            mine = jnp.where(h == 0, ids[1], ids[2])
+            return core, (first + j) ^ mine
+
+        def up_at(h, j, ids):
+            core, chunk = place(h, j, ids)
+            return chunk, 0, core
+
+        def down_at(h, j, ids):
+            core, chunk = place(h, j, ids)
+            return core, 0, chunk, 0, 0
+
+        def out_at(h, j, ids):
+            core, chunk = place(h, j, ids)
+            return core, chunk, 0, 0
+
+        def kernel(ids, *refs):
+            gu, gd, go = refs[-3:]
+            size = width // CHUNKS
+            for h in range(2):
+                for j in range(2):
+
+                    @pl.when((pl.program_id(0) == h) & (pl.program_id(1) == j))
+                    def _(ref=refs[len(own) * h + j % len(own)], at=offsets[j]):
+                        for t in range(half):
+                            row = at + 2 * t * size
+                            columns = slice(t * tile, (t + 1) * tile)
+                            gu[0, :, columns] = ref[row : row + size, :].astype(F32)
+                            gd[0, t, 0] = ref[row + size : row + 2 * size, :].astype(F32)
+                        row = at + 2 * half * size
+                        go[0, 0] = ref[row : row + size // 2, :].astype(F32)
+
+        operands = [*own, *other]
+        return call(
+            kernel,
+            name,
+            4,
+            (2, 2),
+            operands + list(old),
+            [whole(v.shape) for v in operands] + [anywhere] * len(old),
+            ff_outs,
+            [
+                pl.BlockSpec((1, width // CHUNKS, half * tile), up_at),
+                pl.BlockSpec((1, half, 1, tile // CHUNKS, width), down_at),
+                pl.BlockSpec((1, 1, width // 2 // CHUNKS, width), out_at),
+            ],
+            input_output_aliases={1 + len(operands) + i: i for i in range(len(old))},
+        )
+
+    near_da = near_rows(after(send, ff.operand))
+    w_sum = SumOverAll(w_keep, after(w_send, ff.operand), 16, sizes)
     w = w_sum.begin()
-    near = near_rows(after(send, ff.operand))
+    far = add_low(keep, near_da[1])
+    w = w_sum.step(after(w, far))
+    far = far_rows(far)
     w = w_sum.step(w)
-    near = after(near, w_sum.operand)
-    far = far_rows(add_low(keep, near[1]))
-    w = w_sum.step(w)
+    far = after(far, w_sum.operand)
+    w = w_sum.step(after(w, far))
     moving = ff.step(after(moving, w_sum.operand))
-    w = w_sum.step(w)
-    w = w_sum.step(w)
-    moving = ff.step(after(moving, w_sum.operand))
-    w = w_sum.step(w)
-    w = w_sum.step(w)
-    fars = [(own, near, after(far, w_sum.operand))]
-    last_args = [x, dh, gain_one] + [v for triple in fars for v in triple]
+    last_args = [x, dh, gain_one, own, near_da, after(far, ff.operand)]
     grad_atoms = call(
-        lambda ids, *refs: last_kernel(len(fars), *refs),
+        lambda ids, *refs: last_kernel(1, *refs),
         "last",
         2,
         (1,),
@@ -676,74 +756,75 @@
         atom_outs,
         atom_specs,
     )
-    moving = ff.step(after(moving, grad_atoms[0]))
+    w = w_sum.step(after(w, grad_atoms[0]))
+    moving = ff.step(after(moving, w_sum.operand))
+    w = w_sum.step(after(w, ff.operand))
+    grads = finish_ff(
+        "finish_ff_early", ff.own, after_all(ff.other, w_sum.operand), 0, (0, 0), []
+    )
+    w = w_sum.step(after(w, *grads))
+    moving = ff.step(after(moving, w_sum.operand))
     ff.step(moving)
-
-    def ordered(ref, at, size, rows, mine):
-        return jnp.concatenate(
-            [
-                ref[pl.ds(pl.multiple_of((c ^ mine) * rows + at, 16), size), :].astype(F32)
-                for c in range(CHUNKS)
-            ],
-            axis=0,
-        )
-
-    def finish_ff(ids, mine_ref, other_ref, gu, gd, go):
-        step = pl.program_id(0)
-        own_tile = (step // half) == ids[0]
-        size = width // CHUNKS
-        at = (step % half) * 2 * size
-
-        def put(ref, mine):
-            gu[...] = ordered(ref, at, size, ff_rows, mine)
-            gd[...] = ordered(ref, at + size, size, ff_rows, mine)
-
-            @pl.when(step % half == 0)
-            def _():
-                go[...] = ordered(ref, 2 * half * size, size // 2, ff_rows, mine)
-
-        pl.when(own_tile)(lambda: put(mine_ref, ids[1]))
-        pl.when(jnp.logical_not(own_tile))(lambda: put(other_ref, ids[2]))
-
-    grad_up, grad_down, go = call(
-        finish_ff,
-        "finish_ff",
-        6,
-        (tiles,),
-        list(ff.result),
-        [whole(ff_shape)] * 2,
-        [(wu.shape, F32), (wd.shape, F32), (wo.shape, F32)],
-        [
-            pl.BlockSpec((width, tile), lambda t, ids: (0, t)),
-            pl.BlockSpec((tile, width), lambda t, ids: (t, 0)),
-            pl.BlockSpec((width // 2, width), lambda t, ids: (t // half, 0)),
-        ],
-    )
+    grad_up, grad_down, go = finish_ff(
+        "finish_ff", ff.own[2:], ff.other[2:], 2, (0, ff_rows), grads
+    )
+
+    def ordered(pieces, at, size, rows, mine):
+        blocks = []
+        for chunk in range(CHUNKS):
+            place = chunk ^ mine
+            start = at + (rows if place == 3 else 0)
+            blocks.append(pieces[min(place, 2)][pl.ds(start, size), :])
+        return jnp.concatenate(blocks, axis=0)
+
+    def for_each_order(mine, put):
+        for value in range(CHUNKS):
+            pl.when(mine == value)(lambda value=value: put(value))
+
     w = w_sum.step(after(w, grad_down))
     w_sum.step(w)
 
-    def finish_rest(ids, mine_ref, other_ref, gq_out, gk_out, gv_out, gs_out):
+    def finish_rest(ids, *refs):
+        own_refs, other_refs = refs[0:3], refs[3:6]
+        gq_out, gk_out, gv_out = refs[6:9]
+        gains = refs[9:13]
         size = width // CHUNKS
 
-        def put(zero, zero_at, one, one_at):
-            gq_out[...] = ordered(zero, 0, size, share, zero_at)
-            gk_out[...] = ordered(one, 0, size, share, one_at).T
-            gv_out[:, : width // 2] = ordered(zero, size, size // 2, share, zero_at).T
-            gv_out[:, width // 2 :] = ordered(one, size, size // 2, share, one_at).T
-            gs_out[...] = zero[CHUNKS * share :, :].astype(F32)
-
-        pl.when(ids[0] == 0)(lambda: put(mine_ref, ids[1], other_ref, ids[2]))
-        pl.when(ids[0] == 1)(lambda: put(other_ref, ids[2], mine_ref, ids[1]))
-
-    gq, gk, gv, gs = call(
+        def put_zero(refs, mine):
+            gq_out[...] = ordered(refs, 0, size, share, mine).astype(F32)
+            gv_out[:, : width // 2] = ordered(refs, size, size // 2, share, mine).T.astype(F32)
+
+        def put_gains(ref):
+            rows = ref[share : share + 16, :].astype(F32)
+            for at, out in enumerate(gains):
+                out[...] = rows[at]
+
+        def put_one(refs, mine):
+            gk_out[...] = ordered(refs, 0, size, share, mine).T.astype(F32)
+            gv_out[:, width // 2 :] = ordered(refs, size, size // 2, share, mine).T.astype(F32)
+
+        @pl.when(ids[0] == 0)
+        def _():
+            for_each_order(ids[1], functools.partial(put_zero, own_refs))
+            for_each_order(ids[2], functools.partial(put_one, other_refs))
+            put_gains(own_refs[0])
+
+        @pl.when(ids[0] == 1)
+        def _():
+            for_each_order(ids[2], functools.partial(put_zero, other_refs))
+            for_each_order(ids[1], functools.partial(put_one, own_refs))
+            put_gains(other_refs[0])
+
+    pieces = w_sum.own + w_sum.other
+    gq, gk, gv, *gs = call(
         finish_rest,
         "finish_rest",
         3,
         (1,),
-        list(w_sum.result),
-        [whole(w_shape)] * 2,
-        [(wq.shape, F32)] * 3 + [((16, width), F32)],
-        [whole(wq.shape)] * 3 + [whole((16, width))],
+        pieces,
+        [whole(v.shape) for v in pieces],
+        [(wq.shape, F32)] * 3 + [((width,), F32)] * 4,
+        [whole(wq.shape)] * 3 + [whole((width,))] * 4,
     )
 
     return (
@@ -754,13 +835,10 @@
         gq,
         gk,
         gv,
-        go,
-        grad_up,
-        grad_down,
-        gs[0],
-        gs[1],
-        gs[2],
-        gs[3],
+        go.reshape(wo.shape),
+        grad_up.reshape(wu.shape),
+        grad_down.reshape(wd.shape),
+        *gs,
     )
 
 

time: 213 us -> 194 us (0.911)
  waiting for transfers between devices: 59.3 us -> 43.5 us
  starting transfers between devices: 26.2 us -> 20.8 us
  other arithmetic: 7.67 us -> 11.1 us
    ppermute x12, waiting for transfers between devices: 41.4 us -> 19.6 us  [send_all(): return lax.ppermute(value, ('dp', 'rows'), perm)]
    ppermute x9 -> x13, waiting for transfers between devices: 17.9 us -> 23.9 us  [exchange(): return lax.ppermute(value, axis, [(i, i ^ distance) for i in range(size)])]
    ppermute x9 -> x13, starting transfers between devices: 8.56 us -> 5.53 us  [exchange(): return lax.ppermute(value, axis, [(i, i ^ distance) for i in range(size)])]
    ppermute x12, starting transfers between devices: 17.6 us -> 15.3 us  [send_all(): return lax.ppermute(value, ('dp', 'rows'), perm)]
    convert_element_type x12 -> x11, other arithmetic: 4.57 us -> 6.34 us  [add_low(): return total.astype(BF)]
  transfers between devices with their start and end apart: 21 -> 25, of which waited for: 13 -> 16; matrix products, arithmetic and copies ran while one was open for 2% -> 4% of each run, Pallas kernels for 29% -> 33%
where the time goes in v3:
time: 194 us; the launch traced here: 193 us
  Pallas kernels  109 us (56%)
  waiting for transfers between devices  43.5 us (22%)
  starting transfers between devices  20.8 us (11%)
  other arithmetic  11.1 us (6%)
  local copies, waits for them, and re-layouts  7.65 us (4%)
    pallas_call x10, Pallas kernels, call(): pl.pallas_call(kernel, grid_spec=pltpu.PrefetchScalarGridSpec(num_scalar_...  109 us
    ppermute x13, waiting for transfers between devices, exchange(): return lax.ppermute(value, axis, [(i, i ^ distance) for i in range(size)])  23.9 us
    ppermute x12, waiting for transfers between devices, send_all(): return lax.ppermute(value, ('dp', 'rows'), perm)  19.6 us
    ppermute x12, starting transfers between devices, send_all(): return lax.ppermute(value, ('dp', 'rows'), perm)  15.3 us
    convert_element_type x11, other arithmetic, add_low(): return total.astype(BF)  6.34 us
    unnamed x41, local copies, waits for them, and re-layouts  5.66 us
    ppermute x13, starting transfers between devices, exchange(): return lax.ppermute(value, axis, [(i, i ^ distance) for i in range(size)])  5.53 us
  transfers between devices with their start and end apart: 25, of which 16 were waited for; matrix products, arithmetic and copies ran while one was open for 4% of the time, Pallas kernels for 33%

profile of v3, /device:TPU:0, one launch (start us, length us, event | category | flops | bytes accessed | tf_op | source)
XLA Modules:
  0.0 193.0 jit_solution(5005864420551313127)
XLA Ops:
  0.7 1.1 pad_maximum_fusion.1
  1.8 0.5 collective-permute-start
  2.3 2.6 %collective-permute-start.1 = (bf16[512,512]{1,0:T(8,128)(2,1)S(1)}, bf16[512,512]{1,0:T(8,128)(2,1)S(1)}, u32[]{:S(2)}, u32[]{:S(2)}) collective-permute-start(bf16[512,512]{1,0:T(8,128)(2,1)S(1)} %bitcast.64), channel_id=1, source_target_pairs={{0,2},{1,3},{2,0},{3,1},{4,6},{5,7},{6,4},{7,5},{8,10},{9,11},{10,... | collective-permute-start | bytes 1572872 | tf_op jit(solution)/shard_map/ppermute | solution.py:358
  4.9 0.8 copy.63
  5.7 0.6 reshape.160.refs_2_
  6.3 0.6 stack.23.ids
  6.9 1.9 pad_maximum_fusion.2
  8.8 0.8 copy-done.14
  9.6 6.3 %front.1 = (bf16[512,512]{1,0:T(8,128)(2,1)}, bf16[4,512,512]{2,1,0:T(8,128)(2,1)}, bf16[4,512,512]{2,1,0:T(8,128)(2,1)}, bf16[4,512,512]{2,1,0:T(8,128)(2,1)}, bf16[4,512,512]{2,1,0:T(8,128)(2,1)}) custom-call(s32[5]{0:T(128)} %stack.23.ids, bf16[512,512]{1,0:T(8,128)(2,1)} %bitcast.65, bf16[512,512]{1,0:T(8,128)(2,1)} %copy-done.14, ...), custom_call_target="tpu_custom_call" | custom-call | bytes 3200000 | tf_op jit(solution)/shard_map/front/pallas_call | solution.py:508
  15.9 1.6 collective-permute-done.1.refs_4_
  17.4 1.9 collective-permute-done.2.refs_5_
  19.3 0.8 copy-done.13
  20.1 22.5 %attend.1 = (bf16[4,64,64,256]{3,2,1,0:T(8,128)(2,1)}, bf16[4,64,32,128]{3,2,1,0:T(8,128)(2,1)}, bf16[8,64,16,64]{3,2,1,0:T(8,128)(2,1)}, bf16[4,64,64,256]{3,2,...) custom-call(s32[5]{0:T(128)} %stack.23.ids, ...), custom_call_target="tpu_custom_call", output_to_operand_aliasing={{7}: (14, {}), {8}: (15, {}), {9}: (16, {}), {10}: (17, {})} | custom-call | bytes 14400000 | tf_op jit(solution)/shard_map/attend/pallas_call | solution.py:508
  42.6 19.3 %dense.1 = (bf16[4,64,512]{2,1,0:T(8,128)(2,1)}, bf16[4,32,512]{2,1,0:T(8,128)(2,1)}, bf16[4,32,512]{2,1,0:T(8,128)(2,1)}, f32[512,512]{1,0:T(8,128)}, bf16[512,...) custom-call(s32[5]{0:T(128)} %stack.23.ids, ...), custom_call_target="tpu_custom_call" | custom-call | bytes 12800000 | tf_op jit(solution)/shard_map/dense/pallas_call | solution.py:508
  62.1 4.6 %collective-permute-done.3 = bf16[2304,512]{1,0:T(8,128)(2,1)S(1)} collective-permute-done((bf16[2304,512]{1,0:T(8,128)(2,1)}, bf16[2304,512]{1,0:T(8,128)(2,1)S(1)}, u32[]{:S(2)}, u32[]{:S(2)}) %collective-permute-start.3) | collective-permute-done | bytes 2359328 | tf_op jit(solution)/shard_map/ppermute | solution.py:358
  66.7 2.5 %add_convert_fusion = bf16[1152,512]{1,0:T(8,128)(2,1)S(1)} fusion(bf16[2304,512]{1,0:T(8,128)(2,1)S(1)} %collective-permute-done.3, bf16[2304,512]{1,0:T(8,128)(2,1)} %get-tuple-element.114), kind=kLoop, calls=%fused_computation | loop fusion | flops 2359296 | bytes 3538944 | tf_op jit(solution)/shard_map/convert_element_type | solution.py:365
  69.2 1.8 collective-permute-start.4
  71.0 15.8 %attend_back_big.1 = (bf16[4,64,64,256]{3,2,1,0:T(8,128)(2,1)}, bf16[256,512]{1,0:T(8,128)(2,1)}, bf16[512,1024]{1,0:T(8,128)(2,1)}, bf16[512,1024]{1,0:T(8,128)(2,1)}) custom-call(s32[5]{0:T(128)} %stack.23.ids, bf16[512,512]{1,0:T(8,128)(2,1)} %get-tuple-element.99.refs_3_.refs_0_, bf16[512,512]{1,0:T(8,128)(2,1)} %get-tuple-element.123.refs_1_, ...), custom_call_target="tpu_custom_call" | custom-call | bytes 12000000 | tf_op jit(solution)/shard_map/attend_back_big/pallas_call | solution.py:508
  86.8 1.5 add_convert_fusion.4
  88.3 1.6 collective-permute-start.5
  89.9 15.2 %attend_back_rest.1 = (bf16[4,64,32,128]{3,2,1,0:T(8,128)(2,1)}, bf16[8,64,16,64]{3,2,1,0:T(8,128)(2,1)}, bf16[256,512]{1,0:T(8,128)(2,1)}, bf16[512,1024]{1,0:T(8,128)(2,1)}, bf16[512,1024]{1,0:T(8,128)(2,1)}) custom-call(s32[5]{0:T(128)} %stack.23.ids, bf16[512,512]{1,0:T(8,128)(2,1)} %get-tuple-element.99.refs_3_.refs_0_, ...), custom_call_target="tpu_custom_call" | custom-call | bytes 12000000 | tf_op jit(solution)/shard_map/attend_back_rest/pallas_call | solution.py:508
  105.1 1.6 add_convert_fusion.3
  106.6 1.6 collective-permute-start.6
  108.3 11.4 %back.1 = (f32[512,512]{1,0:T(8,128)}, bf16[512,512]{1,0:T(8,128)(2,1)}, bf16[2,512,512]{2,1,0:T(8,128)(2,1)}, bf16[784,512]{1,0:T(8,128)(2,1)}, bf16[784,512]{1,0:T(8,128)(2,1)}) custom-call(s32[5]{0:T(128)} %stack.23.ids, bf16[256,512]{1,0:T(8,128)(2,1)} %get-tuple-element.121.refs_0_, bf16[256,512]{1,0:T(8,128)(2,1)} %get-tuple-element.128.refs_1_, ...), custom_call_target="tpu_custom_call" | custom-call | bytes 7200000 | tf_op jit(solution)/shard_map/back/pallas_call | solution.py:508
  119.7 2.3 %collective-permute-done.6 = bf16[576,512]{1,0:T(8,128)(2,1)S(1)} collective-permute-done((bf16[576,512]{1,0:T(8,128)(2,1)S(1)}, bf16[576,512]{1,0:T(8,128)(2,1)S(1)}, u32[]{:S(2)}, u32[]{:S(2)}) %collective-permute-start.6) | collective-permute-done | bytes 589856 | tf_op jit(solution)/shard_map/ppermute | solution.py:381
  122.0 0.2 add_convert_fusion.2
  122.1 0.3 collective-permute-start.7
  122.5 0.2 collective-permute-start.9
  122.7 0.7 slice.78
  123.4 1.6 collective-permute-done.7.refs_4_
  125.2 1.0 collective-permute-done.9
  126.3 0.6 collective-permute-start.10
  126.9 2.6 %collective-permute-start.11 = (bf16[576,512]{1,0:T(8,128)(2,1)S(1)}, bf16[576,512]{1,0:T(8,128)(2,1)S(1)}, u32[]{:S(2)}, u32[]{:S(2)}) collective-permute-start(bf16[576,512]{1,0:T(8,128)(2,1)S(1)} %add_convert_fusion.2), channel_id=1, source_target_pairs={{0,16},{1,9},{2,18},{3,11},{4,20},{5,13},{6,22},{7,15},{8,24},{9,1... | collective-permute-start | bytes 1769480 | tf_op jit(solution)/shard_map/ppermute | solution.py:381
  129.5 0.5 collective-permute-start.8
  130.1 4.3 %collective-permute-done.10 = bf16[400,512]{1,0:T(8,128)(2,1)S(1)} collective-permute-done((bf16[400,512]{1,0:T(8,128)(2,1)S(1)}, bf16[400,512]{1,0:T(8,128)(2,1)S(1)}, u32[]{:S(2)}, u32[]{:S(2)}) %collective-permute-start.10) | collective-permute-done | bytes 409632 | tf_op jit(solution)/shard_map/ppermute | solution.py:381
  134.4 0.6 collective-permute-start.12
  135.0 9.4 %collective-permute-done.8.refs_5_ = bf16[512,512]{1,0:T(8,128)(2,1)S(1)} collective-permute-done((bf16[512,512]{1,0:T(8,128)(2,1)S(1)}, bf16[512,512]{1,0:T(8,128)(2,1)S(1)}, u32[]{:S(2)}, u32[]{:S(2)}) %collective-permute-start.8) | collective-permute-done | bytes 524320 | tf_op jit(solution)/shard_map/ppermute | solution.py:358
  144.4 2.8 %collective-permute-done.12 = bf16[208,512]{1,0:T(8,128)(2,1)S(1)} collective-permute-done((bf16[208,512]{1,0:T(8,128)(2,1)S(1)}, bf16[208,512]{1,0:T(8,128)(2,1)S(1)}, u32[]{:S(2)}, u32[]{:S(2)}) %collective-permute-start.12) | collective-permute-done | bytes 213024 | tf_op jit(solution)/shard_map/ppermute | solution.py:381
  147.3 0.2 add_convert_fusion.1.refs_0_
  147.4 0.6 collective-permute-start.15
  148.0 2.0 %collective-permute-start.13 = (bf16[208,512]{1,0:T(8,128)(2,1)S(1)}, bf16[208,512]{1,0:T(8,128)(2,1)S(1)}, u32[]{:S(2)}, u32[]{:S(2)}) collective-permute-start(bf16[208,512]{1,0:T(8,128)(2,1)S(1)} %add_convert_fusion.8), channel_id=1, source_target_pairs={{0,8},{1,17},{2,10},{3,19},{4,12},{5,21},{6,14},{7,23},{8,0},{9,25... | collective-permute-start | bytes 638984 | tf_op jit(solution)/shard_map/ppermute | solution.py:381
  150.0 4.3 %last.1 = (bf16[4,64,512]{2,1,0:T(8,128)(2,1)}, bf16[4,32,512]{2,1,0:T(8,128)(2,1)}, bf16[4,32,512]{2,1,0:T(8,128)(2,1)}) custom-call(s32[5]{0:T(128)} %stack.23.ids, bf16[512,512]{1,0:T(8,128)(2,1)} %bitcast.67, f32[512,512]{1,0:T(8,128)} %get-tuple-element.112.refs_1_, f32[1,512]{1,0:T(1,128)} %bitcast.84, f32[512,512]{1,0:T(8,128)} %get-tuple-element.136.refs_3_, ...), custom_call_target="tpu_custom_call" | custom-call | bytes 1600000 | tf_op jit(solution)/shard_map/last/pallas_call | solution.py:508
  154.4 1.0 collective-permute-done.13
  155.4 2.0 %collective-permute-done.15.refs_1_ = bf16[576,512]{1,0:T(8,128)(2,1)S(1)} collective-permute-done((bf16[576,512]{1,0:T(8,128)(2,1)S(1)}, bf16[576,512]{1,0:T(8,128)(2,1)S(1)}, u32[]{:S(2)}, u32[]{:S(2)}) %collective-permute-start.15) | collective-permute-done | bytes 589856 | tf_op jit(solution)/shard_map/ppermute | solution.py:381
  157.5 0.6 collective-permute-start.20
  158.1 2.4 %collective-permute-start.14 = (bf16[208,512]{1,0:T(8,128)(2,1)S(1)}, bf16[208,512]{1,0:T(8,128)(2,1)S(1)}, u32[]{:S(2)}, u32[]{:S(2)}) collective-permute-start(bf16[208,512]{1,0:T(8,128)(2,1)S(1)} %add_convert_fusion.7), channel_id=1, source_target_pairs={{0,16},{1,9},{2,18},{3,11},{4,20},{5,13},{6,22},{7,15},{8,24},{9,1... | collective-permute-start | bytes 638984 | tf_op jit(solution)/shard_map/ppermute | solution.py:381
  160.5 0.5 collective-permute-start.18
  161.0 6.1 %collective-permute-done.14 = bf16[208,512]{1,0:T(8,128)(2,1)S(1)} collective-permute-done((bf16[208,512]{1,0:T(8,128)(2,1)S(1)}, bf16[208,512]{1,0:T(8,128)(2,1)S(1)}, u32[]{:S(2)}, u32[]{:S(2)}) %collective-permute-start.14) | collective-permute-done | bytes 213024 | tf_op jit(solution)/shard_map/ppermute | solution.py:381
  167.3 0.8 copy-done.10
  168.1 4.9 %finish_ff_early.1 = (f32[4,128,2048]{2,1,0:T(8,128)}, f32[2,2,4,128,512]{4,3,2,1,0:T(8,128)}, f32[2,4,64,512]{3,2,1,0:T(8,128)}) custom-call(s32[5]{0:T(128)} %stack.23.ids, bf16[576,512]{1,0:T(8,128)(2,1)} %copy-done.1, bf16[576,512]{1,0:T(8,128)(2,1)} %copy-done.4, bf16[576,512]{1,0:T(8,128)(2,1)} %copy-done.10, ...), custom_call_target="tpu_custom_call" | custom-call | bytes 3200000 | tf_op jit(solution)/shard_map/finish_ff_early/pallas_call | solution.py:508
  173.0 1.7 pad_maximum_fusion.3
  174.7 1.1 collective-permute-done.20.refs_0_
  175.9 0.9 collective-permute-start.19
  176.8 1.9 %collective-permute-done.21.refs_1_ = bf16[1152,512]{1,0:T(8,128)(2,1)S(1)} collective-permute-done((bf16[1152,512]{1,0:T(8,128)(2,1)S(1)}, bf16[1152,512]{1,0:T(8,128)(2,1)S(1)}, u32[]{:S(2)}, u32[]{:S(2)}) %collective-permute-start.21) | collective-permute-done | bytes 1179680 | tf_op jit(solution)/shard_map/ppermute | solution.py:358
  178.7 1.0 copy-done.8
  179.7 4.9 %finish_ff.1 = (f32[4,128,2048]{2,1,0:T(8,128)}, f32[2,2,4,128,512]{4,3,2,1,0:T(8,128)}, f32[2,4,64,512]{3,2,1,0:T(8,128)}) custom-call(s32[5]{0:T(128)} %stack.23.ids, bf16[1152,512]{1,0:T(8,128)(2,1)} %copy-done.7, bf16[1152,512]{1,0:T(8,128)(2,1)} %copy-done.8, ...), custom_call_target="tpu_custom_call", output_to_operand_aliasing={{0}: (3, {}), {1}: (4, {}), {2}: (5, {})} | custom-call | bytes 3200000 | tf_op jit(solution)/shard_map/finish_ff/pallas_call | solution.py:508
  184.7 0.2 collective-permute-start.24
  184.9 0.4 collective-permute-start.22
  185.4 1.7 collective-permute-done.22.refs_3_
  187.0 0.2 collective-permute-done.23.refs_4_
  187.2 0.5 copy-done.18
  187.7 0.2 copy-done.19
  187.9 0.8 copy-done.17
  188.7 4.3 %finish_rest.1 = (f32[512,512]{1,0:T(8,128)}, f32[512,512]{1,0:T(8,128)}, f32[512,512]{1,0:T(8,128)}, f32[512]{0:T(512)}, f32[512]{0:T(512)}, /*index=5*/f32[512]{0:T(512)}, f32[512]{0:T(512)}) custom-call(s32[5]{0:T(128)} %stack.23.ids, bf16[208,512]{1,0:T(8,128)(2,1)} %copy-done.6, bf16[192,512]{1,0:T(8,128)(2,1)} %collective-permute-done.16.refs_1_, ...), custom_call_target="tpu_custom_call" | custom-call | bytes 2400000 | tf_op jit(solution)/shard_map/finish_rest/pallas_call | solution.py:508
  (61 shorter events, 1.1 us)
Async XLA Ops:
  1.8 7.0 %copy-start = (bf16[4,128,512]{2,1,0:T(8,128)(2,1)}, bf16[4,128,512]{2,1,0:T(8,128)(2,1)S(1)}, u32[]{:S(2)}) copy-start(bf16[4,128,512]{2,1,0:T(8,128)(2,1)S(1)} %pad_maximum_fusion.1) | copy-start | bytes 1572868
  1.8 7.0 %collective-permute-start = (bf16[512,512]{1,0:T(8,128)(2,1)S(1)}, bf16[512,512]{1,0:T(8,128)(2,1)S(1)}, u32[]{:S(2)}, u32[]{:S(2)}) collective-permute-start(bf16[512,512]{1,0:T(8,128)(2,1)S(1)} %bitcast.63), channel_id=1, source_target_pairs={{0,1},{1,0},{2,3},{3,2},{4,5},{5,4},{6,7},{7,6},{8,9},{9,8},{10,11... | collective-permute-start | bytes 1572872 | tf_op jit(solution)/shard_map/ppermute | solution.py:358
  2.3 15.1 %collective-permute-start.1 = (bf16[512,512]{1,0:T(8,128)(2,1)S(1)}, bf16[512,512]{1,0:T(8,128)(2,1)S(1)}, u32[]{:S(2)}, u32[]{:S(2)}) collective-permute-start(bf16[512,512]{1,0:T(8,128)(2,1)S(1)} %bitcast.64), channel_id=1, source_target_pairs={{0,2},{1,3},{2,0},{3,1},{4,6},{5,7},{6,4},{7,5},{8,10},{9,11},{10,... | collective-permute-start | bytes 1572872 | tf_op jit(solution)/shard_map/ppermute | solution.py:358
  8.8 0.8 copy-start.14
  17.4 1.9 copy-start.11
  17.4 1.9 collective-permute-start.2
  19.3 0.8 copy-start.13
  62.0 4.7 %collective-permute-start.3 = (bf16[2304,512]{1,0:T(8,128)(2,1)}, bf16[2304,512]{1,0:T(8,128)(2,1)S(1)}, u32[]{:S(2)}, u32[]{:S(2)}) collective-permute-start(bf16[2304,512]{1,0:T(8,128)(2,1)} %get-tuple-element.115), channel_id=1, source_target_pairs={{0,1},{1,0},{2,3},{3,2},{4,5},{5,4},{6,7},{7,6},{8,9},{9,8},{10,11... | collective-permute-start | bytes 7077896 | tf_op jit(solution)/shard_map/ppermute | solution.py:358
  66.7 4.2 %copy-start.3 = (bf16[2304,512]{1,0:T(8,128)(2,1)}, bf16[2304,512]{1,0:T(8,128)(2,1)S(1)}, u32[]{:S(2)}) copy-start(bf16[2304,512]{1,0:T(8,128)(2,1)S(1)} %collective-permute-done.3) | copy-start | bytes 7077892
  69.2 17.6 %collective-permute-start.4 = (bf16[1152,512]{1,0:T(8,128)(2,1)S(1)}, bf16[1152,512]{1,0:T(8,128)(2,1)}, u32[]{:S(2)}, u32[]{:S(2)}) collective-permute-start(bf16[1152,512]{1,0:T(8,128)(2,1)S(1)} %add_convert_fusion), channel_id=1, source_target_pairs={{0,4},{1,3},{2,6},{3,1},{4,0},{5,7},{6,2},{7,5},{8,12},{9,11},{10,... | collective-permute-start | bytes 3538952 | tf_op jit(solution)/shard_map/ppermute | solution.py:381
  71.0 15.8 %copy-start.2 = (bf16[2304,512]{1,0:T(8,128)(2,1)S(1)}, bf16[2304,512]{1,0:T(8,128)(2,1)}, u32[]{:S(2)}) copy-start(bf16[2304,512]{1,0:T(8,128)(2,1)} %get-tuple-element.114) | copy-start | bytes 7077892
  88.3 16.8 %collective-permute-start.5 = (bf16[576,512]{1,0:T(8,128)(2,1)S(1)}, bf16[576,512]{1,0:T(8,128)(2,1)S(1)}, u32[]{:S(2)}, u32[]{:S(2)}) collective-permute-start(bf16[576,512]{1,0:T(8,128)(2,1)S(1)} %add_convert_fusion.4), channel_id=1, source_target_pairs={{0,2},{1,5},{2,0},{3,7},{4,6},{5,1},{6,4},{7,3},{8,10},{9,13},{10,... | collective-permute-start | bytes 1769480 | tf_op jit(solution)/shard_map/ppermute | solution.py:381
  106.6 15.3 %collective-permute-start.6 = (bf16[576,512]{1,0:T(8,128)(2,1)S(1)}, bf16[576,512]{1,0:T(8,128)(2,1)S(1)}, u32[]{:S(2)}, u32[]{:S(2)}) collective-permute-start(bf16[576,512]{1,0:T(8,128)(2,1)S(1)} %add_convert_fusion.3), channel_id=1, source_target_pairs={{0,8},{1,17},{2,10},{3,19},{4,12},{5,21},{6,14},{7,23},{8,0},{9,25... | collective-permute-start | bytes 1769480 | tf_op jit(solution)/shard_map/ppermute | solution.py:381
  119.6 5.4 %copy-start.12 = (bf16[512,512]{1,0:T(8,128)(2,1)S(1)}, bf16[512,512]{1,0:T(8,128)(2,1)}, u32[]{:S(2)}) copy-start(bf16[512,512]{1,0:T(8,128)(2,1)} %get-tuple-element.141) | copy-start | bytes 1572868
  119.7 6.5 %copy-start.9 = (bf16[784,512]{1,0:T(8,128)(2,1)S(1)}, bf16[784,512]{1,0:T(8,128)(2,1)}, u32[]{:S(2)}) copy-start(bf16[784,512]{1,0:T(8,128)(2,1)} %get-tuple-element.142) | copy-start | bytes 2408452
  122.1 2.9 %collective-permute-start.7 = (bf16[2,512,512]{2,1,0:T(8,128)(2,1)}, bf16[2,512,512]{2,1,0:T(8,128)(2,1)S(1)}, u32[]{:S(2)}, u32[]{:S(2)}) collective-permute-start(bf16[2,512,512]{2,1,0:T(8,128)(2,1)} %get-tuple-element.140), channel_id=1, source_target_pairs={{0,1},{1,0},{2,3},{3,2},{4,5},{5,4},{6,7},{7,6},{8,9},{9,8},{10,11... | collective-permute-start | bytes 3145736 | tf_op jit(solution)/shard_map/ppermute | solution.py:358
  122.5 3.7 %collective-permute-start.9 = (bf16[784,512]{1,0:T(8,128)(2,1)}, bf16[784,512]{1,0:T(8,128)(2,1)S(1)}, u32[]{:S(2)}, u32[]{:S(2)}) collective-permute-start(bf16[784,512]{1,0:T(8,128)(2,1)} %get-tuple-element.143), channel_id=1, source_target_pairs={{0,1},{1,0},{2,3},{3,2},{4,5},{5,4},{6,7},{7,6},{8,9},{9,8},{10,11... | collective-permute-start | bytes 2408456 | tf_op jit(solution)/shard_map/ppermute | solution.py:358
  125.0 5.0 %copy-start.5 = (bf16[2,512,512]{2,1,0:T(8,128)(2,1)}, bf16[2,512,512]{2,1,0:T(8,128)(2,1)S(1)}, u32[]{:S(2)}) copy-start(bf16[2,512,512]{2,1,0:T(8,128)(2,1)S(1)} %collective-permute-done.7.refs_4_) | copy-start | bytes 3145732
  126.3 8.0 %collective-permute-start.10 = (bf16[400,512]{1,0:T(8,128)(2,1)S(1)}, bf16[400,512]{1,0:T(8,128)(2,1)S(1)}, u32[]{:S(2)}, u32[]{:S(2)}) collective-permute-start(bf16[400,512]{1,0:T(8,128)(2,1)S(1)} %add_convert_fusion.5), channel_id=1, source_target_pairs={{0,4},{1,3},{2,6},{3,1},{4,0},{5,7},{6,2},{7,5},{8,12},{9,11},{10,... | collective-permute-start | bytes 1228808 | tf_op jit(solution)/shard_map/ppermute | solution.py:381
  126.9 20.3 %collective-permute-start.11 = (bf16[576,512]{1,0:T(8,128)(2,1)S(1)}, bf16[576,512]{1,0:T(8,128)(2,1)S(1)}, u32[]{:S(2)}, u32[]{:S(2)}) collective-permute-start(bf16[576,512]{1,0:T(8,128)(2,1)S(1)} %add_convert_fusion.2), channel_id=1, source_target_pairs={{0,16},{1,9},{2,18},{3,11},{4,20},{5,13},{6,22},{7,15},{8,24},{9,1... | collective-permute-start | bytes 1769480 | tf_op jit(solution)/shard_map/ppermute | solution.py:381
  129.5 14.9 %collective-permute-start.8 = (bf16[512,512]{1,0:T(8,128)(2,1)S(1)}, bf16[512,512]{1,0:T(8,128)(2,1)S(1)}, u32[]{:S(2)}, u32[]{:S(2)}) collective-permute-start(bf16[512,512]{1,0:T(8,128)(2,1)S(1)} %fusion), channel_id=1, source_target_pairs={{0,2},{1,3},{2,0},{3,1},{4,6},{5,7},{6,4},{7,5},{8,10},{9,11},{10,... | collective-permute-start | bytes 1572872 | tf_op jit(solution)/shard_map/ppermute | solution.py:358
  134.4 12.7 %collective-permute-start.12 = (bf16[208,512]{1,0:T(8,128)(2,1)S(1)}, bf16[208,512]{1,0:T(8,128)(2,1)S(1)}, u32[]{:S(2)}, u32[]{:S(2)}) collective-permute-start(bf16[208,512]{1,0:T(8,128)(2,1)S(1)} %add_convert_fusion.9), channel_id=1, source_target_pairs={{0,2},{1,5},{2,0},{3,7},{4,6},{5,1},{6,4},{7,3},{8,10},{9,13},{10,... | collective-permute-start | bytes 638984 | tf_op jit(solution)/shard_map/ppermute | solution.py:381
  144.4 5.7 %copy-start.15 = (bf16[512,512]{1,0:T(8,128)(2,1)}, bf16[512,512]{1,0:T(8,128)(2,1)S(1)}, u32[]{:S(2)}) copy-start(bf16[512,512]{1,0:T(8,128)(2,1)S(1)} %collective-permute-done.8.refs_5_) | copy-start | bytes 1572868
  147.4 13.0 %copy-start.1 = (bf16[576,512]{1,0:T(8,128)(2,1)}, bf16[576,512]{1,0:T(8,128)(2,1)S(1)}, u32[]{:S(2)}) copy-start(bf16[576,512]{1,0:T(8,128)(2,1)S(1)} %add_convert_fusion.1.refs_0_) | copy-start | bytes 1769476
  147.4 9.9 %collective-permute-start.15 = (bf16[576,512]{1,0:T(8,128)(2,1)S(1)}, bf16[576,512]{1,0:T(8,128)(2,1)S(1)}, u32[]{:S(2)}, u32[]{:S(2)}) collective-permute-start(bf16[576,512]{1,0:T(8,128)(2,1)S(1)} %add_convert_fusion.1.refs_0_), channel_id=1, source_target_pairs={{0,2},{1,5},{2,0},{3,7},{4,6},{5,1},{6,4},{7,3},{8,10},{9,13},{10,... | collective-permute-start | bytes 1769480 | tf_op jit(solution)/shard_map/ppermute | solution.py:381
  148.0 7.3 %collective-permute-start.13 = (bf16[208,512]{1,0:T(8,128)(2,1)S(1)}, bf16[208,512]{1,0:T(8,128)(2,1)S(1)}, u32[]{:S(2)}, u32[]{:S(2)}) collective-permute-start(bf16[208,512]{1,0:T(8,128)(2,1)S(1)} %add_convert_fusion.8), channel_id=1, source_target_pairs={{0,8},{1,17},{2,10},{3,19},{4,12},{5,21},{6,14},{7,23},{8,0},{9,25... | collective-permute-start | bytes 638984 | tf_op jit(solution)/shard_map/ppermute | solution.py:381
  157.4 10.7 %copy-start.4 = (bf16[576,512]{1,0:T(8,128)(2,1)}, bf16[576,512]{1,0:T(8,128)(2,1)S(1)}, u32[]{:S(2)}) copy-start(bf16[576,512]{1,0:T(8,128)(2,1)S(1)} %collective-permute-done.15.refs_1_) | copy-start | bytes 1769476
  157.5 18.4 %collective-permute-start.20 = (bf16[1152,512]{1,0:T(8,128)(2,1)S(1)}, bf16[1152,512]{1,0:T(8,128)(2,1)S(1)}, u32[]{:S(2)}, u32[]{:S(2)}) collective-permute-start(bf16[1152,512]{1,0:T(8,128)(2,1)S(1)} %pad_maximum_fusion), channel_id=1, source_target_pairs={{0,4},{1,3},{2,6},{3,1},{4,0},{5,7},{6,2},{7,5},{8,12},{9,11},{10,... | collective-permute-start | bytes 3538952 | tf_op jit(solution)/shard_map/ppermute | solution.py:381
  158.1 9.0 %collective-permute-start.14 = (bf16[208,512]{1,0:T(8,128)(2,1)S(1)}, bf16[208,512]{1,0:T(8,128)(2,1)S(1)}, u32[]{:S(2)}, u32[]{:S(2)}) collective-permute-start(bf16[208,512]{1,0:T(8,128)(2,1)S(1)} %add_convert_fusion.7), channel_id=1, source_target_pairs={{0,16},{1,9},{2,18},{3,11},{4,20},{5,13},{6,22},{7,15},{8,24},{9,1... | collective-permute-start | bytes 638984 | tf_op jit(solution)/shard_map/ppermute | solution.py:381
  160.5 6.8 %collective-permute-start.17 = (bf16[576,512]{1,0:T(8,128)(2,1)S(1)}, bf16[576,512]{1,0:T(8,128)(2,1)S(1)}, u32[]{:S(2)}, u32[]{:S(2)}) collective-permute-start(bf16[576,512]{1,0:T(8,128)(2,1)S(1)} %add_convert_fusion.1.refs_0_), channel_id=1, source_target_pairs={{0,1},{1,0},{2,3},{3,2},{4,5},{5,4},{6,7},{7,6},{8,9},{9,8},{10,11... | collective-permute-start | bytes 1769480 | tf_op jit(solution)/shard_map/ppermute | solution.py:358
  160.5 7.7 %collective-permute-start.18 = (bf16[576,512]{1,0:T(8,128)(2,1)S(1)}, bf16[576,512]{1,0:T(8,128)(2,1)}, u32[]{:S(2)}, u32[]{:S(2)}) collective-permute-start(bf16[576,512]{1,0:T(8,128)(2,1)S(1)} %collective-permute-done.15.refs_1_), channel_id=1, source_target_pairs={{0,1},{1,0},{2,3},{3,2},{4,5},{5,4},{6,7},{7,6},{8,9},{9,8},{10,11... | collective-permute-start | bytes 1769480 | tf_op jit(solution)/shard_map/ppermute | solution.py:358
  167.2 17.7 %copy-start.6 = (bf16[208,512]{1,0:T(8,128)(2,1)}, bf16[208,512]{1,0:T(8,128)(2,1)S(1)}, u32[]{:S(2)}) copy-start(bf16[208,512]{1,0:T(8,128)(2,1)S(1)} %add_convert_fusion.6.refs_0_) | copy-start | bytes 638980
  167.2 5.8 %collective-permute-start.16 = (bf16[192,512]{1,0:T(8,128)(2,1)S(1)}, bf16[192,512]{1,0:T(8,128)(2,1)}, u32[]{:S(2)}, u32[]{:S(2)}) collective-permute-start(bf16[192,512]{1,0:T(8,128)(2,1)S(1)} %slice.92), channel_id=1, source_target_pairs={{0,2},{1,5},{2,0},{3,7},{4,6},{5,1},{6,4},{7,3},{8,10},{9,13},{10,... | collective-permute-start | bytes 589832 | tf_op jit(solution)/shard_map/ppermute | solution.py:381
  167.3 0.8 copy-start.10
  175.9 2.9 %copy-start.7 = (bf16[1152,512]{1,0:T(8,128)(2,1)}, bf16[1152,512]{1,0:T(8,128)(2,1)S(1)}, u32[]{:S(2)}) copy-start(bf16[1152,512]{1,0:T(8,128)(2,1)S(1)} %collective-permute-done.20.refs_0_) | copy-start | bytes 3538948
  175.9 2.8 %collective-permute-start.21 = (bf16[1152,512]{1,0:T(8,128)(2,1)S(1)}, bf16[1152,512]{1,0:T(8,128)(2,1)S(1)}, u32[]{:S(2)}, u32[]{:S(2)}) collective-permute-start(bf16[1152,512]{1,0:T(8,128)(2,1)S(1)} %collective-permute-done.20.refs_0_), channel_id=1, source_target_pairs={{0,1},{1,0},{2,3},{3,2},{4,5},{5,4},{6,7},{7,6},{8,9},{9,8},{10,11... | collective-permute-start | bytes 3538952 | tf_op jit(solution)/shard_map/ppermute | solution.py:358
  175.9 8.8 %collective-permute-start.19 = (bf16[384,512]{1,0:T(8,128)(2,1)}, bf16[384,512]{1,0:T(8,128)(2,1)S(1)}, u32[]{:S(2)}, u32[]{:S(2)}) collective-permute-start(bf16[384,512]{1,0:T(8,128)(2,1)} %pad_maximum_fusion.3), channel_id=1, source_target_pairs={{0,4},{1,3},{2,6},{3,1},{4,0},{5,7},{6,2},{7,5},{8,12},{9,11},{10,... | collective-permute-start | bytes 1179656 | tf_op jit(solution)/shard_map/ppermute | solution.py:381
  178.7 1.0 copy-start.8
  184.7 2.6 %copy-start.16 = (bf16[384,512]{1,0:T(8,128)(2,1)}, bf16[384,512]{1,0:T(8,128)(2,1)S(1)}, u32[]{:S(2)}) copy-start(bf16[384,512]{1,0:T(8,128)(2,1)S(1)} %collective-permute-done.19.refs_2_) | copy-start | bytes 1179652
  184.7 2.6 %collective-permute-start.24 = (bf16[384,512]{1,0:T(8,128)(2,1)S(1)}, bf16[384,512]{1,0:T(8,128)(2,1)S(1)}, u32[]{:S(2)}, u32[]{:S(2)}) collective-permute-start(bf16[384,512]{1,0:T(8,128)(2,1)S(1)} %collective-permute-done.19.refs_2_), channel_id=1, source_target_pairs={{0,1},{1,0},{2,3},{3,2},{4,5},{5,4},{6,7},{7,6},{8,9},{9,8},{10,11... | collective-permute-start | bytes 1179656 | tf_op jit(solution)/shard_map/ppermute | solution.py:358
  184.9 2.2 %collective-permute-start.22 = (bf16[208,512]{1,0:T(8,128)(2,1)S(1)}, bf16[208,512]{1,0:T(8,128)(2,1)S(1)}, u32[]{:S(2)}, u32[]{:S(2)}) collective-permute-start(bf16[208,512]{1,0:T(8,128)(2,1)S(1)} %add_convert_fusion.6.refs_0_), channel_id=1, source_target_pairs={{0,1},{1,0},{2,3},{3,2},{4,5},{5,4},{6,7},{7,6},{8,9},{9,8},{10,11... | collective-permute-start | bytes 638984 | tf_op jit(solution)/shard_map/ppermute | solution.py:358
  185.2 2.0 %collective-permute-start.23 = (bf16[192,512]{1,0:T(8,128)(2,1)}, bf16[192,512]{1,0:T(8,128)(2,1)S(1)}, u32[]{:S(2)}, u32[]{:S(2)}) collective-permute-start(bf16[192,512]{1,0:T(8,128)(2,1)} %collective-permute-done.16.refs_1_), channel_id=1, source_target_pairs={{0,1},{1,0},{2,3},{3,2},{4,5},{5,4},{6,7},{7,6},{8,9},{9,8},{10,11... | collective-permute-start | bytes 589832 | tf_op jit(solution)/shard_map/ppermute | solution.py:358
  187.0 0.7 copy-start.18
  187.2 0.7 copy-start.19
  187.9 0.8 copy-start.17

commit v4 on v3

--- a/solution.py
+++ b/solution.py
@@ -263,6 +263,18 @@
 
 def shard_rows(ref, value, at, rows, mine):
     size = value.shape[0] // CHUNKS
+    if isinstance(ref, tuple):
+        for chunk in range(CHUNKS):
+            place = chunk ^ mine
+            to = pl.multiple_of((place % 2) * rows + at, 16)
+            for half, part in enumerate(ref):
+
+                @pl.when(place // 2 == half)
+                def _(part=part, to=to, chunk=chunk):
+                    block = value[chunk * size : (chunk + 1) * size]
+                    part[pl.ds(to, size), :] = block.astype(part.dtype)
+
+        return
     for chunk in range(CHUNKS):
         to = pl.multiple_of((chunk ^ mine) * rows + at, 16)
         ref[pl.ds(to, size), :] = value[chunk * size : (chunk + 1) * size].astype(ref.dtype)
@@ -290,11 +302,12 @@
 
 def dense_kernel(
     tiles, rows, ids, x_ref, o_ref, dy_ref, wo, wu, wd, gain, shift,
-    yb, ym, ys, dh_ref, do_ref, dd_ref, gs_ref, send_ref, keep_ref,
-    a2_s, y_s, xhat_s, inv_s, da_s,
+    yb, ym, ys, dh_ref, do_ref, dd_ref, gs_ref, send_low, send_high, keep_ref,
+    a2_s, a2t_s, y_s, xhat_s, inv_s, da_s,
 ):
     step = pl.program_id(0)
     half_tiles = tiles // 2
+    send_ref = (send_low, send_high)
 
     @pl.when(step == 0)
     def _():
@@ -303,20 +316,23 @@
         y_s[...] = hidden
         xhat_s[...] = xhat
         inv_s[...] = jnp.broadcast_to(inv, inv_s.shape)
-        a2_s[...] = (xhat * gain[...] + shift[...]).astype(BF)
+        a2 = (xhat * gain[...] + shift[...]).astype(BF)
+        a2_s[...] = a2
+        a2t_s[...] = a2.T
         da_s[...] = jnp.zeros_like(da_s)
 
     dy = dy_ref[...]
     u = dot_nn(a2_s[...], wu[...])
     u2 = u * u
-    th = jnp.tanh(GELU_C * (u + GELU_A * u * u2))
-    half = 0.5 * (1.0 + th)
-    g = (u * half).astype(BF)
-    slope = half + 0.5 * u * (1.0 - th * th) * (GELU_C * (1.0 + 3.0 * GELU_A * u2))
+    th = jnp.tanh(u * (GELU_C + (GELU_C * GELU_A) * u2))
+    half = 0.5 + 0.5 * th
+    g = u * half
+    slope = half + g * (1.0 - th) * (GELU_C + (3.0 * GELU_C * GELU_A) * u2)
+    g = g.astype(BF)
     y_s[...] += dot_nn(g, wd[...])
     store_tile(send_ref, keep_ref, dot_tn(g, dy), step, 1, half_tiles, rows, ids)
     du = (dot_nt(dy, wd[...]) * slope).astype(BF)
-    store_tile(send_ref, keep_ref, dot_tn(a2_s[...], du), step, 0, half_tiles, rows, ids)
+    store_tile(send_ref, keep_ref, dot_nn(a2t_s[...], du), step, 0, half_tiles, rows, ids)
     da_s[...] += dot_nt(du, wu[...])
 
     @pl.when(step == tiles - 1)
@@ -412,9 +428,18 @@
         return send
 
     def reduce(self):
-        got = yield self.send, self.swap
-        for stage in self.stages[:2]:
-            got = yield self.split(got), functools.partial(send_all, perm=stage)
+        if isinstance(self.send, tuple):
+            half = self.size // 2
+            low = self.swap(self.send[0])
+            high = yield self.send[1], self.swap
+            first = add_low(self.terms[0][half:], high)
+            self.size = half
+            got = yield first, functools.partial(send_all, perm=self.stages[0])
+            self.terms.append(low)
+        else:
+            got = yield self.send, self.swap
+            got = yield self.split(got), functools.partial(send_all, perm=self.stages[0])
+        got = yield self.split(got), functools.partial(send_all, perm=self.stages[1])
         part = add_low(*[self.cut(v, 0, self.size) for v in self.terms + [got]])
         for stage in self.stages[2:4]:
             got = yield part, functools.partial(send_all, perm=stage)
@@ -581,9 +606,10 @@
     flat = whole(local_shape)
     ff_rows = (2 * half * tile + width // 2) // CHUNKS
     ff_shape = (CHUNKS * ff_rows, width)
+    ff_half = (CHUNKS // 2 * ff_rows, width)
     atom_outs = [((micros, a.shape[1] * a.shape[2], width), BF) for a in atoms]
     atom_specs = [whole(shape) for shape, _ in atom_outs]
-    *atoms_out, dh, do, dd, gs_two, ff_send, ff_keep = call(
+    *atoms_out, dh, do, dd, gs_two, ff_low, ff_high, ff_keep = call(
         functools.partial(dense_kernel, tiles, ff_rows),
         "dense",
         16,
@@ -592,17 +618,19 @@
         [flat, flat, flat, whole(wo.shape), up_spec, down_spec] + [whole((1, width))] * 2,
         atom_outs
         + [(local_shape, F32), (local_shape, BF), (local_shape, BF), ((8, width), F32)]
-        + [(ff_shape, BF)] * 2,
-        atom_specs + [flat, flat, flat, whole((8, width)), whole(ff_shape), whole(ff_shape)],
+        + [(ff_half, BF), (ff_half, BF), (ff_shape, BF)],
+        atom_specs
+        + [flat, flat, flat, whole((8, width)), whole(ff_half), whole(ff_half), whole(ff_shape)],
         [
             pltpu.VMEM(local_shape, BF),
+            pltpu.VMEM((width, local), BF),
             pltpu.VMEM(local_shape, F32),
             pltpu.VMEM(local_shape, F32),
             pltpu.VMEM((local, LANES), F32),
             pltpu.VMEM(local_shape, F32),
         ],
     )
-    ff = SumOverAll(ff_keep, ff_send, 0, sizes)
+    ff = SumOverAll(ff_keep, (ff_low, ff_high), 0, sizes)
     moving = ff.step(ff.begin())
     do = after(do, ff.operand)
 

time: 194 us -> 192 us (0.990)
  waiting for transfers between devices: 43.5 us -> 38.6 us
  starting transfers between devices: 20.8 us -> 25 us
    ppermute x12, starting transfers between devices: 15.3 us -> 18.5 us  [send_all(): return lax.ppermute(value, ('dp', 'rows'), perm)]
    ppermute x12, waiting for transfers between devices: 19.6 us -> 16.7 us  [send_all(): return lax.ppermute(value, ('dp', 'rows'), perm)]
    ppermute x13 -> x14, waiting for transfers between devices: 23.9 us -> 22 us  [exchange(): return lax.ppermute(value, axis, [(i, i ^ distance) for i in range(size)])]
    ppermute x13 -> x14, starting transfers between devices: 5.53 us -> 6.41 us  [exchange(): return lax.ppermute(value, axis, [(i, i ^ distance) for i in range(size)])]
    unnamed x41 -> x39, local copies, waits for them, and re-layouts: 5.66 us -> 5.66 us
  transfers between devices with their start and end apart: 25 -> 26, of which waited for: 16 -> 15; matrix products, arithmetic and copies ran while one was open for 4% -> 4% of each run, Pallas kernels for 33% -> 33%
where the time goes in v4:
time: 192 us; the launch traced here: 191 us
  Pallas kernels  109 us (57%)
  waiting for transfers between devices  38.6 us (20%)
  starting transfers between devices  25 us (13%)
  other arithmetic  10.3 us (5%)
  local copies, waits for them, and re-layouts  7.74 us (4%)
    pallas_call x10, Pallas kernels, call(): pl.pallas_call(kernel, grid_spec=pltpu.PrefetchScalarGridSpec(num_scalar_...  109 us
    ppermute x14, waiting for transfers between devices, exchange(): return lax.ppermute(value, axis, [(i, i ^ distance) for i in range(size)])  22 us
    ppermute x12, starting transfers between devices, send_all(): return lax.ppermute(value, ('dp', 'rows'), perm)  18.5 us
    ppermute x12, waiting for transfers between devices, send_all(): return lax.ppermute(value, ('dp', 'rows'), perm)  16.7 us
    ppermute x14, starting transfers between devices, exchange(): return lax.ppermute(value, axis, [(i, i ^ distance) for i in range(size)])  6.41 us
    unnamed x39, local copies, waits for them, and re-layouts  5.66 us
    convert_element_type x11, other arithmetic, add_low(): return total.astype(BF)  5.48 us
  transfers between devices with their start and end apart: 26, of which 15 were waited for; matrix products, arithmetic and copies ran while one was open for 4% of the time, Pallas kernels for 33%

profile of v4, /device:TPU:0, one launch (start us, length us, event | category | flops | bytes accessed | tf_op | source)
XLA Modules:
  0.0 191.2 jit_solution(6608874610407479380)
XLA Ops:
  0.7 1.1 pad_maximum_fusion.1
  1.8 0.5 collective-permute-start
  2.3 2.6 %collective-permute-start.1 = (bf16[512,512]{1,0:T(8,128)(2,1)S(1)}, bf16[512,512]{1,0:T(8,128)(2,1)S(1)}, u32[]{:S(2)}, u32[]{:S(2)}) collective-permute-start(bf16[512,512]{1,0:T(8,128)(2,1)S(1)} %bitcast.64), channel_id=1, source_target_pairs={{0,2},{1,3},{2,0},{3,1},{4,6},{5,7},{6,4},{7,5},{8,10},{9,11},{10,... | collective-permute-start | bytes 1572872 | tf_op jit(solution)/shard_map/ppermute | solution.py:374
  4.9 0.8 copy.63
  5.7 0.6 reshape.160.refs_2_
  6.3 0.7 stack.23.ids
  6.9 1.9 pad_maximum_fusion.2
  8.9 0.8 copy-done.13
  9.7 6.2 %front.1 = (bf16[512,512]{1,0:T(8,128)(2,1)}, bf16[4,512,512]{2,1,0:T(8,128)(2,1)}, bf16[4,512,512]{2,1,0:T(8,128)(2,1)}, bf16[4,512,512]{2,1,0:T(8,128)(2,1)}, bf16[4,512,512]{2,1,0:T(8,128)(2,1)}) custom-call(s32[5]{0:T(128)} %stack.23.ids, bf16[512,512]{1,0:T(8,128)(2,1)} %bitcast.65, bf16[512,512]{1,0:T(8,128)(2,1)} %copy-done.13, ...), custom_call_target="tpu_custom_call" | custom-call | bytes 3200000 | tf_op jit(solution)/shard_map/front/pallas_call | solution.py:533
  15.9 1.5 collective-permute-done.1.refs_4_
  17.4 1.9 collective-permute-done.2.refs_5_
  19.3 0.8 copy-done.12
  20.1 22.5 %attend.1 = (bf16[4,64,64,256]{3,2,1,0:T(8,128)(2,1)}, bf16[4,64,32,128]{3,2,1,0:T(8,128)(2,1)}, bf16[8,64,16,64]{3,2,1,0:T(8,128)(2,1)}, bf16[4,64,64,256]{3,2,...) custom-call(s32[5]{0:T(128)} %stack.23.ids, ...), custom_call_target="tpu_custom_call", output_to_operand_aliasing={{7}: (14, {}), {8}: (15, {}), {9}: (16, {}), {10}: (17, {})} | custom-call | bytes 14400000 | tf_op jit(solution)/shard_map/attend/pallas_call | solution.py:533
  42.7 19.2 %dense.1 = (bf16[4,64,512]{2,1,0:T(8,128)(2,1)}, bf16[4,32,512]{2,1,0:T(8,128)(2,1)}, bf16[4,32,512]{2,1,0:T(8,128)(2,1)}, f32[512,512]{1,0:T(8,128)}, bf16[512,...) custom-call(s32[5]{0:T(128)} %stack.23.ids, ...), custom_call_target="tpu_custom_call" | custom-call | bytes 12800000 | tf_op jit(solution)/shard_map/dense/pallas_call | solution.py:533
  62.0 2.9 %collective-permute-done.3 = bf16[1152,512]{1,0:T(8,128)(2,1)S(1)} collective-permute-done((bf16[1152,512]{1,0:T(8,128)(2,1)}, bf16[1152,512]{1,0:T(8,128)(2,1)S(1)}, u32[]{:S(2)}, u32[]{:S(2)}) %collective-permute-start.3) | collective-permute-done | bytes 1179680 | tf_op jit(solution)/shard_map/ppermute | solution.py:374
  64.9 1.6 add_convert_fusion
  66.5 1.8 collective-permute-start.5
  68.3 15.8 %attend_back_big.1 = (bf16[4,64,64,256]{3,2,1,0:T(8,128)(2,1)}, bf16[256,512]{1,0:T(8,128)(2,1)}, bf16[512,1024]{1,0:T(8,128)(2,1)}, bf16[512,1024]{1,0:T(8,128)(2,1)}) custom-call(s32[5]{0:T(128)} %stack.23.ids, bf16[512,512]{1,0:T(8,128)(2,1)} %get-tuple-element.100.refs_3_.refs_0_, bf16[512,512]{1,0:T(8,128)(2,1)} %get-tuple-element.125.refs_1_, ...), custom_call_target="tpu_custom_call" | custom-call | bytes 12000000 | tf_op jit(solution)/shard_map/attend_back_big/pallas_call | solution.py:533
  84.1 1.5 add_convert_fusion.4
  85.6 1.6 collective-permute-start.6
  87.2 15.2 %attend_back_rest.1 = (bf16[4,64,32,128]{3,2,1,0:T(8,128)(2,1)}, bf16[8,64,16,64]{3,2,1,0:T(8,128)(2,1)}, bf16[256,512]{1,0:T(8,128)(2,1)}, bf16[512,1024]{1,0:T(8,128)(2,1)}, bf16[512,1024]{1,0:T(8,128)(2,1)}) custom-call(s32[5]{0:T(128)} %stack.23.ids, bf16[512,512]{1,0:T(8,128)(2,1)} %get-tuple-element.100.refs_3_.refs_0_, ...), custom_call_target="tpu_custom_call" | custom-call | bytes 12000000 | tf_op jit(solution)/shard_map/attend_back_rest/pallas_call | solution.py:533
  102.4 1.5 add_convert_fusion.3
  104.0 1.6 collective-permute-start.7
  105.6 11.4 %back.1 = (f32[512,512]{1,0:T(8,128)}, bf16[512,512]{1,0:T(8,128)(2,1)}, bf16[2,512,512]{2,1,0:T(8,128)(2,1)}, bf16[784,512]{1,0:T(8,128)(2,1)}, bf16[784,512]{1,0:T(8,128)(2,1)}) custom-call(s32[5]{0:T(128)} %stack.23.ids, bf16[256,512]{1,0:T(8,128)(2,1)} %get-tuple-element.122.refs_0_, bf16[256,512]{1,0:T(8,128)(2,1)} %get-tuple-element.130.refs_1_, ...), custom_call_target="tpu_custom_call" | custom-call | bytes 7200000 | tf_op jit(solution)/shard_map/back/pallas_call | solution.py:533
  117.0 2.3 %collective-permute-done.7 = bf16[576,512]{1,0:T(8,128)(2,1)S(1)} collective-permute-done((bf16[576,512]{1,0:T(8,128)(2,1)S(1)}, bf16[576,512]{1,0:T(8,128)(2,1)S(1)}, u32[]{:S(2)}, u32[]{:S(2)}) %collective-permute-start.7) | collective-permute-done | bytes 589856 | tf_op jit(solution)/shard_map/ppermute | solution.py:397
  119.3 0.2 add_convert_fusion.2
  119.4 0.4 collective-permute-start.8
  119.8 0.2 collective-permute-start.10
  120.0 0.7 slice.74
  120.7 1.6 collective-permute-done.8.refs_4_
  122.5 1.0 collective-permute-done.10
  123.6 1.5 collective-permute-start.11
  125.2 2.1 %collective-permute-start.12 = (bf16[576,512]{1,0:T(8,128)(2,1)S(1)}, bf16[576,512]{1,0:T(8,128)(2,1)S(1)}, u32[]{:S(2)}, u32[]{:S(2)}) collective-permute-start(bf16[576,512]{1,0:T(8,128)(2,1)S(1)} %add_convert_fusion.2), channel_id=1, source_target_pairs={{0,16},{1,9},{2,18},{3,11},{4,20},{5,13},{6,22},{7,15},{8,24},{9,1... | collective-permute-start | bytes 1769480 | tf_op jit(solution)/shard_map/ppermute | solution.py:397
  127.3 1.4 collective-permute-start.9
  128.7 2.9 %collective-permute-done.11 = bf16[400,512]{1,0:T(8,128)(2,1)S(1)} collective-permute-done((bf16[400,512]{1,0:T(8,128)(2,1)S(1)}, bf16[400,512]{1,0:T(8,128)(2,1)S(1)}, u32[]{:S(2)}, u32[]{:S(2)}) %collective-permute-start.11) | collective-permute-done | bytes 409632 | tf_op jit(solution)/shard_map/ppermute | solution.py:397
  131.7 1.5 collective-permute-start.13
  133.2 8.9 %collective-permute-done.9.refs_5_ = bf16[512,512]{1,0:T(8,128)(2,1)S(1)} collective-permute-done((bf16[512,512]{1,0:T(8,128)(2,1)S(1)}, bf16[512,512]{1,0:T(8,128)(2,1)S(1)}, u32[]{:S(2)}, u32[]{:S(2)}) %collective-permute-start.9) | collective-permute-done | bytes 524320 | tf_op jit(solution)/shard_map/ppermute | solution.py:374
  142.1 2.3 %collective-permute-done.13 = bf16[208,512]{1,0:T(8,128)(2,1)S(1)} collective-permute-done((bf16[208,512]{1,0:T(8,128)(2,1)S(1)}, bf16[208,512]{1,0:T(8,128)(2,1)S(1)}, u32[]{:S(2)}, u32[]{:S(2)}) %collective-permute-start.13) | collective-permute-done | bytes 213024 | tf_op jit(solution)/shard_map/ppermute | solution.py:397
  144.6 0.2 add_convert_fusion.1.refs_0_
  144.8 1.3 collective-permute-start.16
  146.1 1.3 collective-permute-start.14
  147.4 4.3 %last.1 = (bf16[4,64,512]{2,1,0:T(8,128)(2,1)}, bf16[4,32,512]{2,1,0:T(8,128)(2,1)}, bf16[4,32,512]{2,1,0:T(8,128)(2,1)}) custom-call(s32[5]{0:T(128)} %stack.23.ids, bf16[512,512]{1,0:T(8,128)(2,1)} %bitcast.67, f32[512,512]{1,0:T(8,128)} %get-tuple-element.113.refs_1_, f32[1,512]{1,0:T(1,128)} %bitcast.84, f32[512,512]{1,0:T(8,128)} %get-tuple-element.138.refs_3_, ...), custom_call_target="tpu_custom_call" | custom-call | bytes 1600000 | tf_op jit(solution)/shard_map/last/pallas_call | solution.py:533
  151.8 1.1 collective-permute-done.14
  152.9 1.8 collective-permute-done.16.refs_1_
  154.8 1.4 collective-permute-start.21
  156.2 2.3 %collective-permute-start.15 = (bf16[208,512]{1,0:T(8,128)(2,1)S(1)}, bf16[208,512]{1,0:T(8,128)(2,1)S(1)}, u32[]{:S(2)}, u32[]{:S(2)}) collective-permute-start(bf16[208,512]{1,0:T(8,128)(2,1)S(1)} %add_convert_fusion.7), channel_id=1, source_target_pairs={{0,16},{1,9},{2,18},{3,11},{4,20},{5,13},{6,22},{7,15},{8,24},{9,1... | collective-permute-start | bytes 638984 | tf_op jit(solution)/shard_map/ppermute | solution.py:397
  158.5 0.5 collective-permute-start.19
  159.0 6.2 %collective-permute-done.15 = bf16[208,512]{1,0:T(8,128)(2,1)S(1)} collective-permute-done((bf16[208,512]{1,0:T(8,128)(2,1)S(1)}, bf16[208,512]{1,0:T(8,128)(2,1)S(1)}, u32[]{:S(2)}, u32[]{:S(2)}) %collective-permute-start.15) | collective-permute-done | bytes 213024 | tf_op jit(solution)/shard_map/ppermute | solution.py:397
  165.3 1.4 collective-permute-start.17
  166.7 0.8 copy-done.9
  167.5 4.9 %finish_ff_early.1 = (f32[4,128,2048]{2,1,0:T(8,128)}, f32[2,2,4,128,512]{4,3,2,1,0:T(8,128)}, f32[2,4,64,512]{3,2,1,0:T(8,128)}) custom-call(s32[5]{0:T(128)} %stack.23.ids, bf16[576,512]{1,0:T(8,128)(2,1)} %copy-done.1, bf16[576,512]{1,0:T(8,128)(2,1)} %copy-done.3, bf16[576,512]{1,0:T(8,128)(2,1)} %copy-done.9, ...), custom_call_target="tpu_custom_call" | custom-call | bytes 3200000 | tf_op jit(solution)/shard_map/finish_ff_early/pallas_call | solution.py:533
  172.4 1.7 pad_maximum_fusion.3
  174.1 0.7 collective-permute-start.20
  174.8 2.2 %collective-permute-done.22.refs_1_ = bf16[1152,512]{1,0:T(8,128)(2,1)S(1)} collective-permute-done((bf16[1152,512]{1,0:T(8,128)(2,1)S(1)}, bf16[1152,512]{1,0:T(8,128)(2,1)S(1)}, u32[]{:S(2)}, u32[]{:S(2)}) %collective-permute-start.22) | collective-permute-done | bytes 1179680 | tf_op jit(solution)/shard_map/ppermute | solution.py:374
  177.0 1.0 copy-done.7
  178.0 4.9 %finish_ff.1 = (f32[4,128,2048]{2,1,0:T(8,128)}, f32[2,2,4,128,512]{4,3,2,1,0:T(8,128)}, f32[2,4,64,512]{3,2,1,0:T(8,128)}) custom-call(s32[5]{0:T(128)} %stack.23.ids, bf16[1152,512]{1,0:T(8,128)(2,1)} %copy-done.6, bf16[1152,512]{1,0:T(8,128)(2,1)} %copy-done.7, ...), custom_call_target="tpu_custom_call", output_to_operand_aliasing={{0}: (3, {}), {1}: (4, {}), {2}: (5, {})} | custom-call | bytes 3200000 | tf_op jit(solution)/shard_map/finish_ff/pallas_call | solution.py:533
  182.9 0.2 collective-permute-start.25
  183.1 0.4 collective-permute-start.23
  183.7 1.7 collective-permute-done.23.refs_3_
  185.3 0.2 collective-permute-done.24.refs_4_
  185.5 0.5 copy-done.17
  186.0 0.2 copy-done.18
  186.2 0.8 copy-done.16
  186.9 4.3 %finish_rest.1 = (f32[512,512]{1,0:T(8,128)}, f32[512,512]{1,0:T(8,128)}, f32[512,512]{1,0:T(8,128)}, f32[512]{0:T(512)}, f32[512]{0:T(512)}, /*index=5*/f32[512]{0:T(512)}, f32[512]{0:T(512)}) custom-call(s32[5]{0:T(128)} %stack.23.ids, bf16[208,512]{1,0:T(8,128)(2,1)} %copy-done.5, bf16[192,512]{1,0:T(8,128)(2,1)} %collective-permute-done.17.refs_1_, ...), custom_call_target="tpu_custom_call" | custom-call | bytes 2400000 | tf_op jit(solution)/shard_map/finish_rest/pallas_call | solution.py:533
  (61 shorter events, 1.1 us)
Async XLA Ops:
  1.8 7.1 %copy-start = (bf16[4,128,512]{2,1,0:T(8,128)(2,1)}, bf16[4,128,512]{2,1,0:T(8,128)(2,1)S(1)}, u32[]{:S(2)}) copy-start(bf16[4,128,512]{2,1,0:T(8,128)(2,1)S(1)} %pad_maximum_fusion.1) | copy-start | bytes 1572868
  1.8 7.1 %collective-permute-start = (bf16[512,512]{1,0:T(8,128)(2,1)S(1)}, bf16[512,512]{1,0:T(8,128)(2,1)S(1)}, u32[]{:S(2)}, u32[]{:S(2)}) collective-permute-start(bf16[512,512]{1,0:T(8,128)(2,1)S(1)} %bitcast.63), channel_id=1, source_target_pairs={{0,1},{1,0},{2,3},{3,2},{4,5},{5,4},{6,7},{7,6},{8,9},{9,8},{10,11... | collective-permute-start | bytes 1572872 | tf_op jit(solution)/shard_map/ppermute | solution.py:374
  2.3 15.1 %collective-permute-start.1 = (bf16[512,512]{1,0:T(8,128)(2,1)S(1)}, bf16[512,512]{1,0:T(8,128)(2,1)S(1)}, u32[]{:S(2)}, u32[]{:S(2)}) collective-permute-start(bf16[512,512]{1,0:T(8,128)(2,1)S(1)} %bitcast.64), channel_id=1, source_target_pairs={{0,2},{1,3},{2,0},{3,1},{4,6},{5,7},{6,4},{7,5},{8,10},{9,11},{10,... | collective-permute-start | bytes 1572872 | tf_op jit(solution)/shard_map/ppermute | solution.py:374
  8.9 0.8 copy-start.13
  17.4 1.9 %copy-start.10 = (bf16[512,512]{1,0:T(8,128)(2,1)}, bf16[512,512]{1,0:T(8,128)(2,1)S(1)}, u32[]{:S(2)}) copy-start(bf16[512,512]{1,0:T(8,128)(2,1)S(1)} %collective-permute-done.1.refs_4_) | copy-start | bytes 1572868
  17.4 1.9 collective-permute-start.2
  19.3 0.8 copy-start.12
  61.8 3.1 %collective-permute-start.3 = (bf16[1152,512]{1,0:T(8,128)(2,1)}, bf16[1152,512]{1,0:T(8,128)(2,1)S(1)}, u32[]{:S(2)}, u32[]{:S(2)}) collective-permute-start(bf16[1152,512]{1,0:T(8,128)(2,1)} %get-tuple-element.116), channel_id=1, source_target_pairs={{0,1},{1,0},{2,3},{3,2},{4,5},{5,4},{6,7},{7,6},{8,9},{9,8},{10,11... | collective-permute-start | bytes 3538952 | tf_op jit(solution)/shard_map/ppermute | solution.py:374
  66.5 17.6 %collective-permute-start.5 = (bf16[1152,512]{1,0:T(8,128)(2,1)S(1)}, bf16[1152,512]{1,0:T(8,128)(2,1)}, u32[]{:S(2)}, u32[]{:S(2)}) collective-permute-start(bf16[1152,512]{1,0:T(8,128)(2,1)S(1)} %add_convert_fusion), channel_id=1, source_target_pairs={{0,4},{1,3},{2,6},{3,1},{4,0},{5,7},{6,2},{7,5},{8,12},{9,11},{10,... | collective-permute-start | bytes 3538952 | tf_op jit(solution)/shard_map/ppermute | solution.py:397
  68.3 15.8 %collective-permute-start.4 = (bf16[1152,512]{1,0:T(8,128)(2,1)}, bf16[1152,512]{1,0:T(8,128)(2,1)}, u32[]{:S(2)}, u32[]{:S(2)}) collective-permute-start(bf16[1152,512]{1,0:T(8,128)(2,1)} %get-tuple-element.123), channel_id=1, source_target_pairs={{0,1},{1,0},{2,3},{3,2},{4,5},{5,4},{6,7},{7,6},{8,9},{9,8},{10,11... | collective-permute-start | bytes 3538952 | tf_op jit(solution)/shard_map/ppermute | solution.py:374
  68.3 15.8 %copy-start.2 = (bf16[2304,512]{1,0:T(8,128)(2,1)S(1)}, bf16[2304,512]{1,0:T(8,128)(2,1)}, u32[]{:S(2)}) copy-start(bf16[2304,512]{1,0:T(8,128)(2,1)} %get-tuple-element.115) | copy-start | bytes 7077892
  85.6 16.8 %collective-permute-start.6 = (bf16[576,512]{1,0:T(8,128)(2,1)S(1)}, bf16[576,512]{1,0:T(8,128)(2,1)S(1)}, u32[]{:S(2)}, u32[]{:S(2)}) collective-permute-start(bf16[576,512]{1,0:T(8,128)(2,1)S(1)} %add_convert_fusion.4), channel_id=1, source_target_pairs={{0,2},{1,5},{2,0},{3,7},{4,6},{5,1},{6,4},{7,3},{8,10},{9,13},{10,... | collective-permute-start | bytes 1769480 | tf_op jit(solution)/shard_map/ppermute | solution.py:397
  104.0 15.3 %collective-permute-start.7 = (bf16[576,512]{1,0:T(8,128)(2,1)S(1)}, bf16[576,512]{1,0:T(8,128)(2,1)S(1)}, u32[]{:S(2)}, u32[]{:S(2)}) collective-permute-start(bf16[576,512]{1,0:T(8,128)(2,1)S(1)} %add_convert_fusion.3), channel_id=1, source_target_pairs={{0,8},{1,17},{2,10},{3,19},{4,12},{5,21},{6,14},{7,23},{8,0},{9,25... | collective-permute-start | bytes 1769480 | tf_op jit(solution)/shard_map/ppermute | solution.py:397
  117.0 5.4 %copy-start.11 = (bf16[512,512]{1,0:T(8,128)(2,1)S(1)}, bf16[512,512]{1,0:T(8,128)(2,1)}, u32[]{:S(2)}) copy-start(bf16[512,512]{1,0:T(8,128)(2,1)} %get-tuple-element.143) | copy-start | bytes 1572868
  117.0 6.5 %copy-start.8 = (bf16[784,512]{1,0:T(8,128)(2,1)S(1)}, bf16[784,512]{1,0:T(8,128)(2,1)}, u32[]{:S(2)}) copy-start(bf16[784,512]{1,0:T(8,128)(2,1)} %get-tuple-element.144) | copy-start | bytes 2408452
  119.4 2.9 %collective-permute-start.8 = (bf16[2,512,512]{2,1,0:T(8,128)(2,1)}, bf16[2,512,512]{2,1,0:T(8,128)(2,1)S(1)}, u32[]{:S(2)}, u32[]{:S(2)}) collective-permute-start(bf16[2,512,512]{2,1,0:T(8,128)(2,1)} %get-tuple-element.142), channel_id=1, source_target_pairs={{0,1},{1,0},{2,3},{3,2},{4,5},{5,4},{6,7},{7,6},{8,9},{9,8},{10,11... | collective-permute-start | bytes 3145736 | tf_op jit(solution)/shard_map/ppermute | solution.py:374
  119.8 3.7 %collective-permute-start.10 = (bf16[784,512]{1,0:T(8,128)(2,1)}, bf16[784,512]{1,0:T(8,128)(2,1)S(1)}, u32[]{:S(2)}, u32[]{:S(2)}) collective-permute-start(bf16[784,512]{1,0:T(8,128)(2,1)} %get-tuple-element.145), channel_id=1, source_target_pairs={{0,1},{1,0},{2,3},{3,2},{4,5},{5,4},{6,7},{7,6},{8,9},{9,8},{10,11... | collective-permute-start | bytes 2408456 | tf_op jit(solution)/shard_map/ppermute | solution.py:374
  122.4 6.3 %copy-start.4 = (bf16[2,512,512]{2,1,0:T(8,128)(2,1)}, bf16[2,512,512]{2,1,0:T(8,128)(2,1)S(1)}, u32[]{:S(2)}) copy-start(bf16[2,512,512]{2,1,0:T(8,128)(2,1)S(1)} %collective-permute-done.8.refs_4_) | copy-start | bytes 3145732
  123.6 8.0 %collective-permute-start.11 = (bf16[400,512]{1,0:T(8,128)(2,1)S(1)}, bf16[400,512]{1,0:T(8,128)(2,1)S(1)}, u32[]{:S(2)}, u32[]{:S(2)}) collective-permute-start(bf16[400,512]{1,0:T(8,128)(2,1)S(1)} %add_convert_fusion.5), channel_id=1, source_target_pairs={{0,4},{1,3},{2,6},{3,1},{4,0},{5,7},{6,2},{7,5},{8,12},{9,11},{10,... | collective-permute-start | bytes 1228808 | tf_op jit(solution)/shard_map/ppermute | solution.py:397
  125.2 19.4 %collective-permute-start.12 = (bf16[576,512]{1,0:T(8,128)(2,1)S(1)}, bf16[576,512]{1,0:T(8,128)(2,1)S(1)}, u32[]{:S(2)}, u32[]{:S(2)}) collective-permute-start(bf16[576,512]{1,0:T(8,128)(2,1)S(1)} %add_convert_fusion.2), channel_id=1, source_target_pairs={{0,16},{1,9},{2,18},{3,11},{4,20},{5,13},{6,22},{7,15},{8,24},{9,1... | collective-permute-start | bytes 1769480 | tf_op jit(solution)/shard_map/ppermute | solution.py:397
  127.3 14.9 %collective-permute-start.9 = (bf16[512,512]{1,0:T(8,128)(2,1)S(1)}, bf16[512,512]{1,0:T(8,128)(2,1)S(1)}, u32[]{:S(2)}, u32[]{:S(2)}) collective-permute-start(bf16[512,512]{1,0:T(8,128)(2,1)S(1)} %fusion), channel_id=1, source_target_pairs={{0,2},{1,3},{2,0},{3,1},{4,6},{5,7},{6,4},{7,5},{8,10},{9,11},{10,... | collective-permute-start | bytes 1572872 | tf_op jit(solution)/shard_map/ppermute | solution.py:374
  131.7 12.8 %collective-permute-start.13 = (bf16[208,512]{1,0:T(8,128)(2,1)S(1)}, bf16[208,512]{1,0:T(8,128)(2,1)S(1)}, u32[]{:S(2)}, u32[]{:S(2)}) collective-permute-start(bf16[208,512]{1,0:T(8,128)(2,1)S(1)} %add_convert_fusion.9), channel_id=1, source_target_pairs={{0,2},{1,5},{2,0},{3,7},{4,6},{5,1},{6,4},{7,3},{8,10},{9,13},{10,... | collective-permute-start | bytes 638984 | tf_op jit(solution)/shard_map/ppermute | solution.py:397
  142.1 5.3 %copy-start.14 = (bf16[512,512]{1,0:T(8,128)(2,1)}, bf16[512,512]{1,0:T(8,128)(2,1)S(1)}, u32[]{:S(2)}) copy-start(bf16[512,512]{1,0:T(8,128)(2,1)S(1)} %collective-permute-done.9.refs_5_) | copy-start | bytes 1572868
  144.8 13.7 %copy-start.1 = (bf16[576,512]{1,0:T(8,128)(2,1)}, bf16[576,512]{1,0:T(8,128)(2,1)S(1)}, u32[]{:S(2)}) copy-start(bf16[576,512]{1,0:T(8,128)(2,1)S(1)} %add_convert_fusion.1.refs_0_) | copy-start | bytes 1769476
  144.8 9.9 %collective-permute-start.16 = (bf16[576,512]{1,0:T(8,128)(2,1)S(1)}, bf16[576,512]{1,0:T(8,128)(2,1)S(1)}, u32[]{:S(2)}, u32[]{:S(2)}) collective-permute-start(bf16[576,512]{1,0:T(8,128)(2,1)S(1)} %add_convert_fusion.1.refs_0_), channel_id=1, source_target_pairs={{0,2},{1,5},{2,0},{3,7},{4,6},{5,1},{6,4},{7,3},{8,10},{9,13},{10,... | collective-permute-start | bytes 1769480 | tf_op jit(solution)/shard_map/ppermute | solution.py:397
  146.1 6.8 %collective-permute-start.14 = (bf16[208,512]{1,0:T(8,128)(2,1)S(1)}, bf16[208,512]{1,0:T(8,128)(2,1)S(1)}, u32[]{:S(2)}, u32[]{:S(2)}) collective-permute-start(bf16[208,512]{1,0:T(8,128)(2,1)S(1)} %add_convert_fusion.8), channel_id=1, source_target_pairs={{0,8},{1,17},{2,10},{3,19},{4,12},{5,21},{6,14},{7,23},{8,0},{9,25... | collective-permute-start | bytes 638984 | tf_op jit(solution)/shard_map/ppermute | solution.py:397
  154.7 12.8 %copy-start.3 = (bf16[576,512]{1,0:T(8,128)(2,1)}, bf16[576,512]{1,0:T(8,128)(2,1)S(1)}, u32[]{:S(2)}) copy-start(bf16[576,512]{1,0:T(8,128)(2,1)S(1)} %collective-permute-done.16.refs_1_) | copy-start | bytes 1769476
  154.8 19.3 %collective-permute-start.21 = (bf16[1152,512]{1,0:T(8,128)(2,1)S(1)}, bf16[1152,512]{1,0:T(8,128)(2,1)S(1)}, u32[]{:S(2)}, u32[]{:S(2)}) collective-permute-start(bf16[1152,512]{1,0:T(8,128)(2,1)S(1)} %pad_maximum_fusion), channel_id=1, source_target_pairs={{0,4},{1,3},{2,6},{3,1},{4,0},{5,7},{6,2},{7,5},{8,12},{9,11},{10,... | collective-permute-start | bytes 3538952 | tf_op jit(solution)/shard_map/ppermute | solution.py:397
  156.2 9.0 %collective-permute-start.15 = (bf16[208,512]{1,0:T(8,128)(2,1)S(1)}, bf16[208,512]{1,0:T(8,128)(2,1)S(1)}, u32[]{:S(2)}, u32[]{:S(2)}) collective-permute-start(bf16[208,512]{1,0:T(8,128)(2,1)S(1)} %add_convert_fusion.7), channel_id=1, source_target_pairs={{0,16},{1,9},{2,18},{3,11},{4,20},{5,13},{6,22},{7,15},{8,24},{9,1... | collective-permute-start | bytes 638984 | tf_op jit(solution)/shard_map/ppermute | solution.py:397
  158.5 8.2 %collective-permute-start.18 = (bf16[576,512]{1,0:T(8,128)(2,1)S(1)}, bf16[576,512]{1,0:T(8,128)(2,1)S(1)}, u32[]{:S(2)}, u32[]{:S(2)}) collective-permute-start(bf16[576,512]{1,0:T(8,128)(2,1)S(1)} %add_convert_fusion.1.refs_0_), channel_id=1, source_target_pairs={{0,1},{1,0},{2,3},{3,2},{4,5},{5,4},{6,7},{7,6},{8,9},{9,8},{10,11... | collective-permute-start | bytes 1769480 | tf_op jit(solution)/shard_map/ppermute | solution.py:374
  158.5 9.1 %collective-permute-start.19 = (bf16[576,512]{1,0:T(8,128)(2,1)S(1)}, bf16[576,512]{1,0:T(8,128)(2,1)}, u32[]{:S(2)}, u32[]{:S(2)}) collective-permute-start(bf16[576,512]{1,0:T(8,128)(2,1)S(1)} %collective-permute-done.16.refs_1_), channel_id=1, source_target_pairs={{0,1},{1,0},{2,3},{3,2},{4,5},{5,4},{6,7},{7,6},{8,9},{9,8},{10,11... | collective-permute-start | bytes 1769480 | tf_op jit(solution)/shard_map/ppermute | solution.py:374
  165.2 17.9 %copy-start.5 = (bf16[208,512]{1,0:T(8,128)(2,1)}, bf16[208,512]{1,0:T(8,128)(2,1)S(1)}, u32[]{:S(2)}) copy-start(bf16[208,512]{1,0:T(8,128)(2,1)S(1)} %add_convert_fusion.6.refs_0_) | copy-start | bytes 638980
  165.3 7.1 %collective-permute-start.17 = (bf16[192,512]{1,0:T(8,128)(2,1)S(1)}, bf16[192,512]{1,0:T(8,128)(2,1)}, u32[]{:S(2)}, u32[]{:S(2)}) collective-permute-start(bf16[192,512]{1,0:T(8,128)(2,1)S(1)} %slice.87), channel_id=1, source_target_pairs={{0,2},{1,5},{2,0},{3,7},{4,6},{5,1},{6,4},{7,3},{8,10},{9,13},{10,... | collective-permute-start | bytes 589832 | tf_op jit(solution)/shard_map/ppermute | solution.py:397
  166.7 0.8 copy-start.9
  174.1 2.9 %copy-start.6 = (bf16[1152,512]{1,0:T(8,128)(2,1)}, bf16[1152,512]{1,0:T(8,128)(2,1)S(1)}, u32[]{:S(2)}) copy-start(bf16[1152,512]{1,0:T(8,128)(2,1)S(1)} %collective-permute-done.21.refs_0_) | copy-start | bytes 3538948
  174.1 2.8 %collective-permute-start.22 = (bf16[1152,512]{1,0:T(8,128)(2,1)S(1)}, bf16[1152,512]{1,0:T(8,128)(2,1)S(1)}, u32[]{:S(2)}, u32[]{:S(2)}) collective-permute-start(bf16[1152,512]{1,0:T(8,128)(2,1)S(1)} %collective-permute-done.21.refs_0_), channel_id=1, source_target_pairs={{0,1},{1,0},{2,3},{3,2},{4,5},{5,4},{6,7},{7,6},{8,9},{9,8},{10,11... | collective-permute-start | bytes 3538952 | tf_op jit(solution)/shard_map/ppermute | solution.py:374
  174.1 8.8 %collective-permute-start.20 = (bf16[384,512]{1,0:T(8,128)(2,1)}, bf16[384,512]{1,0:T(8,128)(2,1)S(1)}, u32[]{:S(2)}, u32[]{:S(2)}) collective-permute-start(bf16[384,512]{1,0:T(8,128)(2,1)} %pad_maximum_fusion.3), channel_id=1, source_target_pairs={{0,4},{1,3},{2,6},{3,1},{4,0},{5,7},{6,2},{7,5},{8,12},{9,11},{10,... | collective-permute-start | bytes 1179656 | tf_op jit(solution)/shard_map/ppermute | solution.py:397
  177.0 1.0 copy-start.7
  182.9 2.6 %copy-start.15 = (bf16[384,512]{1,0:T(8,128)(2,1)}, bf16[384,512]{1,0:T(8,128)(2,1)S(1)}, u32[]{:S(2)}) copy-start(bf16[384,512]{1,0:T(8,128)(2,1)S(1)} %collective-permute-done.20.refs_2_) | copy-start | bytes 1179652
  182.9 2.6 %collective-permute-start.25 = (bf16[384,512]{1,0:T(8,128)(2,1)S(1)}, bf16[384,512]{1,0:T(8,128)(2,1)S(1)}, u32[]{:S(2)}, u32[]{:S(2)}) collective-permute-start(bf16[384,512]{1,0:T(8,128)(2,1)S(1)} %collective-permute-done.20.refs_2_), channel_id=1, source_target_pairs={{0,1},{1,0},{2,3},{3,2},{4,5},{5,4},{6,7},{7,6},{8,9},{9,8},{10,11... | collective-permute-start | bytes 1179656 | tf_op jit(solution)/shard_map/ppermute | solution.py:374
  183.1 2.2 %collective-permute-start.23 = (bf16[208,512]{1,0:T(8,128)(2,1)S(1)}, bf16[208,512]{1,0:T(8,128)(2,1)S(1)}, u32[]{:S(2)}, u32[]{:S(2)}) collective-permute-start(bf16[208,512]{1,0:T(8,128)(2,1)S(1)} %add_convert_fusion.6.refs_0_), channel_id=1, source_target_pairs={{0,1},{1,0},{2,3},{3,2},{4,5},{5,4},{6,7},{7,6},{8,9},{9,8},{10,11... | collective-permute-start | bytes 638984 | tf_op jit(solution)/shard_map/ppermute | solution.py:374
  183.5 2.0 %collective-permute-start.24 = (bf16[192,512]{1,0:T(8,128)(2,1)}, bf16[192,512]{1,0:T(8,128)(2,1)S(1)}, u32[]{:S(2)}, u32[]{:S(2)}) collective-permute-start(bf16[192,512]{1,0:T(8,128)(2,1)} %collective-permute-done.17.refs_1_), channel_id=1, source_target_pairs={{0,1},{1,0},{2,3},{3,2},{4,5},{5,4},{6,7},{7,6},{8,9},{9,8},{10,11... | collective-permute-start | bytes 589832 | tf_op jit(solution)/shard_map/ppermute | solution.py:374
  185.3 0.7 copy-start.17
  185.5 0.7 copy-start.18
  186.2 0.8 copy-start.16

commit v5 on v4

--- a/solution.py
+++ b/solution.py
@@ -770,9 +770,9 @@
     w = w_sum.step(after(w, far))
     far = far_rows(far)
     w = w_sum.step(w)
-    far = after(far, w_sum.operand)
+    moving = ff.step(after(moving, w_sum.operand))
+    far = after(far, ff.operand)
     w = w_sum.step(after(w, far))
-    moving = ff.step(after(moving, w_sum.operand))
     last_args = [x, dh, gain_one, own, near_da, after(far, ff.operand)]
     grad_atoms = call(
         lambda ids, *refs: last_kernel(1, *refs),

time: 192 us -> 189 us (0.984)
    ppermute x14, waiting for transfers between devices: 22 us -> 12.7 us  [exchange(): return lax.ppermute(value, axis, [(i, i ^ distance) for i in range(size)])]
    ppermute x12, waiting for transfers between devices: 16.7 us -> 25.1 us  [send_all(): return lax.ppermute(value, ('dp', 'rows'), perm)]
  transfers between devices with their start and end apart: 26 -> 26, of which waited for: 15 -> 15; matrix products, arithmetic and copies ran while one was open for 4% -> 3% of each run, Pallas kernels for 33% -> 33%
where the time goes in v5:
time: 189 us
  Pallas kernels  109 us (58%)
  waiting for transfers between devices  37.8 us (20%)
  starting transfers between devices  23.8 us (13%)
  other arithmetic  10.3 us (5%)
  local copies, waits for them, and re-layouts  7.03 us (4%)
    pallas_call x10, Pallas kernels, call(): pl.pallas_call(kernel, grid_spec=pltpu.PrefetchScalarGridSpec(num_scalar_...  109 us
    ppermute x12, waiting for transfers between devices, send_all(): return lax.ppermute(value, ('dp', 'rows'), perm)  25.1 us
    ppermute x12, starting transfers between devices, send_all(): return lax.ppermute(value, ('dp', 'rows'), perm)  17.3 us
    ppermute x14, waiting for transfers between devices, exchange(): return lax.ppermute(value, axis, [(i, i ^ distance) for i in range(size)])  12.7 us
    ppermute x14, starting transfers between devices, exchange(): return lax.ppermute(value, axis, [(i, i ^ distance) for i in range(size)])  6.46 us
    unnamed x39, local copies, waits for them, and re-layouts  5.66 us
    convert_element_type x11, other arithmetic, add_low(): return total.astype(BF)  5.48 us
  transfers between devices with their start and end apart: 26, of which 15 were waited for; matrix products, arithmetic and copies ran while one was open for 3% of the time, Pallas kernels for 33%

profile of v5, /device:TPU:0, one launch (start us, length us, event | category | flops | bytes accessed | tf_op | source)
XLA Modules:
  0.0 188.5 jit_solution(12875666425089247094)
XLA Ops:
  0.7 1.1 pad_maximum_fusion.1
  1.8 0.5 collective-permute-start
  2.3 2.6 %collective-permute-start.1 = (bf16[512,512]{1,0:T(8,128)(2,1)S(1)}, bf16[512,512]{1,0:T(8,128)(2,1)S(1)}, u32[]{:S(2)}, u32[]{:S(2)}) collective-permute-start(bf16[512,512]{1,0:T(8,128)(2,1)S(1)} %bitcast.64), channel_id=1, source_target_pairs={{0,2},{1,3},{2,0},{3,1},{4,6},{5,7},{6,4},{7,5},{8,10},{9,11},{10,... | collective-permute-start | bytes 1572872 | tf_op jit(solution)/shard_map/ppermute | solution.py:374
  4.9 0.8 copy.63
  5.7 0.6 reshape.160.refs_2_
  6.3 0.7 stack.23.ids
  6.9 1.9 %pad_maximum_fusion.2 = bf16[4,128,512]{2,1,0:T(8,128)(2,1)} fusion(bf16[4,32,512]{2,1,0:T(8,128)(2,1)} %bitcast.80, bf16[4,32,512]{2,1,0:T(8,128)(2,1)} %bitcast.81, bf16[4,64,512]{2,1,0:T(8,128)(2,1)} %bitcast.77), kind=kLoop, calls=%fused_computation.11 | loop fusion | flops 1572864 | bytes 1048576 | tf_op jit(solution)/shard_map/concatenate | solution.py:511
  8.9 0.8 copy-done.13
  9.7 6.2 %front.1 = (bf16[512,512]{1,0:T(8,128)(2,1)}, bf16[4,512,512]{2,1,0:T(8,128)(2,1)}, bf16[4,512,512]{2,1,0:T(8,128)(2,1)}, bf16[4,512,512]{2,1,0:T(8,128)(2,1)}, bf16[4,512,512]{2,1,0:T(8,128)(2,1)}) custom-call(s32[5]{0:T(128)} %stack.23.ids, bf16[512,512]{1,0:T(8,128)(2,1)} %bitcast.65, bf16[512,512]{1,0:T(8,128)(2,1)} %copy-done.13, ...), custom_call_target="tpu_custom_call" | custom-call | bytes 3200000 | tf_op jit(solution)/shard_map/front/pallas_call | solution.py:533
  15.9 1.5 collective-permute-done.1.refs_4_
  17.4 1.9 %collective-permute-done.2.refs_5_ = bf16[512,512]{1,0:T(8,128)(2,1)S(1)} collective-permute-done((bf16[512,512]{1,0:T(8,128)(2,1)S(1)}, bf16[512,512]{1,0:T(8,128)(2,1)S(1)}, u32[]{:S(2)}, u32[]{:S(2)}) %collective-permute-start.2) | collective-permute-done | bytes 524320 | tf_op jit(solution)/shard_map/ppermute | solution.py:374
  19.3 0.8 copy-done.12
  20.1 22.5 %attend.1 = (bf16[4,64,64,256]{3,2,1,0:T(8,128)(2,1)}, bf16[4,64,32,128]{3,2,1,0:T(8,128)(2,1)}, bf16[8,64,16,64]{3,2,1,0:T(8,128)(2,1)}, bf16[4,64,64,256]{3,2,...) custom-call(s32[5]{0:T(128)} %stack.23.ids, ...), custom_call_target="tpu_custom_call", output_to_operand_aliasing={{7}: (14, {}), {8}: (15, {}), {9}: (16, {}), {10}: (17, {})} | custom-call | bytes 14400000 | tf_op jit(solution)/shard_map/attend/pallas_call | solution.py:533
  42.7 19.2 %dense.1 = (bf16[4,64,512]{2,1,0:T(8,128)(2,1)}, bf16[4,32,512]{2,1,0:T(8,128)(2,1)}, bf16[4,32,512]{2,1,0:T(8,128)(2,1)}, f32[512,512]{1,0:T(8,128)}, bf16[512,...) custom-call(s32[5]{0:T(128)} %stack.23.ids, ...), custom_call_target="tpu_custom_call" | custom-call | bytes 12800000 | tf_op jit(solution)/shard_map/dense/pallas_call | solution.py:533
  61.8 0.1 collective-permute-start.3
  62.0 2.9 %collective-permute-done.3 = bf16[1152,512]{1,0:T(8,128)(2,1)S(1)} collective-permute-done((bf16[1152,512]{1,0:T(8,128)(2,1)}, bf16[1152,512]{1,0:T(8,128)(2,1)S(1)}, u32[]{:S(2)}, u32[]{:S(2)}) %collective-permute-start.3) | collective-permute-done | bytes 1179680 | tf_op jit(solution)/shard_map/ppermute | solution.py:374
  64.9 1.6 add_convert_fusion
  66.5 1.8 collective-permute-start.5
  68.3 15.8 %attend_back_big.1 = (bf16[4,64,64,256]{3,2,1,0:T(8,128)(2,1)}, bf16[256,512]{1,0:T(8,128)(2,1)}, bf16[512,1024]{1,0:T(8,128)(2,1)}, bf16[512,1024]{1,0:T(8,128)(2,1)}) custom-call(s32[5]{0:T(128)} %stack.23.ids, bf16[512,512]{1,0:T(8,128)(2,1)} %get-tuple-element.100.refs_3_.refs_0_, bf16[512,512]{1,0:T(8,128)(2,1)} %get-tuple-element.125.refs_1_, ...), custom_call_target="tpu_custom_call" | custom-call | bytes 12000000 | tf_op jit(solution)/shard_map/attend_back_big/pallas_call | solution.py:533
  84.1 1.5 add_convert_fusion.4
  85.6 1.6 collective-permute-start.6
  87.2 15.2 %attend_back_rest.1 = (bf16[4,64,32,128]{3,2,1,0:T(8,128)(2,1)}, bf16[8,64,16,64]{3,2,1,0:T(8,128)(2,1)}, bf16[256,512]{1,0:T(8,128)(2,1)}, bf16[512,1024]{1,0:T(8,128)(2,1)}, bf16[512,1024]{1,0:T(8,128)(2,1)}) custom-call(s32[5]{0:T(128)} %stack.23.ids, bf16[512,512]{1,0:T(8,128)(2,1)} %get-tuple-element.100.refs_3_.refs_0_, ...), custom_call_target="tpu_custom_call" | custom-call | bytes 12000000 | tf_op jit(solution)/shard_map/attend_back_rest/pallas_call | solution.py:533
  102.4 1.5 add_convert_fusion.3
  104.0 1.6 collective-permute-start.7
  105.6 11.4 %back.1 = (f32[512,512]{1,0:T(8,128)}, bf16[512,512]{1,0:T(8,128)(2,1)}, bf16[2,512,512]{2,1,0:T(8,128)(2,1)}, bf16[784,512]{1,0:T(8,128)(2,1)}, bf16[784,512]{1,0:T(8,128)(2,1)}) custom-call(s32[5]{0:T(128)} %stack.23.ids, bf16[256,512]{1,0:T(8,128)(2,1)} %get-tuple-element.122.refs_0_, bf16[256,512]{1,0:T(8,128)(2,1)} %get-tuple-element.130.refs_1_, ...), custom_call_target="tpu_custom_call" | custom-call | bytes 7200000 | tf_op jit(solution)/shard_map/back/pallas_call | solution.py:533
  117.0 2.3 %collective-permute-done.7 = bf16[576,512]{1,0:T(8,128)(2,1)S(1)} collective-permute-done((bf16[576,512]{1,0:T(8,128)(2,1)S(1)}, bf16[576,512]{1,0:T(8,128)(2,1)S(1)}, u32[]{:S(2)}, u32[]{:S(2)}) %collective-permute-start.7) | collective-permute-done | bytes 589856 | tf_op jit(solution)/shard_map/ppermute | solution.py:397
  119.3 0.2 add_convert_fusion.2
  119.4 0.4 collective-permute-start.8
  119.8 0.2 collective-permute-start.11
  120.0 2.5 %collective-permute-start.10 = (bf16[576,512]{1,0:T(8,128)(2,1)S(1)}, bf16[576,512]{1,0:T(8,128)(2,1)S(1)}, u32[]{:S(2)}, u32[]{:S(2)}) collective-permute-start(bf16[576,512]{1,0:T(8,128)(2,1)S(1)} %add_convert_fusion.2), channel_id=1, source_target_pairs={{0,16},{1,9},{2,18},{3,11},{4,20},{5,13},{6,22},{7,15},{8,24},{9,1... | collective-permute-start | bytes 1769480 | tf_op jit(solution)/shard_map/ppermute | solution.py:397
  122.5 0.1 fusion
  122.7 0.8 collective-permute-done.11
  123.6 1.5 collective-permute-start.12
  125.2 1.4 collective-permute-start.9
  126.6 5.0 %collective-permute-done.12 = bf16[400,512]{1,0:T(8,128)(2,1)S(1)} collective-permute-done((bf16[400,512]{1,0:T(8,128)(2,1)S(1)}, bf16[400,512]{1,0:T(8,128)(2,1)S(1)}, u32[]{:S(2)}, u32[]{:S(2)}) %collective-permute-start.12) | collective-permute-done | bytes 409632 | tf_op jit(solution)/shard_map/ppermute | solution.py:397
  131.7 3.9 %collective-permute-done.10 = bf16[576,512]{1,0:T(8,128)(2,1)S(1)} collective-permute-done((bf16[576,512]{1,0:T(8,128)(2,1)S(1)}, bf16[576,512]{1,0:T(8,128)(2,1)S(1)}, u32[]{:S(2)}, u32[]{:S(2)}) %collective-permute-start.10) | collective-permute-done | bytes 589856 | tf_op jit(solution)/shard_map/ppermute | solution.py:397
  135.6 2.1 %collective-permute-start.13 = (bf16[208,512]{1,0:T(8,128)(2,1)S(1)}, bf16[208,512]{1,0:T(8,128)(2,1)S(1)}, u32[]{:S(2)}, u32[]{:S(2)}) collective-permute-start(bf16[208,512]{1,0:T(8,128)(2,1)S(1)} %add_convert_fusion.9), channel_id=1, source_target_pairs={{0,2},{1,5},{2,0},{3,7},{4,6},{5,1},{6,4},{7,3},{8,10},{9,13},{10,... | collective-permute-start | bytes 638984 | tf_op jit(solution)/shard_map/ppermute | solution.py:397
  137.7 0.2 add_convert_fusion.1.refs_0_
  138.0 2.1 %collective-permute-done.9.refs_5_ = bf16[512,512]{1,0:T(8,128)(2,1)S(1)} collective-permute-done((bf16[512,512]{1,0:T(8,128)(2,1)S(1)}, bf16[512,512]{1,0:T(8,128)(2,1)S(1)}, u32[]{:S(2)}, u32[]{:S(2)}) %collective-permute-start.9) | collective-permute-done | bytes 524320 | tf_op jit(solution)/shard_map/ppermute | solution.py:374
  140.1 4.4 %collective-permute-done.13 = bf16[208,512]{1,0:T(8,128)(2,1)S(1)} collective-permute-done((bf16[208,512]{1,0:T(8,128)(2,1)S(1)}, bf16[208,512]{1,0:T(8,128)(2,1)S(1)}, u32[]{:S(2)}, u32[]{:S(2)}) %collective-permute-start.13) | collective-permute-done | bytes 213024 | tf_op jit(solution)/shard_map/ppermute | solution.py:397
  144.6 2.1 %collective-permute-start.14 = (bf16[208,512]{1,0:T(8,128)(2,1)S(1)}, bf16[208,512]{1,0:T(8,128)(2,1)S(1)}, u32[]{:S(2)}, u32[]{:S(2)}) collective-permute-start(bf16[208,512]{1,0:T(8,128)(2,1)S(1)} %add_convert_fusion.8), channel_id=1, source_target_pairs={{0,8},{1,17},{2,10},{3,19},{4,12},{5,21},{6,14},{7,23},{8,0},{9,25... | collective-permute-start | bytes 638984 | tf_op jit(solution)/shard_map/ppermute | solution.py:397
  146.7 4.3 %last.1 = (bf16[4,64,512]{2,1,0:T(8,128)(2,1)}, bf16[4,32,512]{2,1,0:T(8,128)(2,1)}, bf16[4,32,512]{2,1,0:T(8,128)(2,1)}) custom-call(s32[5]{0:T(128)} %stack.23.ids, bf16[512,512]{1,0:T(8,128)(2,1)} %bitcast.67, f32[512,512]{1,0:T(8,128)} %get-tuple-element.113.refs_1_, f32[1,512]{1,0:T(1,128)} %bitcast.84, f32[512,512]{1,0:T(8,128)} %get-tuple-element.138.refs_3_, ...), custom_call_target="tpu_custom_call" | custom-call | bytes 1600000 | tf_op jit(solution)/shard_map/last/pallas_call | solution.py:533
  151.0 1.7 collective-permute-done.14
  152.8 1.2 collective-permute-start.21
  154.0 1.4 collective-permute-start.15
  155.4 0.5 collective-permute-start.19
  156.0 7.1 %collective-permute-done.15 = bf16[208,512]{1,0:T(8,128)(2,1)S(1)} collective-permute-done((bf16[208,512]{1,0:T(8,128)(2,1)S(1)}, bf16[208,512]{1,0:T(8,128)(2,1)S(1)}, u32[]{:S(2)}, u32[]{:S(2)}) %collective-permute-start.15) | collective-permute-done | bytes 213024 | tf_op jit(solution)/shard_map/ppermute | solution.py:397
  163.3 0.8 copy-done.9
  164.1 4.9 %finish_ff_early.1 = (f32[4,128,2048]{2,1,0:T(8,128)}, f32[2,2,4,128,512]{4,3,2,1,0:T(8,128)}, f32[2,4,64,512]{3,2,1,0:T(8,128)}) custom-call(s32[5]{0:T(128)} %stack.23.ids, bf16[576,512]{1,0:T(8,128)(2,1)} %copy-done.1, bf16[576,512]{1,0:T(8,128)(2,1)} %copy-done.3, bf16[576,512]{1,0:T(8,128)(2,1)} %copy-done.9, ...), custom_call_target="tpu_custom_call" | custom-call | bytes 3200000 | tf_op jit(solution)/shard_map/finish_ff_early/pallas_call | solution.py:533
  169.0 0.8 collective-permute-done.17.refs_1_
  169.7 1.7 pad_maximum_fusion.3
  171.4 1.3 collective-permute-start.20
  172.7 1.6 collective-permute-done.22.refs_1_
  174.3 1.0 copy-done.7
  175.3 4.9 %finish_ff.1 = (f32[4,128,2048]{2,1,0:T(8,128)}, f32[2,2,4,128,512]{4,3,2,1,0:T(8,128)}, f32[2,4,64,512]{3,2,1,0:T(8,128)}) custom-call(s32[5]{0:T(128)} %stack.23.ids, bf16[1152,512]{1,0:T(8,128)(2,1)} %copy-done.6, bf16[1152,512]{1,0:T(8,128)(2,1)} %copy-done.7, ...), custom_call_target="tpu_custom_call", output_to_operand_aliasing={{0}: (3, {}), {1}: (4, {}), {2}: (5, {})} | custom-call | bytes 3200000 | tf_op jit(solution)/shard_map/finish_ff/pallas_call | solution.py:533
  180.2 0.2 collective-permute-start.25
  180.4 0.4 collective-permute-start.23
  180.8 0.1 collective-permute-start.24
  181.0 1.7 collective-permute-done.23.refs_3_
  182.6 0.2 collective-permute-done.24.refs_4_
  182.8 0.5 copy-done.17
  183.3 0.2 copy-done.18
  183.5 0.8 copy-done.16
  184.2 4.3 %finish_rest.1 = (f32[512,512]{1,0:T(8,128)}, f32[512,512]{1,0:T(8,128)}, f32[512,512]{1,0:T(8,128)}, f32[512]{0:T(512)}, f32[512]{0:T(512)}, /*index=5*/f32[512]{0:T(512)}, f32[512]{0:T(512)}) custom-call(s32[5]{0:T(128)} %stack.23.ids, bf16[208,512]{1,0:T(8,128)(2,1)} %copy-done.5, bf16[192,512]{1,0:T(8,128)(2,1)} %collective-permute-done.17.refs_1_, ...), custom_call_target="tpu_custom_call" | custom-call | bytes 2400000 | tf_op jit(solution)/shard_map/finish_rest/pallas_call | solution.py:533
  (61 shorter events, 0.8 us)
Async XLA Ops:
  1.8 7.1 %copy-start = (bf16[4,128,512]{2,1,0:T(8,128)(2,1)}, bf16[4,128,512]{2,1,0:T(8,128)(2,1)S(1)}, u32[]{:S(2)}) copy-start(bf16[4,128,512]{2,1,0:T(8,128)(2,1)S(1)} %pad_maximum_fusion.1) | copy-start | bytes 1572868
  1.8 7.1 %collective-permute-start = (bf16[512,512]{1,0:T(8,128)(2,1)S(1)}, bf16[512,512]{1,0:T(8,128)(2,1)S(1)}, u32[]{:S(2)}, u32[]{:S(2)}) collective-permute-start(bf16[512,512]{1,0:T(8,128)(2,1)S(1)} %bitcast.63), channel_id=1, source_target_pairs={{0,1},{1,0},{2,3},{3,2},{4,5},{5,4},{6,7},{7,6},{8,9},{9,8},{10,11... | collective-permute-start | bytes 1572872 | tf_op jit(solution)/shard_map/ppermute | solution.py:374
  2.3 15.1 %collective-permute-start.1 = (bf16[512,512]{1,0:T(8,128)(2,1)S(1)}, bf16[512,512]{1,0:T(8,128)(2,1)S(1)}, u32[]{:S(2)}, u32[]{:S(2)}) collective-permute-start(bf16[512,512]{1,0:T(8,128)(2,1)S(1)} %bitcast.64), channel_id=1, source_target_pairs={{0,2},{1,3},{2,0},{3,1},{4,6},{5,7},{6,4},{7,5},{8,10},{9,11},{10,... | collective-permute-start | bytes 1572872 | tf_op jit(solution)/shard_map/ppermute | solution.py:374
  8.9 0.8 copy-start.13
  17.4 1.9 %copy-start.10 = (bf16[512,512]{1,0:T(8,128)(2,1)}, bf16[512,512]{1,0:T(8,128)(2,1)S(1)}, u32[]{:S(2)}) copy-start(bf16[512,512]{1,0:T(8,128)(2,1)S(1)} %collective-permute-done.1.refs_4_) | copy-start | bytes 1572868
  17.4 1.9 %collective-permute-start.2 = (bf16[512,512]{1,0:T(8,128)(2,1)S(1)}, bf16[512,512]{1,0:T(8,128)(2,1)S(1)}, u32[]{:S(2)}, u32[]{:S(2)}) collective-permute-start(bf16[512,512]{1,0:T(8,128)(2,1)S(1)} %collective-permute-done.1.refs_4_), channel_id=1, source_target_pairs={{0,1},{1,0},{2,3},{3,2},{4,5},{5,4},{6,7},{7,6},{8,9},{9,8},{10,11... | collective-permute-start | bytes 1572872 | tf_op jit(solution)/shard_map/ppermute | solution.py:374
  19.3 0.8 copy-start.12
  61.8 3.1 %collective-permute-start.3 = (bf16[1152,512]{1,0:T(8,128)(2,1)}, bf16[1152,512]{1,0:T(8,128)(2,1)S(1)}, u32[]{:S(2)}, u32[]{:S(2)}) collective-permute-start(bf16[1152,512]{1,0:T(8,128)(2,1)} %get-tuple-element.116), channel_id=1, source_target_pairs={{0,1},{1,0},{2,3},{3,2},{4,5},{5,4},{6,7},{7,6},{8,9},{9,8},{10,11... | collective-permute-start | bytes 3538952 | tf_op jit(solution)/shard_map/ppermute | solution.py:374
  66.5 17.6 %collective-permute-start.5 = (bf16[1152,512]{1,0:T(8,128)(2,1)S(1)}, bf16[1152,512]{1,0:T(8,128)(2,1)}, u32[]{:S(2)}, u32[]{:S(2)}) collective-permute-start(bf16[1152,512]{1,0:T(8,128)(2,1)S(1)} %add_convert_fusion), channel_id=1, source_target_pairs={{0,4},{1,3},{2,6},{3,1},{4,0},{5,7},{6,2},{7,5},{8,12},{9,11},{10,... | collective-permute-start | bytes 3538952 | tf_op jit(solution)/shard_map/ppermute | solution.py:397
  68.3 15.8 %collective-permute-start.4 = (bf16[1152,512]{1,0:T(8,128)(2,1)}, bf16[1152,512]{1,0:T(8,128)(2,1)}, u32[]{:S(2)}, u32[]{:S(2)}) collective-permute-start(bf16[1152,512]{1,0:T(8,128)(2,1)} %get-tuple-element.123), channel_id=1, source_target_pairs={{0,1},{1,0},{2,3},{3,2},{4,5},{5,4},{6,7},{7,6},{8,9},{9,8},{10,11... | collective-permute-start | bytes 3538952 | tf_op jit(solution)/shard_map/ppermute | solution.py:374
  68.3 15.8 %copy-start.2 = (bf16[2304,512]{1,0:T(8,128)(2,1)S(1)}, bf16[2304,512]{1,0:T(8,128)(2,1)}, u32[]{:S(2)}) copy-start(bf16[2304,512]{1,0:T(8,128)(2,1)} %get-tuple-element.115) | copy-start | bytes 7077892
  85.6 16.8 %collective-permute-start.6 = (bf16[576,512]{1,0:T(8,128)(2,1)S(1)}, bf16[576,512]{1,0:T(8,128)(2,1)S(1)}, u32[]{:S(2)}, u32[]{:S(2)}) collective-permute-start(bf16[576,512]{1,0:T(8,128)(2,1)S(1)} %add_convert_fusion.4), channel_id=1, source_target_pairs={{0,2},{1,5},{2,0},{3,7},{4,6},{5,1},{6,4},{7,3},{8,10},{9,13},{10,... | collective-permute-start | bytes 1769480 | tf_op jit(solution)/shard_map/ppermute | solution.py:397
  104.0 15.3 %collective-permute-start.7 = (bf16[576,512]{1,0:T(8,128)(2,1)S(1)}, bf16[576,512]{1,0:T(8,128)(2,1)S(1)}, u32[]{:S(2)}, u32[]{:S(2)}) collective-permute-start(bf16[576,512]{1,0:T(8,128)(2,1)S(1)} %add_convert_fusion.3), channel_id=1, source_target_pairs={{0,8},{1,17},{2,10},{3,19},{4,12},{5,21},{6,14},{7,23},{8,0},{9,25... | collective-permute-start | bytes 1769480 | tf_op jit(solution)/shard_map/ppermute | solution.py:397
  117.0 5.5 %copy-start.11 = (bf16[512,512]{1,0:T(8,128)(2,1)S(1)}, bf16[512,512]{1,0:T(8,128)(2,1)}, u32[]{:S(2)}) copy-start(bf16[512,512]{1,0:T(8,128)(2,1)} %get-tuple-element.143) | copy-start | bytes 1572868
  117.0 6.5 %copy-start.8 = (bf16[784,512]{1,0:T(8,128)(2,1)S(1)}, bf16[784,512]{1,0:T(8,128)(2,1)}, u32[]{:S(2)}) copy-start(bf16[784,512]{1,0:T(8,128)(2,1)} %get-tuple-element.144) | copy-start | bytes 2408452
  119.4 3.1 %collective-permute-start.8 = (bf16[2,512,512]{2,1,0:T(8,128)(2,1)}, bf16[2,512,512]{2,1,0:T(8,128)(2,1)S(1)}, u32[]{:S(2)}, u32[]{:S(2)}) collective-permute-start(bf16[2,512,512]{2,1,0:T(8,128)(2,1)} %get-tuple-element.142), channel_id=1, source_target_pairs={{0,1},{1,0},{2,3},{3,2},{4,5},{5,4},{6,7},{7,6},{8,9},{9,8},{10,11... | collective-permute-start | bytes 3145736 | tf_op jit(solution)/shard_map/ppermute | solution.py:374
  119.8 3.7 %collective-permute-start.11 = (bf16[784,512]{1,0:T(8,128)(2,1)}, bf16[784,512]{1,0:T(8,128)(2,1)S(1)}, u32[]{:S(2)}, u32[]{:S(2)}) collective-permute-start(bf16[784,512]{1,0:T(8,128)(2,1)} %get-tuple-element.145), channel_id=1, source_target_pairs={{0,1},{1,0},{2,3},{3,2},{4,5},{5,4},{6,7},{7,6},{8,9},{9,8},{10,11... | collective-permute-start | bytes 2408456 | tf_op jit(solution)/shard_map/ppermute | solution.py:374
  120.0 15.6 %collective-permute-start.10 = (bf16[576,512]{1,0:T(8,128)(2,1)S(1)}, bf16[576,512]{1,0:T(8,128)(2,1)S(1)}, u32[]{:S(2)}, u32[]{:S(2)}) collective-permute-start(bf16[576,512]{1,0:T(8,128)(2,1)S(1)} %add_convert_fusion.2), channel_id=1, source_target_pairs={{0,16},{1,9},{2,18},{3,11},{4,20},{5,13},{6,22},{7,15},{8,24},{9,1... | collective-permute-start | bytes 1769480 | tf_op jit(solution)/shard_map/ppermute | solution.py:397
  122.5 4.1 %copy-start.4 = (bf16[2,512,512]{2,1,0:T(8,128)(2,1)}, bf16[2,512,512]{2,1,0:T(8,128)(2,1)S(1)}, u32[]{:S(2)}) copy-start(bf16[2,512,512]{2,1,0:T(8,128)(2,1)S(1)} %collective-permute-done.8.refs_4_) | copy-start | bytes 3145732
  123.6 8.0 %collective-permute-start.12 = (bf16[400,512]{1,0:T(8,128)(2,1)S(1)}, bf16[400,512]{1,0:T(8,128)(2,1)S(1)}, u32[]{:S(2)}, u32[]{:S(2)}) collective-permute-start(bf16[400,512]{1,0:T(8,128)(2,1)S(1)} %add_convert_fusion.5), channel_id=1, source_target_pairs={{0,4},{1,3},{2,6},{3,1},{4,0},{5,7},{6,2},{7,5},{8,12},{9,11},{10,... | collective-permute-start | bytes 1228808 | tf_op jit(solution)/shard_map/ppermute | solution.py:397
  125.2 14.9 %collective-permute-start.9 = (bf16[512,512]{1,0:T(8,128)(2,1)S(1)}, bf16[512,512]{1,0:T(8,128)(2,1)S(1)}, u32[]{:S(2)}, u32[]{:S(2)}) collective-permute-start(bf16[512,512]{1,0:T(8,128)(2,1)S(1)} %fusion), channel_id=1, source_target_pairs={{0,2},{1,3},{2,0},{3,1},{4,6},{5,7},{6,4},{7,5},{8,10},{9,11},{10,... | collective-permute-start | bytes 1572872 | tf_op jit(solution)/shard_map/ppermute | solution.py:374
  135.6 8.8 %collective-permute-start.13 = (bf16[208,512]{1,0:T(8,128)(2,1)S(1)}, bf16[208,512]{1,0:T(8,128)(2,1)S(1)}, u32[]{:S(2)}, u32[]{:S(2)}) collective-permute-start(bf16[208,512]{1,0:T(8,128)(2,1)S(1)} %add_convert_fusion.9), channel_id=1, source_target_pairs={{0,2},{1,5},{2,0},{3,7},{4,6},{5,1},{6,4},{7,3},{8,10},{9,13},{10,... | collective-permute-start | bytes 638984 | tf_op jit(solution)/shard_map/ppermute | solution.py:397
  137.9 17.5 %copy-start.1 = (bf16[576,512]{1,0:T(8,128)(2,1)}, bf16[576,512]{1,0:T(8,128)(2,1)S(1)}, u32[]{:S(2)}) copy-start(bf16[576,512]{1,0:T(8,128)(2,1)S(1)} %add_convert_fusion.1.refs_0_) | copy-start | bytes 1769476
  137.9 14.8 %collective-permute-start.16 = (bf16[576,512]{1,0:T(8,128)(2,1)S(1)}, bf16[576,512]{1,0:T(8,128)(2,1)S(1)}, u32[]{:S(2)}, u32[]{:S(2)}) collective-permute-start(bf16[576,512]{1,0:T(8,128)(2,1)S(1)} %add_convert_fusion.1.refs_0_), channel_id=1, source_target_pairs={{0,2},{1,5},{2,0},{3,7},{4,6},{5,1},{6,4},{7,3},{8,10},{9,13},{10,... | collective-permute-start | bytes 1769480 | tf_op jit(solution)/shard_map/ppermute | solution.py:397
  140.1 6.6 %copy-start.14 = (bf16[512,512]{1,0:T(8,128)(2,1)}, bf16[512,512]{1,0:T(8,128)(2,1)S(1)}, u32[]{:S(2)}) copy-start(bf16[512,512]{1,0:T(8,128)(2,1)S(1)} %collective-permute-done.9.refs_5_) | copy-start | bytes 1572868
  144.6 8.1 %collective-permute-start.14 = (bf16[208,512]{1,0:T(8,128)(2,1)S(1)}, bf16[208,512]{1,0:T(8,128)(2,1)S(1)}, u32[]{:S(2)}, u32[]{:S(2)}) collective-permute-start(bf16[208,512]{1,0:T(8,128)(2,1)S(1)} %add_convert_fusion.8), channel_id=1, source_target_pairs={{0,8},{1,17},{2,10},{3,19},{4,12},{5,21},{6,14},{7,23},{8,0},{9,25... | collective-permute-start | bytes 638984 | tf_op jit(solution)/shard_map/ppermute | solution.py:397
  152.7 11.3 %copy-start.3 = (bf16[576,512]{1,0:T(8,128)(2,1)}, bf16[576,512]{1,0:T(8,128)(2,1)S(1)}, u32[]{:S(2)}) copy-start(bf16[576,512]{1,0:T(8,128)(2,1)S(1)} %collective-permute-done.16.refs_1_) | copy-start | bytes 1769476
  152.8 18.6 %collective-permute-start.21 = (bf16[1152,512]{1,0:T(8,128)(2,1)S(1)}, bf16[1152,512]{1,0:T(8,128)(2,1)S(1)}, u32[]{:S(2)}, u32[]{:S(2)}) collective-permute-start(bf16[1152,512]{1,0:T(8,128)(2,1)S(1)} %pad_maximum_fusion), channel_id=1, source_target_pairs={{0,4},{1,3},{2,6},{3,1},{4,0},{5,7},{6,2},{7,5},{8,12},{9,11},{10,... | collective-permute-start | bytes 3538952 | tf_op jit(solution)/shard_map/ppermute | solution.py:397
  154.0 9.0 %collective-permute-start.15 = (bf16[208,512]{1,0:T(8,128)(2,1)S(1)}, bf16[208,512]{1,0:T(8,128)(2,1)S(1)}, u32[]{:S(2)}, u32[]{:S(2)}) collective-permute-start(bf16[208,512]{1,0:T(8,128)(2,1)S(1)} %add_convert_fusion.7), channel_id=1, source_target_pairs={{0,16},{1,9},{2,18},{3,11},{4,20},{5,13},{6,22},{7,15},{8,24},{9,1... | collective-permute-start | bytes 638984 | tf_op jit(solution)/shard_map/ppermute | solution.py:397
  155.4 7.8 %collective-permute-start.18 = (bf16[576,512]{1,0:T(8,128)(2,1)S(1)}, bf16[576,512]{1,0:T(8,128)(2,1)S(1)}, u32[]{:S(2)}, u32[]{:S(2)}) collective-permute-start(bf16[576,512]{1,0:T(8,128)(2,1)S(1)} %add_convert_fusion.1.refs_0_), channel_id=1, source_target_pairs={{0,1},{1,0},{2,3},{3,2},{4,5},{5,4},{6,7},{7,6},{8,9},{9,8},{10,11... | collective-permute-start | bytes 1769480 | tf_op jit(solution)/shard_map/ppermute | solution.py:374
  155.4 8.6 %collective-permute-start.19 = (bf16[576,512]{1,0:T(8,128)(2,1)S(1)}, bf16[576,512]{1,0:T(8,128)(2,1)}, u32[]{:S(2)}, u32[]{:S(2)}) collective-permute-start(bf16[576,512]{1,0:T(8,128)(2,1)S(1)} %collective-permute-done.16.refs_1_), channel_id=1, source_target_pairs={{0,1},{1,0},{2,3},{3,2},{4,5},{5,4},{6,7},{7,6},{8,9},{9,8},{10,11... | collective-permute-start | bytes 1769480 | tf_op jit(solution)/shard_map/ppermute | solution.py:374
  163.1 17.3 %copy-start.5 = (bf16[208,512]{1,0:T(8,128)(2,1)}, bf16[208,512]{1,0:T(8,128)(2,1)S(1)}, u32[]{:S(2)}) copy-start(bf16[208,512]{1,0:T(8,128)(2,1)S(1)} %add_convert_fusion.6.refs_0_) | copy-start | bytes 638980
  163.2 6.6 %collective-permute-start.17 = (bf16[192,512]{1,0:T(8,128)(2,1)S(1)}, bf16[192,512]{1,0:T(8,128)(2,1)}, u32[]{:S(2)}, u32[]{:S(2)}) collective-permute-start(bf16[192,512]{1,0:T(8,128)(2,1)S(1)} %slice.87), channel_id=1, source_target_pairs={{0,2},{1,5},{2,0},{3,7},{4,6},{5,1},{6,4},{7,3},{8,10},{9,13},{10,... | collective-permute-start | bytes 589832 | tf_op jit(solution)/shard_map/ppermute | solution.py:397
  163.2 0.8 copy-start.9
  171.4 2.9 %copy-start.6 = (bf16[1152,512]{1,0:T(8,128)(2,1)}, bf16[1152,512]{1,0:T(8,128)(2,1)S(1)}, u32[]{:S(2)}) copy-start(bf16[1152,512]{1,0:T(8,128)(2,1)S(1)} %collective-permute-done.21.refs_0_) | copy-start | bytes 3538948
  171.4 2.8 %collective-permute-start.22 = (bf16[1152,512]{1,0:T(8,128)(2,1)S(1)}, bf16[1152,512]{1,0:T(8,128)(2,1)S(1)}, u32[]{:S(2)}, u32[]{:S(2)}) collective-permute-start(bf16[1152,512]{1,0:T(8,128)(2,1)S(1)} %collective-permute-done.21.refs_0_), channel_id=1, source_target_pairs={{0,1},{1,0},{2,3},{3,2},{4,5},{5,4},{6,7},{7,6},{8,9},{9,8},{10,11... | collective-permute-start | bytes 3538952 | tf_op jit(solution)/shard_map/ppermute | solution.py:374
  171.4 8.8 %collective-permute-start.20 = (bf16[384,512]{1,0:T(8,128)(2,1)}, bf16[384,512]{1,0:T(8,128)(2,1)S(1)}, u32[]{:S(2)}, u32[]{:S(2)}) collective-permute-start(bf16[384,512]{1,0:T(8,128)(2,1)} %pad_maximum_fusion.3), channel_id=1, source_target_pairs={{0,4},{1,3},{2,6},{3,1},{4,0},{5,7},{6,2},{7,5},{8,12},{9,11},{10,... | collective-permute-start | bytes 1179656 | tf_op jit(solution)/shard_map/ppermute | solution.py:397
  174.3 1.0 copy-start.7
  180.2 2.6 %copy-start.15 = (bf16[384,512]{1,0:T(8,128)(2,1)}, bf16[384,512]{1,0:T(8,128)(2,1)S(1)}, u32[]{:S(2)}) copy-start(bf16[384,512]{1,0:T(8,128)(2,1)S(1)} %collective-permute-done.20.refs_2_) | copy-start | bytes 1179652
  180.2 2.6 %collective-permute-start.25 = (bf16[384,512]{1,0:T(8,128)(2,1)S(1)}, bf16[384,512]{1,0:T(8,128)(2,1)S(1)}, u32[]{:S(2)}, u32[]{:S(2)}) collective-permute-start(bf16[384,512]{1,0:T(8,128)(2,1)S(1)} %collective-permute-done.20.refs_2_), channel_id=1, source_target_pairs={{0,1},{1,0},{2,3},{3,2},{4,5},{5,4},{6,7},{7,6},{8,9},{9,8},{10,11... | collective-permute-start | bytes 1179656 | tf_op jit(solution)/shard_map/ppermute | solution.py:374
  180.4 2.2 %collective-permute-start.23 = (bf16[208,512]{1,0:T(8,128)(2,1)S(1)}, bf16[208,512]{1,0:T(8,128)(2,1)S(1)}, u32[]{:S(2)}, u32[]{:S(2)}) collective-permute-start(bf16[208,512]{1,0:T(8,128)(2,1)S(1)} %add_convert_fusion.6.refs_0_), channel_id=1, source_target_pairs={{0,1},{1,0},{2,3},{3,2},{4,5},{5,4},{6,7},{7,6},{8,9},{9,8},{10,11... | collective-permute-start | bytes 638984 | tf_op jit(solution)/shard_map/ppermute | solution.py:374
  180.8 2.0 %collective-permute-start.24 = (bf16[192,512]{1,0:T(8,128)(2,1)}, bf16[192,512]{1,0:T(8,128)(2,1)S(1)}, u32[]{:S(2)}, u32[]{:S(2)}) collective-permute-start(bf16[192,512]{1,0:T(8,128)(2,1)} %collective-permute-done.17.refs_1_), channel_id=1, source_target_pairs={{0,1},{1,0},{2,3},{3,2},{4,5},{5,4},{6,7},{7,6},{8,9},{9,8},{10,11... | collective-permute-start | bytes 589832 | tf_op jit(solution)/shard_map/ppermute | solution.py:374
  182.6 0.7 copy-start.17
  182.8 0.7 copy-start.18
  183.5 0.8 copy-start.16

commit v6 on v5

--- a/solution.py
+++ b/solution.py
@@ -16,7 +16,7 @@
 GELU_A = 0.044715
 MIB = 1 << 20
 CHUNKS = 4
-LIMIT = 60
+LIMIT = 50
 
 
 def dot_nn(a, b):

time: 189 us -> 184 us (0.974)
  Pallas kernels: 109 us -> 95.6 us
  waiting for transfers between devices: 37.8 us -> 50.3 us
  local copies, waits for them, and re-layouts: 7.03 us -> 4.96 us
  other arithmetic: 10.3 us -> 8.32 us
    pallas_call x10, Pallas kernels: 109 us -> 95.6 us  [call(): pl.pallas_call(kernel, grid_spec=pltpu.PrefetchScalarGridSpec(num_scalar_...]
    ppermute x12, waiting for transfers between devices: 25.1 us -> 33.1 us  [send_all(): return lax.ppermute(value, ('dp', 'rows'), perm)]
    ppermute x14, waiting for transfers between devices: 12.7 us -> 17.3 us  [exchange(): return lax.ppermute(value, axis, [(i, i ^ distance) for i in range(size)])]
  transfers between devices with their start and end apart: 26 -> 26, of which waited for: 15 -> 17; matrix products, arithmetic and copies ran while one was open for 3% -> 2% of each run, Pallas kernels for 33% -> 29%
where the time goes in v6:
time: 184 us; the launch traced here: 183 us
  Pallas kernels  95.6 us (52%)
  waiting for transfers between devices  50.3 us (27%)
  starting transfers between devices  23.1 us (13%)
  other arithmetic  8.32 us (5%)
  local copies, waits for them, and re-layouts  4.96 us (3%)
    pallas_call x10, Pallas kernels, call(): pl.pallas_call(kernel, grid_spec=pltpu.PrefetchScalarGridSpec(num_scalar_...  95.6 us
    ppermute x12, waiting for transfers between devices, send_all(): return lax.ppermute(value, ('dp', 'rows'), perm)  33.1 us
    ppermute x14, waiting for transfers between devices, exchange(): return lax.ppermute(value, axis, [(i, i ^ distance) for i in range(size)])  17.3 us
    ppermute x12, starting transfers between devices, send_all(): return lax.ppermute(value, ('dp', 'rows'), perm)  16.8 us
    ppermute x14, starting transfers between devices, exchange(): return lax.ppermute(value, axis, [(i, i ^ distance) for i in range(size)])  6.3 us
    convert_element_type x11, other arithmetic, add_low(): return total.astype(BF)  5.87 us
    unnamed x39, local copies, waits for them, and re-layouts  4.7 us
  transfers between devices with their start and end apart: 26, of which 17 were waited for; matrix products, arithmetic and copies ran while one was open for 2% of the time, Pallas kernels for 29%

profile of v6, /device:TPU:0, one launch (start us, length us, event | category | flops | bytes accessed | tf_op | source)
XLA Modules:
  0.0 183.3 jit_solution(17017897274034850376)
XLA Ops:
  0.7 1.2 pad_maximum_fusion.1
  2.0 0.5 collective-permute-start
  2.5 2.6 %collective-permute-start.1 = (bf16[512,512]{1,0:T(8,128)(2,1)S(1)}, bf16[512,512]{1,0:T(8,128)(2,1)S(1)}, u32[]{:S(2)}, u32[]{:S(2)}) collective-permute-start(bf16[512,512]{1,0:T(8,128)(2,1)S(1)} %bitcast.62), channel_id=1, source_target_pairs={{0,2},{1,3},{2,0},{3,1},{4,6},{5,7},{6,4},{7,5},{8,10},{9,11},{10,... | collective-permute-start | bytes 1572872 | tf_op jit(solution)/shard_map/ppermute | solution.py:374
  5.1 0.8 copy.63
  5.8 0.1 reshape.160.refs_2_
  5.9 0.1 stack.23.ids
  6.0 1.1 pad_maximum_fusion.2
  7.2 4.2 %front.1 = (bf16[512,512]{1,0:T(8,128)(2,1)S(1)}, bf16[4,512,512]{2,1,0:T(8,128)(2,1)}, bf16[4,512,512]{2,1,0:T(8,128)(2,1)}, bf16[4,512,512]{2,1,0:T(8,128)(2,1)}, bf16[4,512,512]{2,1,0:T(8,128)(2,1)}) custom-call(s32[5]{0:T(128)S(1)} %stack.23.ids, bf16[512,512]{1,0:T(8,128)(2,1)S(1)} %bitcast.63, bf16[512,512]{1,0:T(8,128)(2,1)S(1)} %collective-permute-done.x1, ...), custom_call_target="tpu_custom_call" | custom-call | bytes 3200000 | tf_op jit(solution)/shard_map/front/pallas_call | solution.py:533
  11.4 6.2 %collective-permute-done.1.refs_4_ = bf16[512,512]{1,0:T(8,128)(2,1)S(1)} collective-permute-done((bf16[512,512]{1,0:T(8,128)(2,1)S(1)}, bf16[512,512]{1,0:T(8,128)(2,1)S(1)}, u32[]{:S(2)}, u32[]{:S(2)}) %collective-permute-start.1) | collective-permute-done | bytes 524320 | tf_op jit(solution)/shard_map/ppermute | solution.py:374
  17.6 1.9 %collective-permute-done.2.refs_5_ = bf16[512,512]{1,0:T(8,128)(2,1)S(1)} collective-permute-done((bf16[512,512]{1,0:T(8,128)(2,1)S(1)}, bf16[512,512]{1,0:T(8,128)(2,1)S(1)}, u32[]{:S(2)}, u32[]{:S(2)}) %collective-permute-start.2) | collective-permute-done | bytes 524320 | tf_op jit(solution)/shard_map/ppermute | solution.py:374
  19.5 21.2 %attend.1 = (bf16[4,64,64,256]{3,2,1,0:T(8,128)(2,1)}, bf16[4,64,32,128]{3,2,1,0:T(8,128)(2,1)}, bf16[8,64,16,64]{3,2,1,0:T(8,128)(2,1)}, bf16[4,64,64,256]{3,2,...) custom-call(s32[5]{0:T(128)S(1)} %stack.23.ids, ...), custom_call_target="tpu_custom_call", output_to_operand_aliasing={{7}: (14, {}), {8}: (15, {}), {9}: (16, {}), {10}: (17, {})} | custom-call | bytes 14400000 | tf_op jit(solution)/shard_map/attend/pallas_call | solution.py:533
  40.7 1.0 copy-done.3
  41.7 17.8 %dense.1 = (bf16[4,64,512]{2,1,0:T(8,128)(2,1)}, bf16[4,32,512]{2,1,0:T(8,128)(2,1)}, bf16[4,32,512]{2,1,0:T(8,128)(2,1)}, f32[512,512]{1,0:T(8,128)S(1)}, bf16[...) custom-call(s32[5]{0:T(128)S(1)} %stack.23.ids, ...), custom_call_target="tpu_custom_call" | custom-call | bytes 12800000 | tf_op jit(solution)/shard_map/dense/pallas_call | solution.py:533
  59.5 0.1 collective-permute-start.3
  59.6 2.9 %collective-permute-done.3 = bf16[1152,512]{1,0:T(8,128)(2,1)S(1)} collective-permute-done((bf16[1152,512]{1,0:T(8,128)(2,1)}, bf16[1152,512]{1,0:T(8,128)(2,1)S(1)}, u32[]{:S(2)}, u32[]{:S(2)}) %collective-permute-start.3) | collective-permute-done | bytes 1179680 | tf_op jit(solution)/shard_map/ppermute | solution.py:374
  62.6 1.6 add_convert_fusion
  64.2 1.8 collective-permute-start.5
  66.0 14.7 %attend_back_big.1 = (bf16[4,64,64,256]{3,2,1,0:T(8,128)(2,1)}, bf16[256,512]{1,0:T(8,128)(2,1)S(1)}, bf16[512,1024]{1,0:T(8,128)(2,1)S(1)}, bf16[512,1024]{1,0:T(8,128)(2,1)S(1)}) custom-call(s32[5]{0:T(128)S(1)} %stack.23.ids, bf16[512,512]{1,0:T(8,128)(2,1)S(1)} %get-tuple-element.100.refs_3_.refs_0_, bf16[512,512]{1,0:T(8,128)(2,1)S(1)} %get-tuple-element.125.refs_1_, ...), custom_call_target="tpu_custom_call" | custom-call | bytes 12000000 | tf_op jit(solution)/shard_map/attend_back_big/pallas_call | solution.py:533
  80.7 1.0 copy-done.6
  81.7 1.9 %add_convert_fusion.4 = bf16[576,512]{1,0:T(8,128)(2,1)S(1)} fusion(bf16[1152,512]{1,0:T(8,128)(2,1)} %collective-permute-done.4, bf16[1152,512]{1,0:T(8,128)(2,1)} %collective-permute-done.5, bf16[2304,512]{1,0:T(8,128)(2,1)S(1)} %copy-done.16), kind=kLoop, calls=%fused_computation.5 | loop fusion | flops 1769472 | bytes 2359296 | tf_op jit(solution)/shard_map/convert_element_type | solution.py:381
  83.5 1.6 collective-permute-start.6
  85.1 14.8 %attend_back_rest.1 = (bf16[4,64,32,128]{3,2,1,0:T(8,128)(2,1)}, bf16[8,64,16,64]{3,2,1,0:T(8,128)(2,1)}, bf16[256,512]{1,0:T(8,128)(2,1)S(1)}, bf16[512,1024]{1,0:T(8,128)(2,1)S(1)}, bf16[512,1024]{1,0:T(8,128)(2,1)S(1)}) custom-call(s32[5]{0:T(128)S(1)} %stack.23.ids, bf16[512,512]{1,0:T(8,128)(2,1)S(1)} %get-tuple-element.100.refs_3_.refs_0_, ...), custom_call_target="tpu_custom_call" | custom-call | bytes 12000000 | tf_op jit(solution)/shard_map/attend_back_rest/pallas_call | solution.py:533
  100.0 1.0 copy-done.7
  100.9 1.0 copy-done.8
  101.9 1.6 add_convert_fusion.3
  103.5 1.6 collective-permute-start.7
  105.1 10.4 %back.1 = (f32[512,512]{1,0:T(8,128)}, bf16[512,512]{1,0:T(8,128)(2,1)S(1)}, bf16[2,512,512]{2,1,0:T(8,128)(2,1)}, bf16[784,512]{1,0:T(8,128)(2,1)S(1)}, bf16[784,512]{1,0:T(8,128)(2,1)}) custom-call(s32[5]{0:T(128)S(1)} %stack.23.ids, bf16[256,512]{1,0:T(8,128)(2,1)S(1)} %get-tuple-element.122.refs_0_, bf16[256,512]{1,0:T(8,128)(2,1)S(1)} %get-tuple-element.130.refs_1_, ...), custom_call_target="tpu_custom_call" | custom-call | bytes 7200000 | tf_op jit(solution)/shard_map/back/pallas_call | solution.py:533
  115.5 3.2 %collective-permute-done.7 = bf16[576,512]{1,0:T(8,128)(2,1)S(1)} collective-permute-done((bf16[576,512]{1,0:T(8,128)(2,1)S(1)}, bf16[576,512]{1,0:T(8,128)(2,1)S(1)}, u32[]{:S(2)}, u32[]{:S(2)}) %collective-permute-start.7) | collective-permute-done | bytes 589856 | tf_op jit(solution)/shard_map/ppermute | solution.py:397
  118.8 0.2 add_convert_fusion.2
  118.9 0.4 collective-permute-start.8
  119.3 0.2 collective-permute-start.11
  119.5 2.5 %collective-permute-start.10 = (bf16[576,512]{1,0:T(8,128)(2,1)S(1)}, bf16[576,512]{1,0:T(8,128)(2,1)S(1)}, u32[]{:S(2)}, u32[]{:S(2)}) collective-permute-start(bf16[576,512]{1,0:T(8,128)(2,1)S(1)} %add_convert_fusion.2), channel_id=1, source_target_pairs={{0,16},{1,9},{2,18},{3,11},{4,20},{5,13},{6,22},{7,15},{8,24},{9,1... | collective-permute-start | bytes 1769480 | tf_op jit(solution)/shard_map/ppermute | solution.py:397
  122.0 0.1 fusion
  122.2 0.6 collective-permute-done.11
  122.8 0.1 add_convert_fusion.5
  122.9 1.5 collective-permute-start.12
  124.4 1.5 collective-permute-start.9
  125.9 5.0 %collective-permute-done.12 = bf16[400,512]{1,0:T(8,128)(2,1)S(1)} collective-permute-done((bf16[400,512]{1,0:T(8,128)(2,1)S(1)}, bf16[400,512]{1,0:T(8,128)(2,1)S(1)}, u32[]{:S(2)}, u32[]{:S(2)}) %collective-permute-start.12) | collective-permute-done | bytes 409632 | tf_op jit(solution)/shard_map/ppermute | solution.py:397
  130.9 0.1 add_convert_fusion.9
  131.0 4.1 %collective-permute-done.10 = bf16[576,512]{1,0:T(8,128)(2,1)S(1)} collective-permute-done((bf16[576,512]{1,0:T(8,128)(2,1)S(1)}, bf16[576,512]{1,0:T(8,128)(2,1)S(1)}, u32[]{:S(2)}, u32[]{:S(2)}) %collective-permute-start.10) | collective-permute-done | bytes 589856 | tf_op jit(solution)/shard_map/ppermute | solution.py:397
  135.1 2.1 %collective-permute-start.13 = (bf16[208,512]{1,0:T(8,128)(2,1)S(1)}, bf16[208,512]{1,0:T(8,128)(2,1)S(1)}, u32[]{:S(2)}, u32[]{:S(2)}) collective-permute-start(bf16[208,512]{1,0:T(8,128)(2,1)S(1)} %add_convert_fusion.9), channel_id=1, source_target_pairs={{0,2},{1,5},{2,0},{3,7},{4,6},{5,1},{6,4},{7,3},{8,10},{9,13},{10,... | collective-permute-start | bytes 638984 | tf_op jit(solution)/shard_map/ppermute | solution.py:397
  137.3 0.2 add_convert_fusion.1.refs_0_
  137.5 1.8 collective-permute-done.9.refs_5_
  139.4 4.4 %collective-permute-done.13 = bf16[208,512]{1,0:T(8,128)(2,1)S(1)} collective-permute-done((bf16[208,512]{1,0:T(8,128)(2,1)S(1)}, bf16[208,512]{1,0:T(8,128)(2,1)S(1)}, u32[]{:S(2)}, u32[]{:S(2)}) %collective-permute-start.13) | collective-permute-done | bytes 213024 | tf_op jit(solution)/shard_map/ppermute | solution.py:397
  143.8 0.1 add_convert_fusion.8
  143.9 2.1 %collective-permute-start.14 = (bf16[208,512]{1,0:T(8,128)(2,1)S(1)}, bf16[208,512]{1,0:T(8,128)(2,1)S(1)}, u32[]{:S(2)}, u32[]{:S(2)}) collective-permute-start(bf16[208,512]{1,0:T(8,128)(2,1)S(1)} %add_convert_fusion.8), channel_id=1, source_target_pairs={{0,8},{1,17},{2,10},{3,19},{4,12},{5,21},{6,14},{7,23},{8,0},{9,25... | collective-permute-start | bytes 638984 | tf_op jit(solution)/shard_map/ppermute | solution.py:397
  146.0 3.3 %last.1 = (bf16[4,64,512]{2,1,0:T(8,128)(2,1)}, bf16[4,32,512]{2,1,0:T(8,128)(2,1)}, bf16[4,32,512]{2,1,0:T(8,128)(2,1)}) custom-call(s32[5]{0:T(128)S(1)} %stack.23.ids, bf16[512,512]{1,0:T(8,128)(2,1)S(1)} %bitcast.65, f32[512,512]{1,0:T(8,128)S(1)} %get-tuple-element.113.refs_1_, f32[1,512]{1,0:T(1,128)S(1)} %bitcast.69, f32[512,512]{1,0:T(8,128)S(1)} %copy-done.4, ...), custom_call_target="tpu_custom_call" | custom-call | bytes 1600000 | tf_op jit(solution)/shard_map/last/pallas_call | solution.py:533
  149.3 2.7 %collective-permute-done.14 = bf16[208,512]{1,0:T(8,128)(2,1)S(1)} collective-permute-done((bf16[208,512]{1,0:T(8,128)(2,1)S(1)}, bf16[208,512]{1,0:T(8,128)(2,1)S(1)}, u32[]{:S(2)}, u32[]{:S(2)}) %collective-permute-start.14) | collective-permute-done | bytes 213024 | tf_op jit(solution)/shard_map/ppermute | solution.py:397
  152.0 0.1 pad_maximum_fusion
  152.1 0.9 collective-permute-start.21
  153.0 1.6 collective-permute-start.15
  154.7 0.5 collective-permute-start.19
  155.2 7.0 %collective-permute-done.15 = bf16[208,512]{1,0:T(8,128)(2,1)S(1)} collective-permute-done((bf16[208,512]{1,0:T(8,128)(2,1)S(1)}, bf16[208,512]{1,0:T(8,128)(2,1)S(1)}, u32[]{:S(2)}, u32[]{:S(2)}) %collective-permute-start.15) | collective-permute-done | bytes 213024 | tf_op jit(solution)/shard_map/ppermute | solution.py:397
  162.3 3.2 %finish_ff_early.1 = (f32[4,128,2048]{2,1,0:T(8,128)}, f32[2,2,4,128,512]{4,3,2,1,0:T(8,128)}, f32[2,4,64,512]{3,2,1,0:T(8,128)}) custom-call(s32[5]{0:T(128)S(1)} %stack.23.ids, bf16[576,512]{1,0:T(8,128)(2,1)S(1)} %add_convert_fusion.1.refs_0_, bf16[576,512]{1,0:T(8,128)(2,1)S(1)} %collective-permute-done.16.refs_1_, ...), custom_call_target="tpu_custom_call" | custom-call | bytes 3200000 | tf_op jit(solution)/shard_map/finish_ff_early/pallas_call | solution.py:533
  165.5 3.9 %collective-permute-done.17.refs_1_ = bf16[192,512]{1,0:T(8,128)(2,1)S(1)} collective-permute-done((bf16[192,512]{1,0:T(8,128)(2,1)S(1)}, bf16[192,512]{1,0:T(8,128)(2,1)S(1)}, u32[]{:S(2)}, u32[]{:S(2)}) %collective-permute-start.17) | collective-permute-done | bytes 196640 | tf_op jit(solution)/shard_map/ppermute | solution.py:397
  169.4 1.1 collective-permute-done.21.refs_0_
  170.5 0.9 collective-permute-start.20
  171.4 2.0 %collective-permute-done.22.refs_1_ = bf16[1152,512]{1,0:T(8,128)(2,1)S(1)} collective-permute-done((bf16[1152,512]{1,0:T(8,128)(2,1)S(1)}, bf16[1152,512]{1,0:T(8,128)(2,1)S(1)}, u32[]{:S(2)}, u32[]{:S(2)}) %collective-permute-start.22) | collective-permute-done | bytes 1179680 | tf_op jit(solution)/shard_map/ppermute | solution.py:374
  173.3 3.2 %finish_ff.1 = (f32[4,128,2048]{2,1,0:T(8,128)}, f32[2,2,4,128,512]{4,3,2,1,0:T(8,128)}, f32[2,4,64,512]{3,2,1,0:T(8,128)}) custom-call(s32[5]{0:T(128)S(1)} %stack.23.ids, bf16[1152,512]{1,0:T(8,128)(2,1)S(1)} %collective-permute-done.21.refs_0_, ...), custom_call_target="tpu_custom_call", output_to_operand_aliasing={{0}: (3, {}), {1}: (4, {}), {2}: (5, {})} | custom-call | bytes 3200000 | tf_op jit(solution)/shard_map/finish_ff/pallas_call | solution.py:533
  176.5 1.7 collective-permute-done.20.refs_2_
  178.3 0.5 collective-permute-start.23
  178.8 1.5 collective-permute-done.23.refs_3_
  180.3 0.3 collective-permute-done.24.refs_4_
  180.6 2.7 %finish_rest.1 = (f32[512,512]{1,0:T(8,128)}, f32[512,512]{1,0:T(8,128)}, f32[512,512]{1,0:T(8,128)}, f32[512]{0:T(512)}, f32[512]{0:T(512)}, /*index=5*/f32[512]{0:T(512)}, f32[512]{0:T(512)}) custom-call(s32[5]{0:T(128)S(1)} %stack.23.ids, bf16[208,512]{1,0:T(8,128)(2,1)S(1)} %add_convert_fusion.6.refs_0_, ...), custom_call_target="tpu_custom_call" | custom-call | bytes 2400000 | tf_op jit(solution)/shard_map/finish_rest/pallas_call | solution.py:533
  (61 shorter events, 0.5 us)
Async XLA Ops:
  0.7 6.5 %copy-start.1 = (bf16[512,512]{1,0:T(8,128)(2,1)S(1)}, bf16[512,512]{1,0:T(8,128)(2,1)}, u32[]{:S(2)}) copy-start(bf16[512,512]{1,0:T(8,128)(2,1)} %refs_10_.1) | copy-start | bytes 1572868
  0.7 6.5 %copy-start = (bf16[512,512]{1,0:T(8,128)(2,1)S(1)}, bf16[512,512]{1,0:T(8,128)(2,1)}, u32[]{:S(2)}) copy-start(bf16[512,512]{1,0:T(8,128)(2,1)} %refs_9_.1) | copy-start | bytes 1572868
  0.7 6.5 %copy-start.2 = (bf16[512,512]{1,0:T(8,128)(2,1)S(1)}, bf16[512,512]{1,0:T(8,128)(2,1)}, u32[]{:S(2)}) copy-start(bf16[512,512]{1,0:T(8,128)(2,1)} %refs_8_.1) | copy-start | bytes 1572868
  0.7 6.5 %copy-start.11 = (f32[512]{0:T(512)S(1)}, f32[512]{0:T(512)}, u32[]{:S(2)}) copy-start(f32[512]{0:T(512)} %param.41) | copy-start | bytes 6148
  0.7 6.5 %copy-start.10 = (f32[512]{0:T(512)S(1)}, f32[512]{0:T(512)}, u32[]{:S(2)}) copy-start(f32[512]{0:T(512)} %param.40) | copy-start | bytes 6148
  1.9 17.6 %copy-start.14 = (s32[4,1]{0,1:T(1,128)S(1)}, s32[4,1]{0,1:T(1,128)}, u32[]{:S(2)}) copy-start(s32[4,1]{0,1:T(1,128)} %param.31) | copy-start | bytes 52
  1.9 17.6 %copy-start.15 = (s32[4,1]{0,1:T(1,128)S(1)}, s32[4,1]{0,1:T(1,128)}, u32[]{:S(2)}) copy-start(s32[4,1]{0,1:T(1,128)} %param.32) | copy-start | bytes 52
  2.0 5.2 %collective-permute-start = (bf16[512,512]{1,0:T(8,128)(2,1)S(1)}, bf16[512,512]{1,0:T(8,128)(2,1)S(1)}, u32[]{:S(2)}, u32[]{:S(2)}) collective-permute-start(bf16[512,512]{1,0:T(8,128)(2,1)S(1)} %bitcast.61), channel_id=1, source_target_pairs={{0,1},{1,0},{2,3},{3,2},{4,5},{5,4},{6,7},{7,6},{8,9},{9,8},{10,11... | collective-permute-start | bytes 1572872 | tf_op jit(solution)/shard_map/ppermute | solution.py:374
  2.5 15.1 %collective-permute-start.1 = (bf16[512,512]{1,0:T(8,128)(2,1)S(1)}, bf16[512,512]{1,0:T(8,128)(2,1)S(1)}, u32[]{:S(2)}, u32[]{:S(2)}) collective-permute-start(bf16[512,512]{1,0:T(8,128)(2,1)S(1)} %bitcast.62), channel_id=1, source_target_pairs={{0,2},{1,3},{2,0},{3,1},{4,6},{5,7},{6,4},{7,5},{8,10},{9,11},{10,... | collective-permute-start | bytes 1572872 | tf_op jit(solution)/shard_map/ppermute | solution.py:374
  17.6 1.9 %collective-permute-start.2 = (bf16[512,512]{1,0:T(8,128)(2,1)S(1)}, bf16[512,512]{1,0:T(8,128)(2,1)S(1)}, u32[]{:S(2)}, u32[]{:S(2)}) collective-permute-start(bf16[512,512]{1,0:T(8,128)(2,1)S(1)} %collective-permute-done.1.refs_4_), channel_id=1, source_target_pairs={{0,1},{1,0},{2,3},{3,2},{4,5},{5,4},{6,7},{7,6},{8,9},{9,8},{10,11... | collective-permute-start | bytes 1572872 | tf_op jit(solution)/shard_map/ppermute | solution.py:374
  19.5 22.2 %copy-start.9 = (bf16[512,512]{1,0:T(8,128)(2,1)S(1)}, bf16[512,512]{1,0:T(8,128)(2,1)}, u32[]{:S(2)}) copy-start(bf16[512,512]{1,0:T(8,128)(2,1)} %wo.1) | copy-start | bytes 1572868
  19.5 22.2 %copy-start.12 = (f32[512]{0:T(512)S(1)}, f32[512]{0:T(512)}, u32[]{:S(2)}) copy-start(f32[512]{0:T(512)} %param.42) | copy-start | bytes 6148
  19.5 22.2 %copy-start.13 = (f32[512]{0:T(512)S(1)}, f32[512]{0:T(512)}, u32[]{:S(2)}) copy-start(f32[512]{0:T(512)} %param.43) | copy-start | bytes 6148
  40.7 1.0 copy-start.3
  59.5 3.1 %collective-permute-start.3 = (bf16[1152,512]{1,0:T(8,128)(2,1)}, bf16[1152,512]{1,0:T(8,128)(2,1)S(1)}, u32[]{:S(2)}, u32[]{:S(2)}) collective-permute-start(bf16[1152,512]{1,0:T(8,128)(2,1)} %get-tuple-element.116), channel_id=1, source_target_pairs={{0,1},{1,0},{2,3},{3,2},{4,5},{5,4},{6,7},{7,6},{8,9},{9,8},{10,11... | collective-permute-start | bytes 3538952 | tf_op jit(solution)/shard_map/ppermute | solution.py:374
  64.2 17.5 %collective-permute-start.5 = (bf16[1152,512]{1,0:T(8,128)(2,1)S(1)}, bf16[1152,512]{1,0:T(8,128)(2,1)}, u32[]{:S(2)}, u32[]{:S(2)}) collective-permute-start(bf16[1152,512]{1,0:T(8,128)(2,1)S(1)} %add_convert_fusion), channel_id=1, source_target_pairs={{0,4},{1,3},{2,6},{3,1},{4,0},{5,7},{6,2},{7,5},{8,12},{9,11},{10,... | collective-permute-start | bytes 3538952 | tf_op jit(solution)/shard_map/ppermute | solution.py:397
  66.0 15.7 %collective-permute-start.4 = (bf16[1152,512]{1,0:T(8,128)(2,1)}, bf16[1152,512]{1,0:T(8,128)(2,1)}, u32[]{:S(2)}, u32[]{:S(2)}) collective-permute-start(bf16[1152,512]{1,0:T(8,128)(2,1)} %get-tuple-element.123), channel_id=1, source_target_pairs={{0,1},{1,0},{2,3},{3,2},{4,5},{5,4},{6,7},{7,6},{8,9},{9,8},{10,11... | collective-permute-start | bytes 3538952 | tf_op jit(solution)/shard_map/ppermute | solution.py:374
  66.0 15.7 %copy-start.16 = (bf16[2304,512]{1,0:T(8,128)(2,1)S(1)}, bf16[2304,512]{1,0:T(8,128)(2,1)}, u32[]{:S(2)}) copy-start(bf16[2304,512]{1,0:T(8,128)(2,1)} %get-tuple-element.115) | copy-start | bytes 7077892
  80.7 1.0 copy-start.6
  81.7 18.3 %copy-start.5 = (bf16[512,1024]{1,0:T(8,128)(2,1)}, bf16[512,1024]{1,0:T(8,128)(2,1)S(1)}, u32[]{:S(2)}) copy-start(bf16[512,1024]{1,0:T(8,128)(2,1)S(1)} %get-tuple-element.131.refs_2_) | copy-start | bytes 3145732
  83.5 18.4 %collective-permute-start.6 = (bf16[576,512]{1,0:T(8,128)(2,1)S(1)}, bf16[576,512]{1,0:T(8,128)(2,1)S(1)}, u32[]{:S(2)}, u32[]{:S(2)}) collective-permute-start(bf16[576,512]{1,0:T(8,128)(2,1)S(1)} %add_convert_fusion.4), channel_id=1, source_target_pairs={{0,2},{1,5},{2,0},{3,7},{4,6},{5,1},{6,4},{7,3},{8,10},{9,13},{10,... | collective-permute-start | bytes 1769480 | tf_op jit(solution)/shard_map/ppermute | solution.py:397
  100.0 1.0 copy-start.7
  100.9 1.0 copy-start.8
  103.5 15.3 %collective-permute-start.7 = (bf16[576,512]{1,0:T(8,128)(2,1)S(1)}, bf16[576,512]{1,0:T(8,128)(2,1)S(1)}, u32[]{:S(2)}, u32[]{:S(2)}) collective-permute-start(bf16[576,512]{1,0:T(8,128)(2,1)S(1)} %add_convert_fusion.3), channel_id=1, source_target_pairs={{0,8},{1,17},{2,10},{3,19},{4,12},{5,21},{6,14},{7,23},{8,0},{9,25... | collective-permute-start | bytes 1769480 | tf_op jit(solution)/shard_map/ppermute | solution.py:397
  115.5 7.3 %copy-start.18 = (bf16[784,512]{1,0:T(8,128)(2,1)S(1)}, bf16[784,512]{1,0:T(8,128)(2,1)}, u32[]{:S(2)}) copy-start(bf16[784,512]{1,0:T(8,128)(2,1)} %get-tuple-element.144) | copy-start | bytes 2408452
  118.9 3.1 %collective-permute-start.8 = (bf16[2,512,512]{2,1,0:T(8,128)(2,1)}, bf16[2,512,512]{2,1,0:T(8,128)(2,1)S(1)}, u32[]{:S(2)}, u32[]{:S(2)}) collective-permute-start(bf16[2,512,512]{2,1,0:T(8,128)(2,1)} %get-tuple-element.142), channel_id=1, source_target_pairs={{0,1},{1,0},{2,3},{3,2},{4,5},{5,4},{6,7},{7,6},{8,9},{9,8},{10,11... | collective-permute-start | bytes 3145736 | tf_op jit(solution)/shard_map/ppermute | solution.py:374
  119.3 3.5 %collective-permute-start.11 = (bf16[784,512]{1,0:T(8,128)(2,1)S(1)}, bf16[784,512]{1,0:T(8,128)(2,1)S(1)}, u32[]{:S(2)}, u32[]{:S(2)}) collective-permute-start(bf16[784,512]{1,0:T(8,128)(2,1)S(1)} %get-tuple-element.145), channel_id=1, source_target_pairs={{0,1},{1,0},{2,3},{3,2},{4,5},{5,4},{6,7},{7,6},{8,9},{9,8},{10,11... | collective-permute-start | bytes 2408456 | tf_op jit(solution)/shard_map/ppermute | solution.py:374
  119.5 15.6 %collective-permute-start.10 = (bf16[576,512]{1,0:T(8,128)(2,1)S(1)}, bf16[576,512]{1,0:T(8,128)(2,1)S(1)}, u32[]{:S(2)}, u32[]{:S(2)}) collective-permute-start(bf16[576,512]{1,0:T(8,128)(2,1)S(1)} %add_convert_fusion.2), channel_id=1, source_target_pairs={{0,16},{1,9},{2,18},{3,11},{4,20},{5,13},{6,22},{7,15},{8,24},{9,1... | collective-permute-start | bytes 1769480 | tf_op jit(solution)/shard_map/ppermute | solution.py:397
  122.0 3.9 %copy-start.17 = (bf16[2,512,512]{2,1,0:T(8,128)(2,1)}, bf16[2,512,512]{2,1,0:T(8,128)(2,1)S(1)}, u32[]{:S(2)}) copy-start(bf16[2,512,512]{2,1,0:T(8,128)(2,1)S(1)} %collective-permute-done.8.refs_4_) | copy-start | bytes 3145732
  122.9 8.0 %collective-permute-start.12 = (bf16[400,512]{1,0:T(8,128)(2,1)S(1)}, bf16[400,512]{1,0:T(8,128)(2,1)S(1)}, u32[]{:S(2)}, u32[]{:S(2)}) collective-permute-start(bf16[400,512]{1,0:T(8,128)(2,1)S(1)} %add_convert_fusion.5), channel_id=1, source_target_pairs={{0,4},{1,3},{2,6},{3,1},{4,0},{5,7},{6,2},{7,5},{8,12},{9,11},{10,... | collective-permute-start | bytes 1228808 | tf_op jit(solution)/shard_map/ppermute | solution.py:397
  124.4 14.9 %collective-permute-start.9 = (bf16[512,512]{1,0:T(8,128)(2,1)S(1)}, bf16[512,512]{1,0:T(8,128)(2,1)S(1)}, u32[]{:S(2)}, u32[]{:S(2)}) collective-permute-start(bf16[512,512]{1,0:T(8,128)(2,1)S(1)} %fusion), channel_id=1, source_target_pairs={{0,2},{1,3},{2,0},{3,1},{4,6},{5,7},{6,4},{7,5},{8,10},{9,11},{10,... | collective-permute-start | bytes 1572872 | tf_op jit(solution)/shard_map/ppermute | solution.py:374
  125.9 20.0 %copy-start.4 = (f32[512,512]{1,0:T(8,128)S(1)}, f32[512,512]{1,0:T(8,128)}, u32[]{:S(2)}) copy-start(f32[512,512]{1,0:T(8,128)} %get-tuple-element.138.refs_3_) | copy-start | bytes 3145732
  135.1 8.6 %collective-permute-start.13 = (bf16[208,512]{1,0:T(8,128)(2,1)S(1)}, bf16[208,512]{1,0:T(8,128)(2,1)S(1)}, u32[]{:S(2)}, u32[]{:S(2)}) collective-permute-start(bf16[208,512]{1,0:T(8,128)(2,1)S(1)} %add_convert_fusion.9), channel_id=1, source_target_pairs={{0,2},{1,5},{2,0},{3,7},{4,6},{5,1},{6,4},{7,3},{8,10},{9,13},{10,... | collective-permute-start | bytes 638984 | tf_op jit(solution)/shard_map/ppermute | solution.py:397
  137.4 14.6 %collective-permute-start.16 = (bf16[576,512]{1,0:T(8,128)(2,1)S(1)}, bf16[576,512]{1,0:T(8,128)(2,1)S(1)}, u32[]{:S(2)}, u32[]{:S(2)}) collective-permute-start(bf16[576,512]{1,0:T(8,128)(2,1)S(1)} %add_convert_fusion.1.refs_0_), channel_id=1, source_target_pairs={{0,2},{1,5},{2,0},{3,7},{4,6},{5,1},{6,4},{7,3},{8,10},{9,13},{10,... | collective-permute-start | bytes 1769480 | tf_op jit(solution)/shard_map/ppermute | solution.py:397
  143.9 8.1 %collective-permute-start.14 = (bf16[208,512]{1,0:T(8,128)(2,1)S(1)}, bf16[208,512]{1,0:T(8,128)(2,1)S(1)}, u32[]{:S(2)}, u32[]{:S(2)}) collective-permute-start(bf16[208,512]{1,0:T(8,128)(2,1)S(1)} %add_convert_fusion.8), channel_id=1, source_target_pairs={{0,8},{1,17},{2,10},{3,19},{4,12},{5,21},{6,14},{7,23},{8,0},{9,25... | collective-permute-start | bytes 638984 | tf_op jit(solution)/shard_map/ppermute | solution.py:397
  152.1 18.4 %collective-permute-start.21 = (bf16[1152,512]{1,0:T(8,128)(2,1)S(1)}, bf16[1152,512]{1,0:T(8,128)(2,1)S(1)}, u32[]{:S(2)}, u32[]{:S(2)}) collective-permute-start(bf16[1152,512]{1,0:T(8,128)(2,1)S(1)} %pad_maximum_fusion), channel_id=1, source_target_pairs={{0,4},{1,3},{2,6},{3,1},{4,0},{5,7},{6,2},{7,5},{8,12},{9,11},{10,... | collective-permute-start | bytes 3538952 | tf_op jit(solution)/shard_map/ppermute | solution.py:397
  153.0 9.1 %collective-permute-start.15 = (bf16[208,512]{1,0:T(8,128)(2,1)S(1)}, bf16[208,512]{1,0:T(8,128)(2,1)S(1)}, u32[]{:S(2)}, u32[]{:S(2)}) collective-permute-start(bf16[208,512]{1,0:T(8,128)(2,1)S(1)} %add_convert_fusion.7), channel_id=1, source_target_pairs={{0,16},{1,9},{2,18},{3,11},{4,20},{5,13},{6,22},{7,15},{8,24},{9,1... | collective-permute-start | bytes 638984 | tf_op jit(solution)/shard_map/ppermute | solution.py:397
  154.6 7.6 %collective-permute-start.18 = (bf16[576,512]{1,0:T(8,128)(2,1)S(1)}, bf16[576,512]{1,0:T(8,128)(2,1)S(1)}, u32[]{:S(2)}, u32[]{:S(2)}) collective-permute-start(bf16[576,512]{1,0:T(8,128)(2,1)S(1)} %add_convert_fusion.1.refs_0_), channel_id=1, source_target_pairs={{0,1},{1,0},{2,3},{3,2},{4,5},{5,4},{6,7},{7,6},{8,9},{9,8},{10,11... | collective-permute-start | bytes 1769480 | tf_op jit(solution)/shard_map/ppermute | solution.py:374
  154.7 7.6 %collective-permute-start.19 = (bf16[576,512]{1,0:T(8,128)(2,1)S(1)}, bf16[576,512]{1,0:T(8,128)(2,1)S(1)}, u32[]{:S(2)}, u32[]{:S(2)}) collective-permute-start(bf16[576,512]{1,0:T(8,128)(2,1)S(1)} %collective-permute-done.16.refs_1_), channel_id=1, source_target_pairs={{0,1},{1,0},{2,3},{3,2},{4,5},{5,4},{6,7},{7,6},{8,9},{9,8},{10,11... | collective-permute-start | bytes 1769480 | tf_op jit(solution)/shard_map/ppermute | solution.py:374
  162.2 7.2 %collective-permute-start.17 = (bf16[192,512]{1,0:T(8,128)(2,1)S(1)}, bf16[192,512]{1,0:T(8,128)(2,1)S(1)}, u32[]{:S(2)}, u32[]{:S(2)}) collective-permute-start(bf16[192,512]{1,0:T(8,128)(2,1)S(1)} %slice.87), channel_id=1, source_target_pairs={{0,2},{1,5},{2,0},{3,7},{4,6},{5,1},{6,4},{7,3},{8,10},{9,13},{10,... | collective-permute-start | bytes 589832 | tf_op jit(solution)/shard_map/ppermute | solution.py:397
  170.5 2.8 %collective-permute-start.22 = (bf16[1152,512]{1,0:T(8,128)(2,1)S(1)}, bf16[1152,512]{1,0:T(8,128)(2,1)S(1)}, u32[]{:S(2)}, u32[]{:S(2)}) collective-permute-start(bf16[1152,512]{1,0:T(8,128)(2,1)S(1)} %collective-permute-done.21.refs_0_), channel_id=1, source_target_pairs={{0,1},{1,0},{2,3},{3,2},{4,5},{5,4},{6,7},{7,6},{8,9},{9,8},{10,11... | collective-permute-start | bytes 3538952 | tf_op jit(solution)/shard_map/ppermute | solution.py:374
  170.5 7.8 %collective-permute-start.20 = (bf16[384,512]{1,0:T(8,128)(2,1)S(1)}, bf16[384,512]{1,0:T(8,128)(2,1)S(1)}, u32[]{:S(2)}, u32[]{:S(2)}) collective-permute-start(bf16[384,512]{1,0:T(8,128)(2,1)S(1)} %pad_maximum_fusion.3), channel_id=1, source_target_pairs={{0,4},{1,3},{2,6},{3,1},{4,0},{5,7},{6,2},{7,5},{8,12},{9,11},{10,... | collective-permute-start | bytes 1179656 | tf_op jit(solution)/shard_map/ppermute | solution.py:397
  178.3 2.3 %collective-permute-start.25 = (bf16[384,512]{1,0:T(8,128)(2,1)S(1)}, bf16[384,512]{1,0:T(8,128)(2,1)S(1)}, u32[]{:S(2)}, u32[]{:S(2)}) collective-permute-start(bf16[384,512]{1,0:T(8,128)(2,1)S(1)} %collective-permute-done.20.refs_2_), channel_id=1, source_target_pairs={{0,1},{1,0},{2,3},{3,2},{4,5},{5,4},{6,7},{7,6},{8,9},{9,8},{10,11... | collective-permute-start | bytes 1179656 | tf_op jit(solution)/shard_map/ppermute | solution.py:374
  178.3 2.0 %collective-permute-start.23 = (bf16[208,512]{1,0:T(8,128)(2,1)S(1)}, bf16[208,512]{1,0:T(8,128)(2,1)S(1)}, u32[]{:S(2)}, u32[]{:S(2)}) collective-permute-start(bf16[208,512]{1,0:T(8,128)(2,1)S(1)} %add_convert_fusion.6.refs_0_), channel_id=1, source_target_pairs={{0,1},{1,0},{2,3},{3,2},{4,5},{5,4},{6,7},{7,6},{8,9},{9,8},{10,11... | collective-permute-start | bytes 638984 | tf_op jit(solution)/shard_map/ppermute | solution.py:374
  178.8 1.8 collective-permute-start.24
